TPU v7x, 32 devices: a whole 2x2x4 slice. The times are simulated.
32 devices in a mesh: groups: 2 (over y), sub: 4 (over z), rng: 2 (over x), chan: 2 (over core).
Axes of the slice: x: 2, y: 2, z: 4, core: 2. Of those that a mesh axis runs over, the one named last changes fastest.
Arguments:
- raw: bfloat16 [4, 2, 4096, 512], P('chan', None, ('groups', 'sub'), 'rng'), parts along dimension 2, may hold values from -6 to 6
- filt: float32 [4, 2, 16], P('chan'), may hold values from -1 to 1
- steer: bfloat16 [4, 256, 1024], P('sub'), may hold values from -0.1875 to 0.1875
- chan_w: float32 [4, 2], P('chan'), may hold values from -2 to 2
- merge_w: bfloat16 [4, 2, 2, 256, 256], P('sub'), may hold values from -1 to 1
- samp_index: int32 [8, 4, 8, 32], P(('sub', 'rng')), may hold values from 0 to 32767
- samp_weight: float32 [8, 4, 8, 32], P(('sub', 'rng')), may hold values from 0.1 to 1
- counts: int32 [8, 8], P(('sub', 'rng')), may hold values from 0 to 32, as said below
- pixel_id: int32 [8, 8, 32], P(('sub', 'rng')), may hold values from 0 to 4095
Outputs:
- cart: float32 [2, 65536], P(None, ('groups', 'sub', 'rng')), parts along dimension 1
There are 2 independent parts, one for each index of `groups`. A program takes and returns all parts, laid end to end along the dimension named above; an argument that names none is the same for every part. Nothing has to cross between parts.
Inputs may be any that keep to these rules, and one draw needn't show every extreme that they name: `counts`: A block sends at most 32 live slots to one owner; some owners receive 32 from every block.
All inputs are finite; a program needn't handle non-finite values.
Results may differ from a plain program's by a relative error of at most 0.013.
Values may be sent and summed in bfloat16 or wider, within the bound.
No kernel may reach another device: no remote copies, remote signals or barrier semaphores. Data moves between devices by JAX's collectives and lax.ppermute only.
A program may use at most 64 MiB of HBM per device.

v0:
```python
import jax
import jax.numpy as jnp
from jax import lax
from jax.sharding import PartitionSpec as P

PIX_OWN = 4096


def padded(block, sides, width):
    for axis, dim in sides:
        count = lax.axis_size(axis)
        forward = [(i, i + 1) for i in range(count - 1)]
        backward = [(target, source) for source, target in forward]
        low = lax.ppermute(
            lax.slice_in_dim(block, block.shape[dim] - width, None, axis=dim), axis, forward
        )
        high = lax.ppermute(lax.slice_in_dim(block, 0, width, axis=dim), axis, backward)
        block = jnp.concatenate([low, block, high], axis=dim)
    return block


def from_partner(value, axis, bit):
    return lax.ppermute(value, axis, [(i, i ^ 1 << bit) for i in range(lax.axis_size(axis))])


def local(raw, filt, steer, chan_w, merge_w, samp_index, samp_weight, counts, pixel_id):
    taps_len = filt.shape[2]
    margin = taps_len // 2
    bin_total = raw.shape[3]
    pulse_count = raw.shape[2]
    channel_count = raw.shape[0]
    extended = padded(raw, (("rng", 3),), margin)
    acc_re = jnp.zeros((channel_count, pulse_count, bin_total), jnp.float32)
    acc_im = jnp.zeros((channel_count, pulse_count, bin_total), jnp.float32)
    for offset in range(taps_len):
        tap_re = filt[:, 0, offset][:, None, None]
        tap_im = filt[:, 1, offset][:, None, None]
        seg_re = extended[:, 0, :, offset : offset + bin_total].astype(jnp.float32)
        seg_im = extended[:, 1, :, offset : offset + bin_total].astype(jnp.float32)
        acc_re = acc_re + tap_re * seg_re - tap_im * seg_im
        acc_im = acc_im + tap_re * seg_im + tap_im * seg_re
    compressed = jnp.stack([acc_re, acc_im], 1).astype(jnp.bfloat16)
    compressed = compressed.reshape(channel_count, 2 * pulse_count, bin_total)
    images = jnp.einsum("ij,cjr->cir", steer[0], compressed, preferred_element_type=jnp.float32)
    beam_count = images.shape[1] // 2
    img_re = images[:, :beam_count]
    img_im = images[:, beam_count:]
    weight_re = chan_w[:, 0][:, None, None]
    weight_im = chan_w[:, 1][:, None, None]
    partial_re = jnp.sum(weight_re * img_re - weight_im * img_im, axis=0)
    partial_im = jnp.sum(weight_re * img_im + weight_im * img_re, axis=0)
    partial_value = jnp.concatenate([partial_re, partial_im], 0)
    summed = lax.psum(partial_value, "chan")
    polar = summed.astype(jnp.bfloat16)
    width = polar.shape[1]
    level_count = lax.axis_size("sub").bit_length() - 1
    weights_here = merge_w[0]
    for level_index in range(level_count):
        other = from_partner(polar, "sub", level_index)
        mixed = jnp.dot(weights_here[level_index, 0], polar, preferred_element_type=jnp.float32)
        mixed = mixed + jnp.dot(
            weights_here[level_index, 1], other, preferred_element_type=jnp.float32
        )
        polar = mixed.astype(jnp.bfloat16)
    index_here = samp_index[0]
    tap_weight = samp_weight[0]
    tap_count = index_here.shape[0]
    owner_count = index_here.shape[1]
    slot_count = index_here.shape[2]
    beam_of = index_here // bin_total
    bin_of = index_here % bin_total
    columns = jnp.arange(width, dtype=jnp.int32)
    beam_ids = jnp.arange(beam_count, dtype=jnp.int32)
    gathered = []
    for tap in range(tap_count):
        pick_bin = (bin_of[tap].reshape(-1)[:, None] == columns[None, :]).astype(jnp.bfloat16)
        picked_rows = lax.dot_general(
            pick_bin, polar, (((1,), (1,)), ((), ())), preferred_element_type=jnp.float32
        )
        pick_beam = (beam_of[tap].reshape(-1)[:, None] == beam_ids[None, :]).astype(jnp.float32)
        value_re = jnp.sum(picked_rows[:, :beam_count] * pick_beam, axis=1)
        value_im = jnp.sum(picked_rows[:, beam_count:] * pick_beam, axis=1)
        gathered.append(jnp.stack([value_re, value_im], 0))
    samples = jnp.stack(gathered, 1).reshape(2, tap_count, owner_count, slot_count)
    summed_taps = jnp.sum(samples * tap_weight[None], axis=1)
    live = (jnp.arange(slot_count, dtype=jnp.int32)[None, :] < counts[0][:, None]).astype(
        jnp.float32
    )
    outgoing = (summed_taps * live[None]).transpose(1, 0, 2)
    arrived = lax.all_to_all(outgoing, ("sub", "rng"), split_axis=0, concat_axis=0, tiled=True)
    flat_vals = arrived.transpose(1, 0, 2).reshape(2, -1)
    low_count = 128
    high_count = PIX_OWN // low_count
    pixels = pixel_id[0].reshape(-1)
    pick_high = (
        pixels[:, None] // low_count == jnp.arange(high_count, dtype=jnp.int32)[None, :]
    ).astype(jnp.float32)
    pick_low = (
        pixels[:, None] % low_count == jnp.arange(low_count, dtype=jnp.int32)[None, :]
    ).astype(jnp.float32)
    weighted = flat_vals[:, :, None] * pick_high[None]
    image = jnp.einsum("snh,nl->shl", weighted, pick_low, precision=lax.Precision.HIGHEST)
    image = image.reshape(2, PIX_OWN)
    return image


def solution(mesh):
    placed = (
        P("chan", None, ("groups", "sub"), "rng"),
        P("chan", None, None),
        P("sub", None, None),
        P("chan", None),
        P("sub", None, None, None, None),
        P(("sub", "rng"), None, None, None),
        P(("sub", "rng"), None, None, None),
        P(("sub", "rng"), None),
        P(("sub", "rng"), None, None),
    )
    return jax.shard_map(
        local,
        mesh=mesh,
        in_specs=placed,
        out_specs=P(None, ("groups", "sub", "rng")),
        check_vma=False,
    )
```

profile of v0, /device:TPU:0, one launch (start us, length us, event | category | flops | bytes accessed | tf_op | source)
XLA Modules:
  0.0 76.6 jit_solution(702453004104948909)
XLA Ops:
  0.0 2.5 %fusion.112 = (bf16[2,2,512,8]{3,2,1,0:T(8,128)(2,1)}, bf16[2,2,512,8]{3,2,1,0:T(8,128)(2,1)}) fusion(bf16[2,2,512,256]{3,2,1,0:T(8,128)(2,1)} %param.9), kind=kLoop, calls=%fused_computation.290 | loop fusion | bytes 131072 | tf_op jit(solution)/shard_map/slice | solution.py:15
  2.5 1.4 %collective-permute-start.1 = (bf16[2,2,512,8]{3,2,1,0:T(8,128)(2,1)}, bf16[2,2,512,8]{3,2,1,0:T(8,128)(2,1)}, u32[]{:S(2)}, u32[]{:S(2)}) collective-permute-start(bf16[2,2,512,8]{3,2,1,0:T(8,128)(2,1)} %get-tuple-element.50), channel_id=1, source_target_pairs={{2,0},{3,1},{6,4},{7,5},{10,8},{11,9},{14,12},{15,13},{18,16},{19,... | collective-permute-start | bytes 98312 | tf_op jit(solution)/shard_map/ppermute | solution.py:17
  4.0 6.5 %collective-permute-start = (bf16[2,2,512,8]{3,2,1,0:T(8,128)(2,1)}, bf16[2,2,512,8]{3,2,1,0:T(8,128)(2,1)}, u32[]{:S(2)}, u32[]{:S(2)}) collective-permute-start(bf16[2,2,512,8]{3,2,1,0:T(8,128)(2,1)} %get-tuple-element.49), channel_id=1, source_target_pairs={{0,2},{1,3},{4,6},{5,7},{8,10},{9,11},{12,14},{13,15},{16,18},{17,... | collective-permute-start | bytes 98312 | tf_op jit(solution)/shard_map/ppermute | solution.py:14
  10.4 0.2 slice_reduce_fusion.32
  10.6 0.2 slice_reduce_fusion.31
  11.1 0.1 broadcast_in_dim_reshape_squeeze.2
  11.2 0.2 slice_reduce_fusion.33
  11.3 0.1 eq.158
  11.4 0.1 eq.154
  11.5 0.1 eq.166
  11.6 0.1 eq.162
  11.7 0.1 eq.174
  11.7 0.1 eq.170
  11.8 0.1 eq.182
  11.9 0.1 eq.178
  12.0 7.2 %collective-permute-done.1 = bf16[2,2,512,8]{3,2,1,0:T(8,128)(2,1)} collective-permute-done((bf16[2,2,512,8]{3,2,1,0:T(8,128)(2,1)}, bf16[2,2,512,8]{3,2,1,0:T(8,128)(2,1)}, u32[]{:S(2)}, u32[]{:S(2)}) %collective-permute-start.1) | collective-permute-done | bytes 32800 | tf_op jit(solution)/shard_map/ppermute | solution.py:17
  19.2 1.2 %constant_dynamic-update-slice_fusion = bf16[2,2,512,264]{3,2,1,0:T(8,128)(2,1)S(1)} fusion(bf16[2,2,512,264]{3,2,1,0:T(8,128)(2,1)S(1)} %constant_dynamic-update-slice_fusion.1, bf16[2,2,512,8]{3,2,1,0:T(8,128)(2,1)} %collective-permute-done.1), kind=kLoop, calls=%fused_computation.245 | loop fusion | bytes 557056 | tf_op jit(solution)/shard_map/concatenate | solution.py:18
  20.3 0.8 %collective-permute-done = bf16[2,2,512,8]{3,2,1,0:T(8,128)(2,1)} collective-permute-done((bf16[2,2,512,8]{3,2,1,0:T(8,128)(2,1)}, bf16[2,2,512,8]{3,2,1,0:T(8,128)(2,1)}, u32[]{:S(2)}, u32[]{:S(2)}) %collective-permute-start) | collective-permute-done | bytes 32800 | tf_op jit(solution)/shard_map/ppermute | solution.py:14
  21.1 8.9 %fusion.58 = bf16[2,1,512,256]{3,2,1,0:T(8,128)(2,1)S(1)} fusion(f32[2]{0:T(128)S(1)} %get-tuple-element.45, f32[2]{0:T(128)S(1)} %get-tuple-element.46, f32[2]{0:T(128)S(1)} %get-tuple-element.16, f32[2]{0:T(128)S(1)} %get-tuple-element.17, f32[2]{0:T(128)S(1)} %get-tuple-element.18, f32[2]{0:T(128)S(1)} %get-tuple-element.19, f32[2]{0:T(128)S(1)} %get-tuple-element.20, ...), kind=kLoop, calls=%fused_computation.156 | loop fusion | flops 37748736 | bytes 10010624 | tf_op jit(solution)/shard_map/convert
  30.0 8.9 %fusion.64 = bf16[2,1,512,256]{3,2,1,0:T(8,128)(2,1)S(1)} fusion(f32[2]{0:T(128)S(1)} %get-tuple-element.45, f32[2]{0:T(128)S(1)} %get-tuple-element.46, f32[2]{0:T(128)S(1)} %get-tuple-element.16, f32[2]{0:T(128)S(1)} %get-tuple-element.17, f32[2]{0:T(128)S(1)} %get-tuple-element.18, f32[2]{0:T(128)S(1)} %get-tuple-element.19, f32[2]{0:T(128)S(1)} %get-tuple-element.20, ...), kind=kLoop, calls=%fused_computation.162 | loop fusion | flops 37748736 | bytes 10010624 | tf_op jit(solution)/shard_map/convert.1
  38.9 0.1 pad_maximum_fusion
  39.1 0.5 convolution_bitcast_fusion
  39.5 0.1 subtract_reduce_fusion
  39.7 4.2 %all-reduce.1 = bf16[256,256]{0,1:T(8,128)(2,1)S(1)} all-reduce(f32[256,256]{0,1:T(8,128)S(1)} %pad_maximum_fusion.2), channel_id=1, replica_groups=mesh['groups'=2,'sub'=4,'rng'=2,'chan'=2] {'chan'}, use_global_device_ids=true, to_apply=%region_2.0 | all-reduce | flops 65536 | bytes 393216 | tf_op jit(solution)/shard_map/psum | solution.py:53
  43.9 2.5 %collective-permute-start.2 = (bf16[256,256]{0,1:T(8,128)(2,1)S(1)}, bf16[256,256]{0,1:T(8,128)(2,1)S(1)}, u32[]{:S(2)}, u32[]{:S(2)}) collective-permute-start(bf16[256,256]{0,1:T(8,128)(2,1)S(1)} %all-reduce.1), channel_id=1, source_target_pairs={{0,4},{4,0},{8,12},{12,8},{1,5},{5,1},{9,13},{13,9},{2,6},{6,2},{1... | collective-permute-start | bytes 393224 | tf_op jit(solution)/shard_map/ppermute | solution.py:23
  46.4 0.2 fusion.95
  46.6 3.8 %collective-permute-done.2 = bf16[256,256]{0,1:T(8,128)(2,1)S(1)} collective-permute-done((bf16[256,256]{0,1:T(8,128)(2,1)S(1)}, bf16[256,256]{0,1:T(8,128)(2,1)S(1)}, u32[]{:S(2)}, u32[]{:S(2)}) %collective-permute-start.2) | collective-permute-done | bytes 131104 | tf_op jit(solution)/shard_map/ppermute | solution.py:23
  50.4 0.2 fusion
  50.6 2.8 %collective-permute-start.3 = (bf16[256,256]{0,1:T(8,128)(2,1)S(1)}, bf16[256,256]{0,1:T(8,128)(2,1)S(1)}, u32[]{:S(2)}, u32[]{:S(2)}) collective-permute-start(bf16[256,256]{0,1:T(8,128)(2,1)S(1)} %bitcast.74), channel_id=1, source_target_pairs={{0,8},{4,12},{8,0},{12,4},{1,9},{5,13},{9,1},{13,5},{2,10},{6,14},... | collective-permute-start | bytes 393224 | tf_op jit(solution)/shard_map/ppermute | solution.py:23
  53.4 0.2 fusion.94
  53.7 5.9 %collective-permute-done.3 = bf16[256,256]{0,1:T(8,128)(2,1)S(1)} collective-permute-done((bf16[256,256]{0,1:T(8,128)(2,1)S(1)}, bf16[256,256]{0,1:T(8,128)(2,1)S(1)}, u32[]{:S(2)}, u32[]{:S(2)}) %collective-permute-start.3) | collective-permute-done | bytes 131104 | tf_op jit(solution)/shard_map/ppermute | solution.py:23
  59.6 0.2 fusion.1
  59.8 0.3 fusion.82
  60.1 0.1 stack.50
  60.2 0.1 stack.51
  60.3 0.3 fusion.83
  60.6 0.1 stack.53
  60.7 0.1 stack.54
  60.8 0.3 fusion.84
  61.1 0.1 stack.56
  61.3 0.3 fusion.85
  61.6 0.1 stack.59
  61.8 0.6 copy.16
  62.4 6.6 %all-to-all-start = ((f32[8,2,32]{2,1,0:T(2,128)}), f32[8,2,32]{2,1,0:T(2,128)S(1)}, u32[]{:S(2)}, u32[]{:S(2)}) async-start(f32[8,2,32]{2,1,0:T(2,128)} %copy.16), calls=%async_computation | async-start | bytes 16384 | tf_op jit(solution)/shard_map/all_to_all | solution.py:90
  69.1 6.5 %all-to-all-done = f32[8,2,32]{2,1,0:T(2,128)S(1)} async-done(((f32[8,2,32]{2,1,0:T(2,128)}), f32[8,2,32]{2,1,0:T(2,128)S(1)}, u32[]{:S(2)}, u32[]{:S(2)}) %all-to-all-start) | async-done | bytes 2080 | tf_op jit(solution)/shard_map/all_to_all | solution.py:90
  75.6 0.1 mul.819
  75.6 0.3 convolution_bitcast_fusion.1
  75.9 0.6 copy.21
  (34 shorter events, 0.6 us)
Async XLA Ops:
  0.0 39.0 %copy-start = (bf16[1,256,1024]{2,1,0:T(8,128)(2,1)S(1)}, bf16[1,256,1024]{2,1,0:T(8,128)(2,1)}, u32[]{:S(2)}) copy-start(bf16[1,256,1024]{2,1,0:T(8,128)(2,1)} %param.11) | copy-start | bytes 1572868
  0.0 10.8 %copy-start.1 = (bf16[2,2,512,256]{3,2,1,0:T(8,128)(2,1)S(1)}, bf16[2,2,512,256]{3,2,1,0:T(8,128)(2,1)}, u32[]{:S(2)}) copy-start(bf16[2,2,512,256]{3,2,1,0:T(8,128)(2,1)} %param.9) | copy-start | bytes 3145732
  0.0 10.4 %copy-start.2 = (f32[2,2,16]{2,1,0:T(2,128)S(1)}, f32[2,2,16]{2,1,0:T(2,128)}, u32[]{:S(2)}) copy-start(f32[2,2,16]{2,1,0:T(2,128)} %param.10) | copy-start | bytes 772
  2.5 8.4 %copy-start.4 = (s32[1,4,8,32]{3,2,1,0:T(8,128)S(1)}, s32[1,4,8,32]{3,2,1,0:T(8,128)}, u32[]{:S(2)}) copy-start(s32[1,4,8,32]{3,2,1,0:T(8,128)} %param.14) | copy-start | bytes 12292
  2.5 8.5 %copy-start.8 = (s32[1,8]{1,0:T(1,128)S(1)}, s32[1,8]{1,0:T(1,128)}, u32[]{:S(2)}) copy-start(s32[1,8]{1,0:T(1,128)} %param.16) | copy-start | bytes 100
  2.5 8.5 %copy-start.6 = (s32[1,8,32]{2,1,0:T(8,128)S(1)}, s32[1,8,32]{2,1,0:T(8,128)}, u32[]{:S(2)}) copy-start(s32[1,8,32]{2,1,0:T(8,128)} %param.17) | copy-start | bytes 3076
  2.5 8.6 %copy-start.7 = (f32[2,2]{1,0:T(2,128)S(1)}, f32[2,2]{1,0:T(2,128)}, u32[]{:S(2)}) copy-start(f32[2,2]{1,0:T(2,128)} %param.12) | copy-start | bytes 52
  2.5 16.6 %collective-permute-start.1 = (bf16[2,2,512,8]{3,2,1,0:T(8,128)(2,1)}, bf16[2,2,512,8]{3,2,1,0:T(8,128)(2,1)}, u32[]{:S(2)}, u32[]{:S(2)}) collective-permute-start(bf16[2,2,512,8]{3,2,1,0:T(8,128)(2,1)} %get-tuple-element.50), channel_id=1, source_target_pairs={{2,0},{3,1},{6,4},{7,5},{10,8},{11,9},{14,12},{15,13},{18,16},{19,... | collective-permute-start | bytes 98312 | tf_op jit(solution)/shard_map/ppermute | solution.py:17
  4.0 17.2 %collective-permute-start = (bf16[2,2,512,8]{3,2,1,0:T(8,128)(2,1)}, bf16[2,2,512,8]{3,2,1,0:T(8,128)(2,1)}, u32[]{:S(2)}, u32[]{:S(2)}) collective-permute-start(bf16[2,2,512,8]{3,2,1,0:T(8,128)(2,1)} %get-tuple-element.49), channel_id=1, source_target_pairs={{0,2},{1,3},{4,6},{5,7},{8,10},{9,11},{12,14},{13,15},{16,18},{17,... | collective-permute-start | bytes 98312 | tf_op jit(solution)/shard_map/ppermute | solution.py:14
  39.0 7.3 %copy-start.3 = (bf16[1,2,2,256,256]{4,3,2,1,0:T(8,128)(2,1)S(1)}, bf16[1,2,2,256,256]{4,3,2,1,0:T(8,128)(2,1)}, u32[]{:S(2)}) copy-start(bf16[1,2,2,256,256]{4,3,2,1,0:T(8,128)(2,1)} %param.13) | copy-start | bytes 1572868
  43.9 6.5 %collective-permute-start.2 = (bf16[256,256]{0,1:T(8,128)(2,1)S(1)}, bf16[256,256]{0,1:T(8,128)(2,1)S(1)}, u32[]{:S(2)}, u32[]{:S(2)}) collective-permute-start(bf16[256,256]{0,1:T(8,128)(2,1)S(1)} %all-reduce.1), channel_id=1, source_target_pairs={{0,4},{4,0},{8,12},{12,8},{1,5},{5,1},{9,13},{13,9},{2,6},{6,2},{1... | collective-permute-start | bytes 393224 | tf_op jit(solution)/shard_map/ppermute | solution.py:23
  50.6 9.0 %collective-permute-start.3 = (bf16[256,256]{0,1:T(8,128)(2,1)S(1)}, bf16[256,256]{0,1:T(8,128)(2,1)S(1)}, u32[]{:S(2)}, u32[]{:S(2)}) collective-permute-start(bf16[256,256]{0,1:T(8,128)(2,1)S(1)} %bitcast.74), channel_id=1, source_target_pairs={{0,8},{4,12},{8,0},{12,4},{1,9},{5,13},{9,1},{13,5},{2,10},{6,14},... | collective-permute-start | bytes 393224 | tf_op jit(solution)/shard_map/ppermute | solution.py:23
  53.6 8.2 %copy-start.5 = (f32[1,4,8,32]{3,2,1,0:T(8,128)S(1)}, f32[1,4,8,32]{3,2,1,0:T(8,128)}, u32[]{:S(2)}) copy-start(f32[1,4,8,32]{3,2,1,0:T(8,128)} %param.15) | copy-start | bytes 12292
  62.4 13.1 %all-to-all-start = ((f32[8,2,32]{2,1,0:T(2,128)}), f32[8,2,32]{2,1,0:T(2,128)S(1)}, u32[]{:S(2)}, u32[]{:S(2)}) async-start(f32[8,2,32]{2,1,0:T(2,128)} %copy.16), calls=%async_computation | async-start | bytes 16384 | tf_op jit(solution)/shard_map/all_to_all | solution.py:90
where the time goes:
time: 77.1 us; the launch traced here: 76.6 us
  waiting for transfers between devices  24.2 us (31%)
  starting transfers between devices  19.8 us (26%)
  other arithmetic  18.3 us (24%)
  local copies, waits for them, and re-layouts  7 us (9%)
  blocking collectives  4.17 us (5%)
  matrix products  2.78 us (4%)
    another operation x2, other arithmetic  17.8 us
    ppermute x2, waiting for transfers between devices, from_partner(): lax.ppermute(value, axis, [(i, i ^ 1 << bit) for i in range(lax.axis_size...  9.69 us
    ppermute x1, waiting for transfers between devices, padded(): lax.ppermute(lax.slice_in_dim(block, 0, width, axis=dim), axis, backward)  7.19 us
    all_to_all x1, starting transfers between devices, local(): lax.all_to_all(outgoing, ('sub', 'rng'), split_axis=0, concat_axis=0, til...  6.61 us
    all_to_all x1, waiting for transfers between devices, local(): lax.all_to_all(outgoing, ('sub', 'rng'), split_axis=0, concat_axis=0, til...  6.51 us
    ppermute x1, starting transfers between devices, padded(): lax.ppermute(lax.slice_in_dim(block, block.shape[dim] - width, None, axis...  6.47 us
    ppermute x2, starting transfers between devices, from_partner(): lax.ppermute(value, axis, [(i, i ^ 1 << bit) for i in range(lax.axis_size...  5.3 us
    psum x1, blocking collectives, local(): summed = lax.psum(partial_value, 'chan')  4.17 us
  transfers between devices with their start and end apart: 5, of which 5 were waited for; matrix products, arithmetic and copies ran while one was open for 4% of the time, Pallas kernels for 0%

commit v1 on v0

v1 whole, which is shorter than its diff:
```python
import functools

import jax
import jax.numpy as jnp
from jax import lax
from jax.experimental import pallas as pl
from jax.experimental.pallas import tpu as pltpu
from jax.sharding import PartitionSpec as P

PIX_OWN = 4096
LANES = 128
ROW = 256
EDGE = 8
F32 = jnp.float32
BF16 = jnp.bfloat16
VMEM = pl.BlockSpec(memory_space=pltpu.VMEM)
SMEM = pl.BlockSpec(memory_space=pltpu.SMEM)
NT = (((1,), (1,)), ((), ()))


def dot(a, b):
    return jnp.dot(a, b, preferred_element_type=F32)


def dot_nt(a, b):
    return lax.dot_general(a, b, NT, preferred_element_type=F32)


def prepare_kernel(raw_ref, last_ref, index_ref, weight_ref, counts_ref, edge_ref, pack_ref):
    channels, _, _, bins = raw_ref.shape
    row = lax.broadcasted_iota(jnp.int32, (2 * EDGE, bins), 0)
    column = lax.broadcasted_iota(jnp.int32, (2 * EDGE, bins), 1)
    wanted = jnp.where(row < EDGE, row, row + bins - 2 * EDGE)
    pick = (column == wanted).astype(F32).astype(BF16)
    for c in range(channels):
        for part in range(2):
            edge_ref[c, part] = dot_nt(pick, raw_ref[c, part]).astype(BF16)
    size = last_ref.shape[3]
    pack_ref[:size, :] = last_ref[0, 0, 0]
    taps, owners, slots = index_ref.shape[1:]
    per_row = ROW // slots
    slot = lax.broadcasted_iota(jnp.int32, (taps, slots), 1)
    rows = []
    for first in range(0, owners, per_row):
        parts = []
        for o in range(first, first + per_row):
            index = index_ref[0, :, o, :]
            weight = jnp.where(slot < counts_ref[0, o], weight_ref[0, :, o, :], 0.0)
            coarse = weight.astype(BF16).astype(F32)
            parts.append(
                jnp.concatenate(
                    [
                        (index // bins).astype(F32),
                        (index % bins).astype(F32),
                        coarse,
                        weight - coarse,
                    ],
                    0,
                )
            )
        rows.append(jnp.concatenate(parts, 1))
    pack_ref[size:, :] = jnp.concatenate(rows, 0).astype(BF16)


def circulants(filt_ref, channel, part):
    row = lax.broadcasted_iota(jnp.int32, (LANES, LANES), 0)
    column = lax.broadcasted_iota(jnp.int32, (LANES, LANES), 1)
    place = (row - column + EDGE) & (LANES - 1)
    out = jnp.zeros((LANES, LANES), F32)
    for k in range(filt_ref.shape[2]):
        out = jnp.where(place == k, filt_ref[channel, part, k], out)
    return out


def band(filt_ref, channel, part, bins):
    ring = circulants(filt_ref, channel, part)
    row = lax.broadcasted_iota(jnp.int32, (LANES, LANES), 0)
    column = lax.broadcasted_iota(jnp.int32, (LANES, LANES), 1)
    far = column - row
    zero = jnp.zeros((LANES, LANES), BF16)
    near = jnp.where((far < 64) & (far > -64), ring, 0.0).astype(BF16)
    below = jnp.where(far >= 64, ring, 0.0).astype(BF16)
    above = jnp.where(far <= -64, ring, 0.0).astype(BF16)
    count = bins // LANES
    blocks = {0: near, 1: below, -1: above}
    return jnp.concatenate(
        [
            jnp.concatenate([blocks.get(i - o, zero) for o in range(count)], 1)
            for i in range(count)
        ],
        0,
    )


def turned(value, channel_ref, channel):
    half = value.shape[0] // 2
    re, im = value[:half], value[half:]
    wr, wi = channel_ref[channel, 0], channel_ref[channel, 1]
    return jnp.concatenate([wr * re - wi * im, wr * im + wi * re], 0)


def steered(steer_ref, x_re, x_im, product):
    pulses = steer_ref.shape[2] // 2
    s_re, s_im = steer_ref[0, :, :pulses], steer_ref[0, :, pulses:]
    direct = product(s_re, x_re) + product(s_im, x_im)
    cross = product(s_im, x_re) - product(s_re, x_im)
    return direct.astype(BF16), cross.astype(BF16)


def image_kernel(raw_ref, steer_ref, filt_ref, channel_ref, out_ref):
    channels, _, _, bins = raw_ref.shape
    total = jnp.zeros(out_ref.shape, F32)
    for c in range(channels):
        direct, cross = steered(steer_ref, raw_ref[c, 0], raw_ref[c, 1], dot)
        image = dot(direct, band(filt_ref, c, 0, bins)) + dot(cross, band(filt_ref, c, 1, bins))
        total = total + turned(image, channel_ref, c)
    out_ref[...] = total


def edge_kernel(main_ref, edge_ref, steer_ref, filt_ref, channel_ref, ends_ref, out_ref):
    channels = edge_ref.shape[0]
    bins = main_ref.shape[1]
    row = lax.broadcasted_iota(jnp.int32, (2 * EDGE, bins), 0)
    column = lax.broadcasted_iota(jnp.int32, (2 * EDGE, bins), 1)
    high = row < EDGE
    source = jnp.where(high, row + bins, row - 2 * EDGE)
    there = jnp.where(high, ends_ref[1], ends_ref[0]) > 0
    place = jnp.where(there, source - column + EDGE, -1)
    total = main_ref[...]
    for c in range(channels):
        direct, cross = steered(steer_ref, edge_ref[c, 0], edge_ref[c, 1], dot_nt)
        taps = []
        for part in range(2):
            out = jnp.zeros((2 * EDGE, bins), F32)
            for k in range(filt_ref.shape[2]):
                out = jnp.where(place == k, filt_ref[c, part, k], out)
            taps.append(out.astype(BF16))
        image = dot(direct, taps[0]) + dot(cross, taps[1])
        total = total + turned(image, channel_ref, c)
    out_ref[...] = total.astype(BF16)


def merge_kernel(weight_ref, own_ref, other_ref, out_ref):
    mixed = dot(weight_ref[0, 0, 0], own_ref[...]) + dot(weight_ref[0, 0, 1], other_ref[...])
    out_ref[...] = mixed.astype(BF16)


def sample_kernel(taps, slots, weight_ref, own_ref, other_ref, pack_ref, far_ref, out_ref):
    size, bins = own_ref.shape
    half = size // 2
    mixed = dot(weight_ref[0, 0, 0], own_ref[...]) + dot(weight_ref[0, 0, 1], other_ref[...])
    polar = mixed.astype(BF16)
    chunks = (pack_ref.shape[0] - size) // (4 * taps)
    per_row = ROW // slots
    owners = per_row * chunks
    bin_ids = lax.broadcasted_iota(jnp.int32, (bins, ROW), 0).astype(F32)
    beam_ids = lax.broadcasted_iota(jnp.int32, (half, ROW), 0).astype(F32)
    for block, (merge, ref) in enumerate(
        ((weight_ref[0, 1, 0], pack_ref), (far_ref[:size, :], far_ref))
    ):
        merged = dot(merge, polar).astype(BF16)
        for chunk in range(chunks):
            base = size + 4 * taps * chunk
            rows = ref[base : base + 4 * taps, :].astype(F32)
            sum_re = jnp.zeros((half, ROW), F32)
            sum_im = jnp.zeros((half, ROW), F32)
            for t in range(taps):
                beam = rows[t : t + 1]
                column = rows[taps + t : taps + t + 1]
                weight = rows[2 * taps + t : 2 * taps + t + 1] + rows[3 * taps + t : 3 * taps + t + 1]
                pick_bin = (bin_ids == column).astype(F32).astype(BF16)
                picked = dot(merged, pick_bin)
                pick_beam = jnp.where(beam_ids == beam, weight, 0.0)
                sum_re = sum_re + picked[:half] * pick_beam
                sum_im = sum_im + picked[half:] * pick_beam
            for part, value in enumerate((sum_re, sum_im)):
                flat = jnp.sum(value, axis=0, keepdims=True)
                lane = (2 * block + part) * slots
                for k in range(per_row):
                    o = chunk * per_row + k
                    piece = flat[:, k * slots : (k + 1) * slots]
                    out_ref[o : o + 1, lane : lane + slots] = piece
                    out_ref[owners + o : owners + o + 1, lane : lane + slots] = piece


def scatter_kernel(value_ref, pixel_ref, out_ref, flat_ref, place_ref):
    owners, slots = pixel_ref.shape[1:]
    total = value_ref[:owners, :] + value_ref[owners:, :]
    for b in range(owners):
        far = (b + owners // 2) % owners
        place_ref[0:1, b * slots : (b + 1) * slots] = pixel_ref[0, b : b + 1, :]
        for part in range(2):
            lane = part * slots
            flat_ref[part : part + 1, b * slots : (b + 1) * slots] = (
                total[b : b + 1, lane : lane + slots]
                + total[far : far + 1, 2 * slots + lane : 2 * slots + lane + slots]
            )
    count = owners * slots
    tall = PIX_OWN // LANES
    pixel = place_ref[...]
    high = lax.broadcasted_iota(jnp.int32, (tall, count), 0) == pixel // LANES
    low = lax.broadcasted_iota(jnp.int32, (LANES, count), 0) == pixel % LANES
    pick_low = low.astype(F32).astype(BF16)
    spread = jnp.concatenate(
        [jnp.where(high, flat_ref[part : part + 1, :], 0.0) for part in range(2)], 0
    )
    coarse = spread.astype(BF16)
    fine = (spread - coarse.astype(F32)).astype(BF16)
    image = dot_nt(coarse, pick_low) + dot_nt(fine, pick_low)
    for part in range(2):
        for h in range(tall):
            row = part * tall + h
            out_ref[part : part + 1, h * LANES : (h + 1) * LANES] = image[row : row + 1, :]


def shape(dims, dtype):
    return jax.ShapeDtypeStruct(dims, dtype)


def picked(array, *indices):
    dims = tuple(1 for _ in indices) + array.shape[len(indices) :]
    place = indices + (0,) * (array.ndim - len(indices))
    return pl.BlockSpec(dims, lambda i: place)


def call(kernel, out_shape, in_specs, out_specs, flops=0, nbytes=0, scratch=(), grid=None):
    extra = {} if grid is None else {"grid": grid}
    return pl.pallas_call(
        kernel,
        out_shape=out_shape,
        in_specs=in_specs,
        out_specs=out_specs,
        scratch_shapes=list(scratch),
        cost_estimate=pl.CostEstimate(flops=flops, bytes_accessed=nbytes, transcendentals=0),
        compiler_params=pltpu.CompilerParams(vmem_limit_bytes=48 * 2**20),
        **extra,
    )


def whole(array):
    return pl.BlockSpec(array.shape, lambda i: (0,) * array.ndim)


def swapped(value, axis, bit):
    return lax.ppermute(value, axis, [(i, i ^ 1 << bit) for i in range(lax.axis_size(axis))])


def neighbour_edges(edges):
    count = lax.axis_size("rng")
    if count == 2:
        return lax.ppermute(edges, "rng", [(0, 1), (1, 0)])
    after = lax.ppermute(edges, "rng", [(i + 1, i) for i in range(count - 1)])
    before = lax.ppermute(edges, "rng", [(i, i + 1) for i in range(count - 1)])
    return jnp.concatenate([after[:, :, :EDGE], before[:, :, EDGE:]], 2)


def local(raw, filt, steer, chan_w, merge_w, samp_index, samp_weight, counts, pixel_id):
    channels, _, pulses, bins = raw.shape
    size = steer.shape[1]
    levels = merge_w.shape[1]
    taps, owners, slots = samp_index.shape[1:]
    extra = 4 * taps * owners * slots // ROW
    edge_dims = (channels, 2, 2 * EDGE, pulses)
    edges, pack = call(
        prepare_kernel,
        (shape(edge_dims, BF16), shape((size + extra, ROW), BF16)),
        [
            whole(raw),
            pl.BlockSpec((1, 1, 1, size, size), lambda i: (0, levels - 1, 1, 0, 0)),
            whole(samp_index),
            whole(samp_weight),
            SMEM,
        ],
        (pl.BlockSpec(edge_dims, lambda i: (0, 0, 0, 0)), pl.BlockSpec((size + extra, ROW), lambda i: (0, 0))),
        flops=2**26,
        nbytes=2**20,
        grid=(1,),
    )(raw, merge_w, samp_index, samp_weight, counts)
    beside = neighbour_edges(edges)
    far = swapped(pack, "sub", levels - 1)
    main = call(
        image_kernel,
        shape((size, bins), F32),
        [VMEM, VMEM, SMEM, SMEM],
        VMEM,
        flops=2**30,
        nbytes=2**21,
    )(raw, steer, filt, chan_w)
    place = lax.axis_index("rng")
    ends = jnp.stack([place > 0, place < lax.axis_size("rng") - 1]).astype(jnp.int32)
    polar = call(
        edge_kernel,
        shape((size, bins), BF16),
        [VMEM, VMEM, VMEM, SMEM, SMEM, SMEM],
        VMEM,
        flops=2**27,
        nbytes=2**20,
    )(main, beside, steer, filt, chan_w, ends)
    for level in range(levels - 2):
        other = swapped(polar, "sub", level)
        polar = call(
            merge_kernel,
            shape((size, bins), BF16),
            [
                pl.BlockSpec((1, 1, 2, size, size), lambda i, level=level: (0, level, 0, 0, 0)),
                whole(polar),
                whole(other),
            ],
            pl.BlockSpec((size, bins), lambda i: (0, 0)),
            grid=(1,),
        )(merge_w, polar, other)
    other = swapped(polar, "sub", levels - 2)
    outgoing = call(
        functools.partial(sample_kernel, taps, slots),
        shape((2 * owners, 4 * slots), F32),
        [
            VMEM,
            VMEM,
            VMEM,
            VMEM,
            VMEM,
        ],
        VMEM,
        flops=2**28,
        nbytes=2**20,
    )(merge_w[:, levels - 2 :], polar, other, pack, far)
    arrived = lax.all_to_all(
        outgoing, ("chan", "sub", "rng"), split_axis=0, concat_axis=0, tiled=True
    )
    return call(
        scatter_kernel,
        shape((2, PIX_OWN), F32),
        [VMEM, VMEM],
        VMEM,
        scratch=[
            pltpu.VMEM((2, owners * slots), F32),
            pltpu.VMEM((1, owners * slots), jnp.int32),
        ],
    )(arrived, pixel_id)


def solution(mesh):
    placed = (
        P("chan", None, ("groups", "sub"), "rng"),
        P("chan", None, None),
        P("sub", None, None),
        P("chan", None),
        P("sub", None, None, None, None),
        P(("sub", "rng"), None, None, None),
        P(("sub", "rng"), None, None, None),
        P(("sub", "rng"), None),
        P(("sub", "rng"), None, None),
    )
    return jax.shard_map(
        local,
        mesh=mesh,
        in_specs=placed,
        out_specs=P(None, ("groups", "sub", "rng")),
        check_vma=False,
    )
```

time: 77.1 us -> 33.5 us (0.43)
  waiting for transfers between devices: 24.2 us -> 3.47 us
  other arithmetic: 18.3 us -> 0.07 us
  starting transfers between devices: 19.8 us -> 7.21 us
  blocking collectives: 4.17 us -> 11.1 us
  Pallas kernels: 0 us -> 6.26 us
  matrix products: 2.78 us -> 0 us
  local copies, waits for them, and re-layouts: 7 us -> 4.98 us
    another operation x3 -> x0, other arithmetic: 17.9 us -> none
    ppermute x4 -> x3, waiting for transfers between devices: 17.7 us -> 3.47 us  [the longest x2 3.47 us: swapped(): lax.ppermute(value, axis, [(i, i ^ 1 << bit) for i in range(lax.axis_size...]
    all_to_all x0 -> x1, blocking collectives: none -> 11.1 us  [local(): lax.all_to_all(outgoing, ('chan', 'sub', 'rng'), split_axis=0, concat_axi...]
    all_to_all x1 -> x0, starting transfers between devices: 6.61 us -> none  [local(): lax.all_to_all(outgoing, ('sub', 'rng'), split_axis=0, concat_axis=0, til...]
    all_to_all x1 -> x0, waiting for transfers between devices: 6.51 us -> none  [local(): lax.all_to_all(outgoing, ('sub', 'rng'), split_axis=0, concat_axis=0, til...]
    pallas_call x0 -> x5, Pallas kernels: none -> 6.26 us  [the longest x1 1.72 us: local(): call(image_kernel, shape((size, bins), F32), [VMEM, VMEM, SMEM, SMEM], VM...]
    ppermute x4 -> x3, starting transfers between devices: 13.2 us -> 7.21 us  [the longest x2 4.23 us: swapped(): lax.ppermute(value, axis, [(i, i ^ 1 << bit) for i in range(lax.axis_size...]
    unnamed x20 -> x22, local copies, waits for them, and re-layouts: 0.75 us -> 4.98 us
  transfers between devices with their start and end apart: 5 -> 3, of which waited for: 5 -> 2; matrix products, arithmetic and copies ran while one was open for 4% -> 0% of each run, Pallas kernels for 0% -> 10%
where the time goes in v1:
time: 33.5 us; the launch traced here: 33.1 us
  blocking collectives  11.1 us (33%)
  starting transfers between devices  7.21 us (22%)
  Pallas kernels  6.26 us (19%)
  local copies, waits for them, and re-layouts  4.98 us (15%)
  waiting for transfers between devices  3.47 us (10%)
    all_to_all x1, blocking collectives, local(): lax.all_to_all(outgoing, ('chan', 'sub', 'rng'), split_axis=0, concat_axi...  11.1 us
    unnamed x22, local copies, waits for them, and re-layouts  4.98 us
    ppermute x2, starting transfers between devices, swapped(): lax.ppermute(value, axis, [(i, i ^ 1 << bit) for i in range(lax.axis_size...  4.23 us
    ppermute x2, waiting for transfers between devices, swapped(): lax.ppermute(value, axis, [(i, i ^ 1 << bit) for i in range(lax.axis_size...  3.47 us
    ppermute x1, starting transfers between devices, neighbour_edges(): return lax.ppermute(edges, 'rng', [(0, 1), (1, 0)])  2.98 us
    pallas_call x1, Pallas kernels, local(): call(image_kernel, shape((size, bins), F32), [VMEM, VMEM, SMEM, SMEM], VM...  1.72 us
    pallas_call x1, Pallas kernels, local(): call(edge_kernel, shape((size, bins), BF16), [VMEM, VMEM, VMEM, SMEM, SME...  1.67 us
    pallas_call x1, Pallas kernels, local(): call(functools.partial(sample_kernel, taps, slots), shape((2 * owners, 4...  1.05 us
  transfers between devices with their start and end apart: 3, of which 2 were waited for; matrix products, arithmetic and copies ran while one was open for 0% of the time, Pallas kernels for 10%

profile of v1, /device:TPU:0, one launch (start us, length us, event | category | flops | bytes accessed | tf_op | source)
XLA Modules:
  0.0 33.1 jit_solution(9335514117316074669)
XLA Ops:
  0.0 0.0 copy-start
  0.0 1.0 %copy-done = bf16[1,2,2,256,256]{4,3,2,1,0:T(8,128)(2,1)S(1)} copy-done((bf16[1,2,2,256,256]{4,3,2,1,0:T(8,128)(2,1)S(1)}, bf16[1,2,2,256,256]{4,3,2,1,0:T(8,128)(2,1)}, u32[]{:S(2)}) %copy-start) | copy-done | bytes 524312
  1.0 0.0 copy-start.2
  1.0 1.2 %copy-done.2 = bf16[2,2,512,256]{3,2,1,0:T(8,128)(2,1)S(1)} copy-done((bf16[2,2,512,256]{3,2,1,0:T(8,128)(2,1)S(1)}, bf16[2,2,512,256]{3,2,1,0:T(8,128)(2,1)}, u32[]{:S(2)}) %copy-start.2) | copy-done | bytes 1048600
  2.3 0.0 copy-start.5
  2.3 0.7 %copy-done.5 = s32[1,4,8,32]{3,2,1,0:T(8,128)S(1)} copy-done((s32[1,4,8,32]{3,2,1,0:T(8,128)S(1)}, s32[1,4,8,32]{3,2,1,0:T(8,128)}, u32[]{:S(2)}) %copy-start.5) | copy-done | bytes 4120
  3.0 0.0 copy-start.6
  3.0 0.7 %copy-done.6 = f32[1,4,8,32]{3,2,1,0:T(8,128)S(1)} copy-done((f32[1,4,8,32]{3,2,1,0:T(8,128)S(1)}, f32[1,4,8,32]{3,2,1,0:T(8,128)}, u32[]{:S(2)}) %copy-start.6) | copy-done | bytes 4120
  3.7 0.0 copy-start.10
  3.7 0.7 %copy-done.10 = s32[1,8]{1,0:T(1,128)S(1)} copy-done((s32[1,8]{1,0:T(1,128)S(1)}, s32[1,8]{1,0:T(1,128)}, u32[]{:S(2)}) %copy-start.10) | copy-done | bytes 56
  4.4 0.0 copy-start.3
  4.4 0.0 copy-start.4
  4.4 0.9 %shard_map.92 = (bf16[2,2,16,512]{3,2,1,0:T(8,128)(2,1)S(1)}, bf16[272,256]{1,0:T(8,128)(2,1)S(1)}) custom-call(bf16[2,2,512,256]{3,2,1,0:T(8,128)(2,1)S(1)} %copy-done.2, bf16[1,2,2,256,256]{4,3,2,1,0:T(8,128)(2,1)S(1)} %copy-done, s32[1,4,8,32]{3,2,1,0:T(8,128)S(1)} %copy-done.5, f32[1,4,8,32]{3,2,1,0:T(8,128)S(1)} %copy-done.6, s32[1,8]{1,0:T(1,128)S(1)} %copy-done.10), custom_call_target="tpu_custom_call" | custom-call | flops 67108864 | bytes 1048576 | tf_op jit(solution)/shard_map/pallas_call | solution.py:264
  5.3 3.0 %collective-permute-start = (bf16[2,2,16,512]{3,2,1,0:T(8,128)(2,1)S(1)}, bf16[2,2,16,512]{3,2,1,0:T(8,128)(2,1)S(1)}, u32[]{:S(2)}, u32[]{:S(2)}) collective-permute-start(bf16[2,2,16,512]{3,2,1,0:T(8,128)(2,1)S(1)} %get-tuple-element.7), channel_id=1, source_target_pairs={{0,2},{2,0},{1,3},{3,1},{4,6},{6,4},{5,7},{7,5},{8,10},{10,8},{9,1... | collective-permute-start | bytes 196616 | tf_op jit(solution)/shard_map/ppermute | solution.py:251
  8.3 2.6 %collective-permute-start.2 = (bf16[272,256]{1,0:T(8,128)(2,1)S(1)}, bf16[272,256]{1,0:T(8,128)(2,1)S(1)}, u32[]{:S(2)}, u32[]{:S(2)}) collective-permute-start(bf16[272,256]{1,0:T(8,128)(2,1)S(1)} %get-tuple-element.8.pack_ref), channel_id=1, source_target_pairs={{0,8},{4,12},{8,0},{12,4},{1,9},{5,13},{9,1},{13,5},{2,10},{6,14},... | collective-permute-start | bytes 417800 | tf_op jit(solution)/shard_map/ppermute | solution.py:245
  10.9 0.0 copy-start.8
  10.9 0.0 copy-start.9
  10.9 0.1 add_convert_fusion.ends_ref
  10.9 0.0 copy-done.3
  10.9 0.0 copy-done.4
  10.9 0.6 %copy-done.8 = f32[2,2,16]{2,1,0:T(2,128)S(1)} copy-done((f32[2,2,16]{2,1,0:T(2,128)S(1)}, f32[2,2,16]{2,1,0:T(2,128)}, u32[]{:S(2)}) %copy-start.8) | copy-done | bytes 280
  11.5 0.0 copy-done.9
  11.6 1.7 %shard_map.91.main_ref = f32[256,256]{1,0:T(8,128)S(1)} custom-call(bf16[2,2,512,256]{3,2,1,0:T(8,128)(2,1)S(1)} %copy-done.3, bf16[1,256,1024]{2,1,0:T(8,128)(2,1)S(1)} %copy-done.4, f32[2,2,16]{2,1,0:T(2,128)S(1)} %copy-done.8, f32[2,2]{1,0:T(2,128)S(1)} %copy-done.9), custom_call_target="tpu_custom_call" | custom-call | flops 1073741824 | bytes 2097152 | tf_op jit(solution)/shard_map/pallas_call | solution.py:281
  13.3 0.0 copy-start.1
  13.3 0.0 collective-permute-done.edge_ref
  13.3 1.7 %shard_map.93.own_ref = bf16[256,256]{1,0:T(8,128)(2,1)S(1)} custom-call(f32[256,256]{1,0:T(8,128)S(1)} %shard_map.91.main_ref, bf16[2,2,16,512]{3,2,1,0:T(8,128)(2,1)S(1)} %collective-permute-done.edge_ref, bf16[1,256,1024]{2,1,0:T(8,128)(2,1)S(1)} %copy-done.4, f32[2,2,16]{2,1,0:T(2,128)S(1)} %copy-done.8, f32[2,2]{1,0:T(2,128)S(1)} %copy-done.9, ...), custom_call_target="tpu_custom_call" | custom-call | flops 134217728 | bytes 1048576 | tf_op jit(solution)/shard_map/pallas_call | solution.py:291
  15.0 1.6 %collective-permute-start.1 = (bf16[256,256]{1,0:T(8,128)(2,1)S(1)}, bf16[256,256]{1,0:T(8,128)(2,1)S(1)}, u32[]{:S(2)}, u32[]{:S(2)}) collective-permute-start(bf16[256,256]{1,0:T(8,128)(2,1)S(1)} %shard_map.93.own_ref), channel_id=1, source_target_pairs={{0,4},{4,0},{8,12},{12,8},{1,5},{5,1},{9,13},{13,9},{2,6},{6,2},{1... | collective-permute-start | bytes 393224 | tf_op jit(solution)/shard_map/ppermute | solution.py:245
  16.6 0.7 %collective-permute-done.2.far_ref = bf16[272,256]{1,0:T(8,128)(2,1)S(1)} collective-permute-done((bf16[272,256]{1,0:T(8,128)(2,1)S(1)}, bf16[272,256]{1,0:T(8,128)(2,1)S(1)}, u32[]{:S(2)}, u32[]{:S(2)}) %collective-permute-start.2) | collective-permute-done | bytes 139296 | tf_op jit(solution)/shard_map/ppermute | solution.py:245
  17.3 2.8 %collective-permute-done.1.other_ref = bf16[256,256]{1,0:T(8,128)(2,1)S(1)} collective-permute-done((bf16[256,256]{1,0:T(8,128)(2,1)S(1)}, bf16[256,256]{1,0:T(8,128)(2,1)S(1)}, u32[]{:S(2)}, u32[]{:S(2)}) %collective-permute-start.1) | collective-permute-done | bytes 131104 | tf_op jit(solution)/shard_map/ppermute | solution.py:245
  20.1 0.0 copy-done.1
  20.1 0.0 copy-start.7
  20.1 1.0 %shard_map.94 = f32[16,128]{1,0:T(8,128)S(1)} custom-call(bf16[1,2,2,256,256]{4,3,2,1,0:T(8,128)(2,1)S(1)} %copy-done.1, bf16[256,256]{1,0:T(8,128)(2,1)S(1)} %shard_map.93.own_ref, bf16[256,256]{1,0:T(8,128)(2,1)S(1)} %collective-permute-done.1.other_ref, bf16[272,256]{1,0:T(8,128)(2,1)S(1)} %get-tuple-element.8.pack_ref, ...), custom_call_target="tpu_custom_call" | custom-call | flops 268435456 | bytes 1048576 | tf_op jit(solution)/shard_map/pallas_call | solution.py:313
  21.1 11.1 %all_to_all.11 = f32[16,1,128]{2,1,0:T(1,128)S(1)} all-to-all(f32[16,1,128]{2,1,0:T(1,128)S(1)} %bitcast.6), channel_id=1, replica_groups=mesh['groups'=2,'sub'=4,'rng'=2,'chan'=2] {'chan','sub','rng'}, dimensions={0} | all-to-all | bytes 16384 | tf_op jit(solution)/shard_map/all_to_all | solution.py:327
  32.2 0.0 copy-done.7
  32.2 0.9 %shard_map.95 = f32[2,4096]{1,0:T(2,128)} custom-call(f32[16,128]{1,0:T(8,128)S(1)} %bitcast.7, s32[1,8,32]{2,1,0:T(8,128)S(1)} %copy-done.7), custom_call_target="tpu_custom_call" | custom-call | tf_op jit(solution)/shard_map/pallas_call | solution.py:330
Async XLA Ops:
  0.0 1.0 %copy-start = (bf16[1,2,2,256,256]{4,3,2,1,0:T(8,128)(2,1)S(1)}, bf16[1,2,2,256,256]{4,3,2,1,0:T(8,128)(2,1)}, u32[]{:S(2)}) copy-start(bf16[1,2,2,256,256]{4,3,2,1,0:T(8,128)(2,1)} %weight_ref.3) | copy-start | bytes 1572868
  1.0 1.2 %copy-start.2 = (bf16[2,2,512,256]{3,2,1,0:T(8,128)(2,1)S(1)}, bf16[2,2,512,256]{3,2,1,0:T(8,128)(2,1)}, u32[]{:S(2)}) copy-start(bf16[2,2,512,256]{3,2,1,0:T(8,128)(2,1)} %raw_ref.3) | copy-start | bytes 3145732
  2.3 0.7 %copy-start.5 = (s32[1,4,8,32]{3,2,1,0:T(8,128)S(1)}, s32[1,4,8,32]{3,2,1,0:T(8,128)}, u32[]{:S(2)}) copy-start(s32[1,4,8,32]{3,2,1,0:T(8,128)} %index_ref.1) | copy-start | bytes 12292
  3.0 0.7 %copy-start.6 = (f32[1,4,8,32]{3,2,1,0:T(8,128)S(1)}, f32[1,4,8,32]{3,2,1,0:T(8,128)}, u32[]{:S(2)}) copy-start(f32[1,4,8,32]{3,2,1,0:T(8,128)} %weight_ref.2) | copy-start | bytes 12292
  3.7 0.7 %copy-start.10 = (s32[1,8]{1,0:T(1,128)S(1)}, s32[1,8]{1,0:T(1,128)}, u32[]{:S(2)}) copy-start(s32[1,8]{1,0:T(1,128)} %counts_ref.1) | copy-start | bytes 100
  4.4 6.6 %copy-start.3 = (bf16[2,2,512,256]{3,2,1,0:T(8,128)(2,1)S(1)}, bf16[2,2,512,256]{3,2,1,0:T(8,128)(2,1)}, u32[]{:S(2)}) copy-start(bf16[2,2,512,256]{3,2,1,0:T(8,128)(2,1)} %raw_ref.3) | copy-start | bytes 3145732
  4.4 6.6 %copy-start.4 = (bf16[1,256,1024]{2,1,0:T(8,128)(2,1)S(1)}, bf16[1,256,1024]{2,1,0:T(8,128)(2,1)}, u32[]{:S(2)}) copy-start(bf16[1,256,1024]{2,1,0:T(8,128)(2,1)} %steer_ref.3) | copy-start | bytes 1572868
  5.3 8.0 %collective-permute-start = (bf16[2,2,16,512]{3,2,1,0:T(8,128)(2,1)S(1)}, bf16[2,2,16,512]{3,2,1,0:T(8,128)(2,1)S(1)}, u32[]{:S(2)}, u32[]{:S(2)}) collective-permute-start(bf16[2,2,16,512]{3,2,1,0:T(8,128)(2,1)S(1)} %get-tuple-element.7), channel_id=1, source_target_pairs={{0,2},{2,0},{1,3},{3,1},{4,6},{6,4},{5,7},{7,5},{8,10},{10,8},{9,1... | collective-permute-start | bytes 196616 | tf_op jit(solution)/shard_map/ppermute | solution.py:251
  8.3 9.1 %collective-permute-start.2 = (bf16[272,256]{1,0:T(8,128)(2,1)S(1)}, bf16[272,256]{1,0:T(8,128)(2,1)S(1)}, u32[]{:S(2)}, u32[]{:S(2)}) collective-permute-start(bf16[272,256]{1,0:T(8,128)(2,1)S(1)} %get-tuple-element.8.pack_ref), channel_id=1, source_target_pairs={{0,8},{4,12},{8,0},{12,4},{1,9},{5,13},{9,1},{13,5},{2,10},{6,14},... | collective-permute-start | bytes 417800 | tf_op jit(solution)/shard_map/ppermute | solution.py:245
  10.9 0.7 %copy-start.8 = (f32[2,2,16]{2,1,0:T(2,128)S(1)}, f32[2,2,16]{2,1,0:T(2,128)}, u32[]{:S(2)}) copy-start(f32[2,2,16]{2,1,0:T(2,128)} %filt_ref.3) | copy-start | bytes 772
  10.9 0.7 %copy-start.9 = (f32[2,2]{1,0:T(2,128)S(1)}, f32[2,2]{1,0:T(2,128)}, u32[]{:S(2)}) copy-start(f32[2,2]{1,0:T(2,128)} %channel_ref.3) | copy-start | bytes 52
  13.3 6.8 %copy-start.1 = (bf16[1,2,2,256,256]{4,3,2,1,0:T(8,128)(2,1)S(1)}, bf16[1,2,2,256,256]{4,3,2,1,0:T(8,128)(2,1)}, u32[]{:S(2)}) copy-start(bf16[1,2,2,256,256]{4,3,2,1,0:T(8,128)(2,1)} %weight_ref.3) | copy-start | bytes 1572868
  15.0 5.1 %collective-permute-start.1 = (bf16[256,256]{1,0:T(8,128)(2,1)S(1)}, bf16[256,256]{1,0:T(8,128)(2,1)S(1)}, u32[]{:S(2)}, u32[]{:S(2)}) collective-permute-start(bf16[256,256]{1,0:T(8,128)(2,1)S(1)} %shard_map.93.own_ref), channel_id=1, source_target_pairs={{0,4},{4,0},{8,12},{12,8},{1,5},{5,1},{9,13},{13,9},{2,6},{6,2},{1... | collective-permute-start | bytes 393224 | tf_op jit(solution)/shard_map/ppermute | solution.py:245
  20.1 12.1 %copy-start.7 = (s32[1,8,32]{2,1,0:T(8,128)S(1)}, s32[1,8,32]{2,1,0:T(8,128)}, u32[]{:S(2)}) copy-start(s32[1,8,32]{2,1,0:T(8,128)} %pixel_ref.1) | copy-start | bytes 3076

commit v2 on v1

v2 whole, which is shorter than its diff:
```python
import functools

import jax
import jax.numpy as jnp
from jax import lax
from jax.experimental import pallas as pl
from jax.experimental.pallas import tpu as pltpu
from jax.sharding import PartitionSpec as P

PIX_OWN = 4096
LANES = 128
ROW = 256
EDGE = 8
F32 = jnp.float32
BF16 = jnp.bfloat16
VMEM = pl.BlockSpec(memory_space=pltpu.VMEM)
SMEM = pl.BlockSpec(memory_space=pltpu.SMEM)
NT = (((1,), (1,)), ((), ()))


def dot(a, b):
    return jnp.dot(a, b, preferred_element_type=F32)


def dot_nt(a, b):
    return lax.dot_general(a, b, NT, preferred_element_type=F32)


def rim_kernel(raw_ref, edge_ref):
    channels, _, _, bins = raw_ref.shape
    row = lax.broadcasted_iota(jnp.int32, (2 * EDGE, bins), 0)
    column = lax.broadcasted_iota(jnp.int32, (2 * EDGE, bins), 1)
    wanted = jnp.where(row < EDGE, row, row + bins - 2 * EDGE)
    pick = (column == wanted).astype(F32).astype(BF16)
    for c in range(channels):
        for part in range(2):
            edge_ref[c, part] = dot_nt(pick, raw_ref[c, part]).astype(BF16)


def prepare_kernel(
    bins, chan_axis, merge_ref, index_ref, weight_ref, filt_ref, chan_ref, counts_ref,
    pack_ref, band_ref, end_ref, mix_ref,
):
    channels = filt_ref.shape[0]
    half = merge_ref.shape[3] // 2
    last = merge_ref.shape[1] - 1
    core = lax.axis_index(chan_axis) % 2
    rows = pl.ds(pl.multiple_of(core * half, half), half)
    pack_ref[:half, :] = merge_ref[0, last, 1, rows, :]
    taps = filt_ref.shape[2]
    row = lax.broadcasted_iota(jnp.int32, (LANES, LANES), 0)
    column = lax.broadcasted_iota(jnp.int32, (LANES, LANES), 1)
    far = column - row
    place = (EDGE - far) & (LANES - 1)
    rings = [[jnp.zeros((LANES, LANES), F32) for _ in range(2)] for _ in range(channels)]
    for k in range(taps):
        here = place == k
        for c in range(channels):
            for part in range(2):
                rings[c][part] = jnp.where(here, filt_ref[c, part, k], rings[c][part])
    zero = jnp.zeros((LANES, LANES), BF16)
    count = bins // LANES
    for c in range(channels):
        for part in range(2):
            ring = rings[c][part]
            blocks = {
                0: jnp.where((far < 64) & (far > -64), ring, 0.0).astype(BF16),
                1: jnp.where(far >= 64, ring, 0.0).astype(BF16),
                -1: jnp.where(far <= -64, ring, 0.0).astype(BF16),
            }
            for i in range(count):
                for o in range(count):
                    band_ref[
                        c, part, i * LANES : (i + 1) * LANES, o * LANES : (o + 1) * LANES
                    ] = blocks.get(i - o, zero)
    row = lax.broadcasted_iota(jnp.int32, (2 * EDGE, bins), 0)
    column = lax.broadcasted_iota(jnp.int32, (2 * EDGE, bins), 1)
    place = jnp.where(row < EDGE, row + bins, row - 2 * EDGE) - column + EDGE
    tails = [[jnp.zeros((2 * EDGE, bins), F32) for _ in range(2)] for _ in range(channels)]
    for k in range(taps):
        here = place == k
        for c in range(channels):
            for part in range(2):
                tails[c][part] = jnp.where(here, filt_ref[c, part, k], tails[c][part])
    nothing = jnp.zeros((2 * EDGE, bins), BF16)
    for c in range(channels):
        re, im = tails[c]
        for d in range(channels):
            quads = [re, -im, im, re]
            for q in range(4):
                top = (q // 2) * 2 * channels + 2 * d + q % 2
                end_ref[
                    top * 2 * EDGE : (top + 1) * 2 * EDGE, c * bins : (c + 1) * bins
                ] = quads[q].astype(BF16) if c == d else nothing
        for part in range(2):
            mix_ref[8 * (2 * c + part) : 8 * (2 * c + part + 1), :] = jnp.full(
                (8, bins), chan_ref[c, part], F32
            )
    taps, owners, slots = index_ref.shape[1:]
    per_row = ROW // slots
    slot = lax.broadcasted_iota(jnp.int32, (taps, slots), 1)
    lines = []
    for first in range(0, owners, per_row):
        parts = []
        for o in range(first, first + per_row):
            index = index_ref[0, :, o, :]
            weight = jnp.where(slot < counts_ref[0, o], weight_ref[0, :, o, :], 0.0)
            coarse = weight.astype(BF16).astype(F32)
            parts.append(
                jnp.concatenate(
                    [
                        (index // bins).astype(F32),
                        (index % bins).astype(F32),
                        coarse,
                        weight - coarse,
                    ],
                    0,
                )
            )
        lines.append(jnp.concatenate(parts, 1))
    pack_ref[half:, :] = jnp.concatenate(lines, 0).astype(BF16)


def turned(value, mix_ref, channel):
    half = value.shape[0] // 2
    re, im = value[:half], value[half:]
    wr = mix_ref[16 * channel : 16 * channel + 1, :]
    wi = mix_ref[16 * channel + 8 : 16 * channel + 9, :]
    return jnp.concatenate([wr * re - wi * im, wr * im + wi * re], 0)


def image_kernel(raw_ref, steer_ref, band_ref, mix_ref, out_ref):
    channels, _, pulses, _ = raw_ref.shape
    s_re, s_im = steer_ref[0, :, :pulses], steer_ref[0, :, pulses:]
    total = jnp.zeros(out_ref.shape, F32)
    for c in range(channels):
        x_re, x_im = raw_ref[c, 0], raw_ref[c, 1]
        direct = (dot(s_re, x_re) + dot(s_im, x_im)).astype(BF16)
        cross = (dot(s_im, x_re) - dot(s_re, x_im)).astype(BF16)
        image = dot(direct, band_ref[c, 0]) + dot(cross, band_ref[c, 1])
        total = total + turned(image, mix_ref, c)
    out_ref[...] = total


def edge_kernel(rng_axis, rng_size, main_ref, edge_ref, steer_ref, end_ref, mix_ref, out_ref):
    channels, _, _, pulses = edge_ref.shape
    bins = main_ref.shape[1]
    count = channels * 4 * EDGE
    block = lax.axis_index(rng_axis)
    row = lax.broadcasted_iota(jnp.int32, (count, pulses), 0)
    below = (row & EDGE) > 0
    first = jnp.where(block > 0, 1.0, 0.0)
    last = jnp.where(block < rng_size - 1, 1.0, 0.0)
    keep = jnp.where(below, first, last).astype(BF16)
    edges = edge_ref[...].reshape(count, pulses) * keep
    nothing = jnp.zeros((count, pulses), BF16)
    taken = dot_nt(steer_ref[0, :, :pulses], jnp.concatenate([edges, nothing], 0))
    taken = taken + dot_nt(steer_ref[0, :, pulses:], jnp.concatenate([nothing, edges], 0))
    images = dot(taken.astype(BF16), end_ref[...])
    total = main_ref[...]
    for c in range(channels):
        total = total + turned(images[:, c * bins : (c + 1) * bins], mix_ref, c)
    out_ref[...] = total.astype(BF16)


def merge_kernel(weight_ref, own_ref, other_ref, out_ref):
    mixed = dot(weight_ref[0, 0, 0], own_ref[...]) + dot(weight_ref[0, 0, 1], other_ref[...])
    out_ref[...] = mixed.astype(BF16)


def sample_kernel(
    taps, slots, chan_axis, weight_ref, own_ref, other_ref, pack_ref, near_ref, far_ref, out_ref
):
    size, bins = own_ref.shape
    half = size // 2
    mixed = dot(weight_ref[0, 0, 0], own_ref[...]) + dot(weight_ref[0, 0, 1], other_ref[...])
    polar = mixed.astype(BF16)
    chunks = (pack_ref.shape[0] - half) // (4 * taps)
    per_row = ROW // slots
    owners = per_row * chunks
    even = lax.axis_index(chan_axis) % 2 == 0
    bin_ids = lax.broadcasted_iota(jnp.int32, (bins, ROW), 0).astype(F32)
    beam_ids = lax.broadcasted_iota(jnp.int32, (half, ROW), 0).astype(F32)
    for block, (merges, ref) in enumerate(
        (
            ((weight_ref[0, 1, 0, :half], weight_ref[0, 1, 0, half:]), pack_ref),
            ((near_ref[:half, :], far_ref[:half, :]), near_ref),
        )
    ):
        merged = [dot(merge, polar).astype(BF16) for merge in merges]
        for chunk in range(chunks):
            base = half + 4 * taps * chunk
            rows = ref[base : base + 4 * taps, :].astype(F32)
            sums = [jnp.zeros((half, ROW), F32) for _ in range(2)]
            for t in range(taps):
                beam = rows[t : t + 1]
                column = rows[taps + t : taps + t + 1]
                weight = rows[2 * taps + t : 2 * taps + t + 1] + rows[3 * taps + t : 3 * taps + t + 1]
                pick_bin = (bin_ids == column).astype(F32).astype(BF16)
                pick_beam = jnp.where(beam_ids == beam, weight, 0.0)
                for part in range(2):
                    sums[part] = sums[part] + dot(merged[part], pick_bin) * pick_beam
            flat = [jnp.sum(value, axis=0, keepdims=True) for value in sums]
            if block == 1:
                flat = [jnp.where(even, flat[0], flat[1]), jnp.where(even, flat[1], flat[0])]
            for part in range(2):
                lane = (2 * block + part) * slots
                for k in range(per_row):
                    o = chunk * per_row + k
                    piece = flat[part][:, k * slots : (k + 1) * slots]
                    out_ref[o : o + 1, lane : lane + slots] = piece
                    out_ref[owners + o : owners + o + 1, lane : lane + slots] = piece


def scatter_kernel(value_ref, pixel_ref, out_ref, flat_ref, place_ref):
    owners, slots = pixel_ref.shape[1:]
    total = value_ref[:owners, :] + value_ref[owners:, :]
    for b in range(owners):
        far = (b + owners // 2) % owners
        place_ref[0:1, b * slots : (b + 1) * slots] = pixel_ref[0, b : b + 1, :]
        for part in range(2):
            lane = part * slots
            flat_ref[part : part + 1, b * slots : (b + 1) * slots] = (
                total[b : b + 1, lane : lane + slots]
                + total[far : far + 1, 2 * slots + lane : 2 * slots + lane + slots]
            )
    count = owners * slots
    tall = PIX_OWN // LANES
    pixel = place_ref[...]
    high = lax.broadcasted_iota(jnp.int32, (tall, count), 0) == pixel // LANES
    low = lax.broadcasted_iota(jnp.int32, (LANES, count), 0) == pixel % LANES
    pick_low = low.astype(F32).astype(BF16)
    spread = jnp.concatenate(
        [jnp.where(high, flat_ref[part : part + 1, :], 0.0) for part in range(2)], 0
    )
    coarse = spread.astype(BF16)
    fine = (spread - coarse.astype(F32)).astype(BF16)
    image = dot_nt(coarse, pick_low) + dot_nt(fine, pick_low)
    for part in range(2):
        for h in range(tall):
            row = part * tall + h
            out_ref[part : part + 1, h * LANES : (h + 1) * LANES] = image[row : row + 1, :]


def shape(dims, dtype):
    return jax.ShapeDtypeStruct(dims, dtype)


def call(kernel, out_shape, in_specs, out_specs, flops=0, nbytes=0, scratch=(), grid=None):
    extra = {} if grid is None else {"grid": grid}
    return pl.pallas_call(
        kernel,
        out_shape=out_shape,
        in_specs=in_specs,
        out_specs=out_specs,
        scratch_shapes=list(scratch),
        cost_estimate=pl.CostEstimate(flops=flops, bytes_accessed=nbytes, transcendentals=0),
        compiler_params=pltpu.CompilerParams(vmem_limit_bytes=24 * 2**20),
        **extra,
    )


def whole(array):
    return pl.BlockSpec(array.shape, lambda i: (0,) * array.ndim)


def swapped(value, axis, bit):
    return lax.ppermute(value, axis, [(i, i ^ 1 << bit) for i in range(lax.axis_size(axis))])


def neighbour_edges(edges):
    count = lax.axis_size("rng")
    if count == 2:
        return lax.ppermute(edges, "rng", [(0, 1), (1, 0)])
    after = lax.ppermute(edges, "rng", [(i + 1, i) for i in range(count - 1)])
    before = lax.ppermute(edges, "rng", [(i, i + 1) for i in range(count - 1)])
    return jnp.concatenate([after[:, :, :EDGE], before[:, :, EDGE:]], 2)


def local(raw, filt, steer, chan_w, merge_w, samp_index, samp_weight, counts, pixel_id):
    channels, _, pulses, bins = raw.shape
    size = steer.shape[1]
    levels = merge_w.shape[1]
    taps, owners, slots = samp_index.shape[1:]
    extra = 4 * taps * owners * slots // ROW
    edges = call(
        rim_kernel,
        shape((channels, 2, 2 * EDGE, pulses), BF16),
        [VMEM],
        VMEM,
        flops=2**32,
        nbytes=2**24,
    )(raw)
    beside = neighbour_edges(edges)
    pack, bands, ends, mix = call(
        functools.partial(prepare_kernel, bins, "chan"),
        (
            shape((size // 2 + extra, ROW), BF16),
            shape((channels, 2, bins, bins), BF16),
            shape((channels * 8 * EDGE, channels * bins), BF16),
            shape((16 * channels, bins), F32),
        ),
        [VMEM] * 3 + [SMEM] * 3,
        (VMEM,) * 4,
        flops=2**28,
        nbytes=2**20,
    )(merge_w, samp_index, samp_weight, filt, chan_w, counts)
    near = swapped(pack, "sub", levels - 1)
    main = call(
        image_kernel,
        shape((size, bins), F32),
        [VMEM] * 4,
        VMEM,
        flops=2**30,
        nbytes=2**21,
    )(raw, steer, bands, mix)
    polar = call(
        functools.partial(edge_kernel, "rng", lax.axis_size("rng")),
        shape((size, bins), BF16),
        [VMEM] * 5,
        VMEM,
        flops=2**27,
        nbytes=2**20,
    )(main, beside, steer, ends, mix)
    far = swapped(lax.optimization_barrier((polar, near))[1], "chan", 0)
    for level in range(levels - 2):
        other = swapped(polar, "sub", level)
        polar = call(
            merge_kernel,
            shape((size, bins), BF16),
            [
                pl.BlockSpec((1, 1, 2, size, size), lambda i, level=level: (0, level, 0, 0, 0)),
                whole(polar),
                whole(other),
            ],
            pl.BlockSpec((size, bins), lambda i: (0, 0)),
            grid=(1,),
        )(merge_w, polar, other)
    other = swapped(polar, "sub", levels - 2)
    outgoing = call(
        functools.partial(sample_kernel, taps, slots, "chan"),
        shape((2 * owners, 4 * slots), F32),
        [VMEM] * 6,
        VMEM,
        flops=2**28,
        nbytes=2**20,
    )(merge_w[:, levels - 2 :], polar, other, pack, near, far)
    values = lax.all_to_all(
        outgoing, ("chan", "sub", "rng"), split_axis=0, concat_axis=0, tiled=True
    )
    return call(
        scatter_kernel,
        shape((2, PIX_OWN), F32),
        [VMEM, VMEM],
        VMEM,
        scratch=[
            pltpu.VMEM((2, owners * slots), F32),
            pltpu.VMEM((1, owners * slots), jnp.int32),
        ],
    )(values, pixel_id)


def solution(mesh):
    placed = (
        P("chan", None, ("groups", "sub"), "rng"),
        P("chan", None, None),
        P("sub", None, None),
        P("chan", None),
        P("sub", None, None, None, None),
        P(("sub", "rng"), None, None, None),
        P(("sub", "rng"), None, None, None),
        P(("sub", "rng"), None),
        P(("sub", "rng"), None, None),
    )
    return jax.shard_map(
        local,
        mesh=mesh,
        in_specs=placed,
        out_specs=P(None, ("groups", "sub", "rng")),
        check_vma=False,
    )
```

time: 33.5 us -> 27.3 us (0.81)
  local copies, waits for them, and re-layouts: 4.98 us -> 1.32 us
  Pallas kernels: 6.26 us -> 5.07 us
  blocking collectives: 11.1 us -> 10 us
    unnamed x22 -> x20, local copies, waits for them, and re-layouts: 4.98 us -> 1.32 us
    pallas_call x4 -> x5, Pallas kernels: 5.36 us -> 4.16 us  [the longest x1 1.1 us: local(): call(image_kernel, shape((size, bins), F32), [VMEM] * 4, VMEM, flops=2 **...]
    all_to_all x1, blocking collectives: 11.1 us -> 10 us  [local(): lax.all_to_all(outgoing, ('chan', 'sub', 'rng'), split_axis=0, concat_axi...]
    ppermute x2 -> x3, waiting for transfers between devices: 3.47 us -> 3.39 us  [swapped(): lax.ppermute(value, axis, [(i, i ^ 1 << bit) for i in range(lax.axis_size...]
    ppermute x2 -> x3, starting transfers between devices: 4.23 us -> 4.3 us  [swapped(): lax.ppermute(value, axis, [(i, i ^ 1 << bit) for i in range(lax.axis_size...]
  transfers between devices with their start and end apart: 3 -> 4, of which waited for: 2 -> 3; matrix products, arithmetic and copies ran while one was open for 0% -> 0% of each run, Pallas kernels for 10% -> 10%
where the time goes in v2:
time: 27.3 us; the launch traced here: 27.1 us
  blocking collectives  10 us (37%)
  starting transfers between devices  7.26 us (27%)
  Pallas kernels  5.07 us (19%)
  waiting for transfers between devices  3.39 us (12%)
  local copies, waits for them, and re-layouts  1.32 us (5%)
    all_to_all x1, blocking collectives, local(): lax.all_to_all(outgoing, ('chan', 'sub', 'rng'), split_axis=0, concat_axi...  10 us
    ppermute x3, starting transfers between devices, swapped(): lax.ppermute(value, axis, [(i, i ^ 1 << bit) for i in range(lax.axis_size...  4.3 us
    ppermute x3, waiting for transfers between devices, swapped(): lax.ppermute(value, axis, [(i, i ^ 1 << bit) for i in range(lax.axis_size...  3.39 us
    ppermute x1, starting transfers between devices, neighbour_edges(): return lax.ppermute(edges, 'rng', [(0, 1), (1, 0)])  2.96 us
    unnamed x20, local copies, waits for them, and re-layouts  1.32 us
    pallas_call x1, Pallas kernels, local(): call(image_kernel, shape((size, bins), F32), [VMEM] * 4, VMEM, flops=2 **...  1.1 us
    pallas_call x1, Pallas kernels, local(): call(functools.partial(sample_kernel, taps, slots, 'chan'), shape((2 * ow...  1.07 us
    pallas_call x1, Pallas kernels, local(): call(functools.partial(prepare_kernel, bins, 'chan'), (shape((size // 2 +...  1.06 us
  transfers between devices with their start and end apart: 4, of which 3 were waited for; matrix products, arithmetic and copies ran while one was open for 0% of the time, Pallas kernels for 10%

profile of v2, /device:TPU:0, one launch (start us, length us, event | category | flops | bytes accessed | tf_op | source)
XLA Modules:
  0.0 27.1 jit_solution(3189837232820899920)
XLA Ops:
  0.0 0.0 copy-start.1
  0.0 0.0 copy-start.3
  0.0 1.3 %copy-done.3 = bf16[2,2,512,256]{3,2,1,0:T(8,128)(2,1)S(1)} copy-done((bf16[2,2,512,256]{3,2,1,0:T(8,128)(2,1)S(1)}, bf16[2,2,512,256]{3,2,1,0:T(8,128)(2,1)}, u32[]{:S(2)}) %copy-start.3) | copy-done | bytes 1048600
  1.3 0.0 copy-start.5
  1.3 0.0 copy-start.6
  1.3 0.0 copy-start.7
  1.3 0.0 copy-start.8
  1.3 0.0 copy-start.9
  1.3 0.0 copy-start.4
  1.3 0.4 %shard_map.93 = bf16[2,2,16,512]{3,2,1,0:T(8,128)(2,1)S(1)} custom-call(bf16[2,2,512,256]{3,2,1,0:T(8,128)(2,1)S(1)} %copy-done.3), custom_call_target="tpu_custom_call" | custom-call | flops 4294967296 | bytes 16777216 | tf_op jit(solution)/shard_map/pallas_call | solution.py:286
  1.7 0.0 copy-start
  1.7 3.0 %collective-permute-start = (bf16[2,2,16,512]{3,2,1,0:T(8,128)(2,1)S(1)}, bf16[2,2,16,512]{3,2,1,0:T(8,128)(2,1)S(1)}, u32[]{:S(2)}, u32[]{:S(2)}) collective-permute-start(bf16[2,2,16,512]{3,2,1,0:T(8,128)(2,1)S(1)} %shard_map.93), channel_id=1, source_target_pairs={{0,2},{2,0},{1,3},{3,1},{4,6},{6,4},{5,7},{7,5},{8,10},{10,8},{9,1... | collective-permute-start | bytes 196616 | tf_op jit(solution)/shard_map/ppermute | solution.py:274
  4.7 0.0 copy-done.1
  4.7 0.0 copy-done.5
  4.7 0.0 copy-done.6
  4.7 0.0 copy-done.7
  4.7 0.0 copy-done.8
  4.7 0.0 copy-done.9
  4.7 1.1 %shard_map.91 = (bf16[144,256]{1,0:T(8,128)(2,1)S(1)}, bf16[2,2,256,256]{3,2,1,0:T(8,128)(2,1)S(1)}, bf16[128,512]{1,0:T(8,128)(2,1)S(1)}, f32[32,256]{1,0:T(8,128)S(1)}) custom-call(bf16[1,2,2,256,256]{4,3,2,1,0:T(8,128)(2,1)S(1)} %copy-done.1, s32[1,4,8,32]{3,2,1,0:T(8,128)S(1)} %copy-done.5, f32[1,4,8,32]{3,2,1,0:T(8,128)S(1)} %copy-done.6, ...), custom_call_target="tpu_custom_call" | custom-call | flops 268435456 | bytes 1048576 | tf_op jit(solution)/shard_map/pallas_call | solution.py:295
  5.8 2.7 %collective-permute-start.2 = (bf16[144,256]{1,0:T(8,128)(2,1)S(1)}, bf16[144,256]{1,0:T(8,128)(2,1)S(1)}, u32[]{:S(2)}, u32[]{:S(2)}) collective-permute-start(bf16[144,256]{1,0:T(8,128)(2,1)S(1)} %get-tuple-element.13.pack_ref), channel_id=1, source_target_pairs={{0,8},{4,12},{8,0},{12,4},{1,9},{5,13},{9,1},{13,5},{2,10},{6,14},... | collective-permute-start | bytes 221192 | tf_op jit(solution)/shard_map/ppermute | solution.py:268
  8.4 0.0 copy-done.4
  8.4 0.0 copy-done
  8.4 1.1 %shard_map.92.main_ref = f32[256,256]{1,0:T(8,128)S(1)} custom-call(bf16[2,2,512,256]{3,2,1,0:T(8,128)(2,1)S(1)} %copy-done.4, bf16[1,256,1024]{2,1,0:T(8,128)(2,1)S(1)} %copy-done, bf16[2,2,256,256]{3,2,1,0:T(8,128)(2,1)S(1)} %get-tuple-element.10.band_ref, f32[32,256]{1,0:T(8,128)S(1)} %get-tuple-element.11.mix_ref), custom_call_target="tpu_custom_call" | custom-call | flops 1073741824 | bytes 2097152 | tf_op jit(solution)/shard_map/pallas_call | solution.py:309
  9.5 0.0 collective-permute-done.edge_ref
  9.5 0.6 %shard_map.94.own_ref = bf16[256,256]{1,0:T(8,128)(2,1)S(1)} custom-call(f32[256,256]{1,0:T(8,128)S(1)} %shard_map.92.main_ref, bf16[2,2,16,512]{3,2,1,0:T(8,128)(2,1)S(1)} %collective-permute-done.edge_ref, bf16[1,256,1024]{2,1,0:T(8,128)(2,1)S(1)} %copy-done, bf16[128,512]{1,0:T(8,128)(2,1)S(1)} %get-tuple-element.12.end_ref, ...), custom_call_target="tpu_custom_call" | custom-call | flops 134217728 | bytes 1048576 | tf_op jit(solution)/shard_map/pallas_call | solution.py:317
  10.1 1.6 %collective-permute-start.1 = (bf16[256,256]{1,0:T(8,128)(2,1)S(1)}, bf16[256,256]{1,0:T(8,128)(2,1)S(1)}, u32[]{:S(2)}, u32[]{:S(2)}) collective-permute-start(bf16[256,256]{1,0:T(8,128)(2,1)S(1)} %shard_map.94.own_ref), channel_id=1, source_target_pairs={{0,4},{4,0},{8,12},{12,8},{1,5},{5,1},{9,13},{13,9},{2,6},{6,2},{1... | collective-permute-start | bytes 393224 | tf_op jit(solution)/shard_map/ppermute | solution.py:268
  11.7 0.3 %collective-permute-done.2.near_ref = bf16[144,256]{1,0:T(8,128)(2,1)S(1)} collective-permute-done((bf16[144,256]{1,0:T(8,128)(2,1)S(1)}, bf16[144,256]{1,0:T(8,128)(2,1)S(1)}, u32[]{:S(2)}, u32[]{:S(2)}) %collective-permute-start.2) | collective-permute-done | bytes 73760 | tf_op jit(solution)/shard_map/ppermute | solution.py:268
  12.1 0.0 collective-permute-start.3
  12.1 1.3 %collective-permute-done.3.far_ref = bf16[144,256]{1,0:T(8,128)(2,1)S(1)} collective-permute-done((bf16[144,256]{1,0:T(8,128)(2,1)S(1)}, bf16[144,256]{1,0:T(8,128)(2,1)S(1)}, u32[]{:S(2)}, u32[]{:S(2)}) %collective-permute-start.3) | collective-permute-done | bytes 73760 | tf_op jit(solution)/shard_map/ppermute | solution.py:268
  13.3 1.8 %collective-permute-done.1.other_ref = bf16[256,256]{1,0:T(8,128)(2,1)S(1)} collective-permute-done((bf16[256,256]{1,0:T(8,128)(2,1)S(1)}, bf16[256,256]{1,0:T(8,128)(2,1)S(1)}, u32[]{:S(2)}, u32[]{:S(2)}) %collective-permute-start.1) | collective-permute-done | bytes 131104 | tf_op jit(solution)/shard_map/ppermute | solution.py:268
  15.1 0.0 copy-start.2
  15.1 1.1 %shard_map.95 = f32[16,128]{1,0:T(8,128)S(1)} custom-call(bf16[1,2,2,256,256]{4,3,2,1,0:T(8,128)(2,1)S(1)} %copy-done.1, bf16[256,256]{1,0:T(8,128)(2,1)S(1)} %shard_map.94.own_ref, bf16[256,256]{1,0:T(8,128)(2,1)S(1)} %collective-permute-done.1.other_ref, bf16[144,256]{1,0:T(8,128)(2,1)S(1)} %get-tuple-element.13.pack_ref, ...), custom_call_target="tpu_custom_call" | custom-call | flops 268435456 | bytes 1048576 | tf_op jit(solution)/shard_map/pallas_call | solution.py:340
  16.2 10.0 %all_to_all.11 = f32[16,1,128]{2,1,0:T(1,128)S(1)} all-to-all(f32[16,1,128]{2,1,0:T(1,128)S(1)} %bitcast.4), channel_id=1, replica_groups=mesh['groups'=2,'sub'=4,'rng'=2,'chan'=2] {'chan','sub','rng'}, dimensions={0} | all-to-all | bytes 16384 | tf_op jit(solution)/shard_map/all_to_all | solution.py:348
  26.2 0.0 copy-done.2
  26.2 0.9 %shard_map.96 = f32[2,4096]{1,0:T(2,128)} custom-call(f32[16,128]{1,0:T(8,128)S(1)} %bitcast.5, s32[1,8,32]{2,1,0:T(8,128)S(1)} %copy-done.2), custom_call_target="tpu_custom_call" | custom-call | tf_op jit(solution)/shard_map/pallas_call | solution.py:351
Async XLA Ops:
  0.0 4.7 %copy-start.1 = (bf16[1,2,2,256,256]{4,3,2,1,0:T(8,128)(2,1)S(1)}, bf16[1,2,2,256,256]{4,3,2,1,0:T(8,128)(2,1)}, u32[]{:S(2)}) copy-start(bf16[1,2,2,256,256]{4,3,2,1,0:T(8,128)(2,1)} %weight_ref.3) | copy-start | bytes 1572868
  0.0 1.3 %copy-start.3 = (bf16[2,2,512,256]{3,2,1,0:T(8,128)(2,1)S(1)}, bf16[2,2,512,256]{3,2,1,0:T(8,128)(2,1)}, u32[]{:S(2)}) copy-start(bf16[2,2,512,256]{3,2,1,0:T(8,128)(2,1)} %raw_ref.3) | copy-start | bytes 3145732
  1.3 3.4 %copy-start.5 = (s32[1,4,8,32]{3,2,1,0:T(8,128)S(1)}, s32[1,4,8,32]{3,2,1,0:T(8,128)}, u32[]{:S(2)}) copy-start(s32[1,4,8,32]{3,2,1,0:T(8,128)} %index_ref.1) | copy-start | bytes 12292
  1.3 3.4 %copy-start.6 = (f32[1,4,8,32]{3,2,1,0:T(8,128)S(1)}, f32[1,4,8,32]{3,2,1,0:T(8,128)}, u32[]{:S(2)}) copy-start(f32[1,4,8,32]{3,2,1,0:T(8,128)} %weight_ref.2) | copy-start | bytes 12292
  1.3 3.4 %copy-start.7 = (f32[2,2,16]{2,1,0:T(2,128)S(1)}, f32[2,2,16]{2,1,0:T(2,128)}, u32[]{:S(2)}) copy-start(f32[2,2,16]{2,1,0:T(2,128)} %filt_ref.1) | copy-start | bytes 772
  1.3 3.4 %copy-start.8 = (f32[2,2]{1,0:T(2,128)S(1)}, f32[2,2]{1,0:T(2,128)}, u32[]{:S(2)}) copy-start(f32[2,2]{1,0:T(2,128)} %chan_ref.1) | copy-start | bytes 52
  1.3 3.4 %copy-start.9 = (s32[1,8]{1,0:T(1,128)S(1)}, s32[1,8]{1,0:T(1,128)}, u32[]{:S(2)}) copy-start(s32[1,8]{1,0:T(1,128)} %counts_ref.1) | copy-start | bytes 100
  1.3 7.1 %copy-start.4 = (bf16[2,2,512,256]{3,2,1,0:T(8,128)(2,1)S(1)}, bf16[2,2,512,256]{3,2,1,0:T(8,128)(2,1)}, u32[]{:S(2)}) copy-start(bf16[2,2,512,256]{3,2,1,0:T(8,128)(2,1)} %raw_ref.3) | copy-start | bytes 3145732
  1.7 6.7 %copy-start = (bf16[1,256,1024]{2,1,0:T(8,128)(2,1)S(1)}, bf16[1,256,1024]{2,1,0:T(8,128)(2,1)}, u32[]{:S(2)}) copy-start(bf16[1,256,1024]{2,1,0:T(8,128)(2,1)} %steer_ref.3) | copy-start | bytes 1572868
  1.7 7.8 %collective-permute-start = (bf16[2,2,16,512]{3,2,1,0:T(8,128)(2,1)S(1)}, bf16[2,2,16,512]{3,2,1,0:T(8,128)(2,1)S(1)}, u32[]{:S(2)}, u32[]{:S(2)}) collective-permute-start(bf16[2,2,16,512]{3,2,1,0:T(8,128)(2,1)S(1)} %shard_map.93), channel_id=1, source_target_pairs={{0,2},{2,0},{1,3},{3,1},{4,6},{6,4},{5,7},{7,5},{8,10},{10,8},{9,1... | collective-permute-start | bytes 196616 | tf_op jit(solution)/shard_map/ppermute | solution.py:274
  5.8 6.3 %collective-permute-start.2 = (bf16[144,256]{1,0:T(8,128)(2,1)S(1)}, bf16[144,256]{1,0:T(8,128)(2,1)S(1)}, u32[]{:S(2)}, u32[]{:S(2)}) collective-permute-start(bf16[144,256]{1,0:T(8,128)(2,1)S(1)} %get-tuple-element.13.pack_ref), channel_id=1, source_target_pairs={{0,8},{4,12},{8,0},{12,4},{1,9},{5,13},{9,1},{13,5},{2,10},{6,14},... | collective-permute-start | bytes 221192 | tf_op jit(solution)/shard_map/ppermute | solution.py:268
  10.1 5.0 %collective-permute-start.1 = (bf16[256,256]{1,0:T(8,128)(2,1)S(1)}, bf16[256,256]{1,0:T(8,128)(2,1)S(1)}, u32[]{:S(2)}, u32[]{:S(2)}) collective-permute-start(bf16[256,256]{1,0:T(8,128)(2,1)S(1)} %shard_map.94.own_ref), channel_id=1, source_target_pairs={{0,4},{4,0},{8,12},{12,8},{1,5},{5,1},{9,13},{13,9},{2,6},{6,2},{1... | collective-permute-start | bytes 393224 | tf_op jit(solution)/shard_map/ppermute | solution.py:268
  12.1 1.3 %collective-permute-start.3 = (bf16[144,256]{1,0:T(8,128)(2,1)S(1)}, bf16[144,256]{1,0:T(8,128)(2,1)S(1)}, u32[]{:S(2)}, u32[]{:S(2)}) collective-permute-start(bf16[144,256]{1,0:T(8,128)(2,1)S(1)} %collective-permute-done.2.near_ref), channel_id=1, source_target_pairs={{0,1},{1,0},{2,3},{3,2},{4,5},{5,4},{6,7},{7,6},{8,9},{9,8},{10,11... | collective-permute-start | bytes 221192 | tf_op jit(solution)/shard_map/ppermute | solution.py:268
  15.1 11.1 %copy-start.2 = (s32[1,8,32]{2,1,0:T(8,128)S(1)}, s32[1,8,32]{2,1,0:T(8,128)}, u32[]{:S(2)}) copy-start(s32[1,8,32]{2,1,0:T(8,128)} %pixel_ref.1) | copy-start | bytes 3076

commit v3 on v2

--- a/solution.py
+++ b/solution.py
@@ -14,7 +14,6 @@
 F32 = jnp.float32
 BF16 = jnp.bfloat16
 VMEM = pl.BlockSpec(memory_space=pltpu.VMEM)
-SMEM = pl.BlockSpec(memory_space=pltpu.SMEM)
 NT = (((1,), (1,)), ((), ()))
 
 
@@ -26,99 +25,116 @@
     return lax.dot_general(a, b, NT, preferred_element_type=F32)
 
 
-def rim_kernel(raw_ref, edge_ref):
+def own_rims(rng_axis, rng_size, bins):
+    if rng_size == 2:
+        return [jnp.where(lax.axis_index(rng_axis) == 0, bins - EDGE, 0)]
+    return [0, bins - EDGE]
+
+
+def far_rims(rng_axis, rng_size, bins):
+    if rng_size == 2:
+        return [jnp.where(lax.axis_index(rng_axis) == 0, bins, -EDGE)]
+    return [bins, -EDGE]
+
+
+def rim_kernel(rng_axis, rng_size, raw_ref, edge_ref):
     channels, _, _, bins = raw_ref.shape
-    row = lax.broadcasted_iota(jnp.int32, (2 * EDGE, bins), 0)
-    column = lax.broadcasted_iota(jnp.int32, (2 * EDGE, bins), 1)
-    wanted = jnp.where(row < EDGE, row, row + bins - 2 * EDGE)
-    pick = (column == wanted).astype(F32).astype(BF16)
-    for c in range(channels):
-        for part in range(2):
-            edge_ref[c, part] = dot_nt(pick, raw_ref[c, part]).astype(BF16)
-
-
-def prepare_kernel(
-    bins, chan_axis, merge_ref, index_ref, weight_ref, filt_ref, chan_ref, counts_ref,
-    pack_ref, band_ref, end_ref, mix_ref,
-):
-    channels = filt_ref.shape[0]
+    count = channels * 2 * EDGE
+    row = lax.broadcasted_iota(jnp.int32, (2 * EDGE, LANES), 0)
+    column = lax.broadcasted_iota(jnp.int32, (2 * EDGE, LANES), 1)
+    for side, first in enumerate(own_rims(rng_axis, rng_size, bins)):
+        lane = pl.multiple_of(first - first % LANES, LANES)
+        pick = (column == (row & (EDGE - 1)) + first - lane).astype(F32).astype(BF16)
+        lines = [
+            dot_nt(pick, raw_ref[c, part, :, pl.ds(lane, LANES)])[:EDGE]
+            for c in range(channels)
+            for part in range(2)
+        ]
+        edge_ref[side * count : (side + 1) * count, :] = jnp.concatenate(lines, 0).astype(BF16)
+
+
+def pack_kernel(shift, chan_axis, merge_ref, index_ref, weight_ref, counts_ref, pack_ref):
     half = merge_ref.shape[3] // 2
     last = merge_ref.shape[1] - 1
     core = lax.axis_index(chan_axis) % 2
     rows = pl.ds(pl.multiple_of(core * half, half), half)
     pack_ref[:half, :] = merge_ref[0, last, 1, rows, :]
-    taps = filt_ref.shape[2]
+    taps, owners, slots = index_ref.shape[1:]
+    per_row = ROW // slots
+    slot = lax.broadcasted_iota(jnp.int32, (taps, slots), 1)
+    for first in range(0, owners, per_row):
+        index = jnp.concatenate([index_ref[0, :, first + k, :] for k in range(per_row)], 1)
+        weight = jnp.concatenate(
+            [
+                jnp.where(slot < counts_ref[:, first + k : first + k + 1], weight_ref[0, :, first + k, :], 0.0)
+                for k in range(per_row)
+            ],
+            1,
+        )
+        coarse = weight.astype(BF16).astype(F32)
+        beam = (index >> shift).astype(F32)
+        column = (index & ((1 << shift) - 1)).astype(F32)
+        lines = jnp.concatenate([beam, column, coarse, weight - coarse], 0).astype(BF16)
+        base = half + 4 * taps * (first // per_row)
+        pack_ref[base : base + 4 * taps, :] = lines
+
+
+def filter_kernel(bins, rng_axis, rng_size, filt_ref, chan_ref, band_ref, end_ref, mix_ref):
+    channels, parts, taps = filt_ref.shape
+    rows = jnp.concatenate([filt_ref[c] for c in range(channels)], 0).astype(BF16)
+    source = lax.broadcasted_iota(jnp.int32, (taps, LANES), 0)
+    target = lax.broadcasted_iota(jnp.int32, (taps, LANES), 1)
+    mirror = (source == ((EDGE - target) & (LANES - 1))).astype(F32).astype(BF16)
+    bases = dot(rows, mirror)
     row = lax.broadcasted_iota(jnp.int32, (LANES, LANES), 0)
     column = lax.broadcasted_iota(jnp.int32, (LANES, LANES), 1)
     far = column - row
-    place = (EDGE - far) & (LANES - 1)
-    rings = [[jnp.zeros((LANES, LANES), F32) for _ in range(2)] for _ in range(channels)]
-    for k in range(taps):
-        here = place == k
-        for c in range(channels):
-            for part in range(2):
-                rings[c][part] = jnp.where(here, filt_ref[c, part, k], rings[c][part])
     zero = jnp.zeros((LANES, LANES), BF16)
     count = bins // LANES
+    firsts = far_rims(rng_axis, rng_size, bins)
+    tails = []
     for c in range(channels):
-        for part in range(2):
-            ring = rings[c][part]
+        tails.append([])
+        for part in range(parts):
+            base = bases[c * parts + part : c * parts + part + 1]
+            ring = pltpu.roll(
+                jnp.broadcast_to(base, (LANES, LANES)), 0, 1, stride=1, stride_axis=0
+            )
+            below = jnp.where(far >= 64, ring, 0.0)
+            above = jnp.where(far <= -64, ring, 0.0)
             blocks = {
                 0: jnp.where((far < 64) & (far > -64), ring, 0.0).astype(BF16),
-                1: jnp.where(far >= 64, ring, 0.0).astype(BF16),
-                -1: jnp.where(far <= -64, ring, 0.0).astype(BF16),
+                1: below.astype(BF16),
+                -1: above.astype(BF16),
             }
             for i in range(count):
                 for o in range(count):
                     band_ref[
                         c, part, i * LANES : (i + 1) * LANES, o * LANES : (o + 1) * LANES
                     ] = blocks.get(i - o, zero)
-    row = lax.broadcasted_iota(jnp.int32, (2 * EDGE, bins), 0)
-    column = lax.broadcasted_iota(jnp.int32, (2 * EDGE, bins), 1)
-    place = jnp.where(row < EDGE, row + bins, row - 2 * EDGE) - column + EDGE
-    tails = [[jnp.zeros((2 * EDGE, bins), F32) for _ in range(2)] for _ in range(channels)]
-    for k in range(taps):
-        here = place == k
+            blank = jnp.zeros((EDGE, bins - LANES), F32)
+            ahead = jnp.concatenate([blank, below[:EDGE]], 1)
+            behind = jnp.concatenate([above[LANES - EDGE :], blank], 1)
+            if rng_size == 2:
+                tails[c].append([jnp.where(firsts[0] > 0, ahead, behind)])
+            else:
+                tails[c].append([ahead, behind])
+    nothing = jnp.zeros((2 * EDGE, bins), BF16)
+    for side in range(len(firsts)):
         for c in range(channels):
-            for part in range(2):
-                tails[c][part] = jnp.where(here, filt_ref[c, part, k], tails[c][part])
-    nothing = jnp.zeros((2 * EDGE, bins), BF16)
+            re, im = tails[c][0][side], tails[c][1][side]
+            blocks = [jnp.concatenate(pair, 0).astype(BF16) for pair in ((re, -im), (im, re))]
+            for d in range(channels):
+                for q in range(2):
+                    top = ((q * len(firsts) + side) * channels + d) * 2 * EDGE
+                    end_ref[top : top + 2 * EDGE, c * bins : (c + 1) * bins] = (
+                        blocks[q] if c == d else nothing
+                    )
     for c in range(channels):
-        re, im = tails[c]
-        for d in range(channels):
-            quads = [re, -im, im, re]
-            for q in range(4):
-                top = (q // 2) * 2 * channels + 2 * d + q % 2
-                end_ref[
-                    top * 2 * EDGE : (top + 1) * 2 * EDGE, c * bins : (c + 1) * bins
-                ] = quads[q].astype(BF16) if c == d else nothing
-        for part in range(2):
-            mix_ref[8 * (2 * c + part) : 8 * (2 * c + part + 1), :] = jnp.full(
-                (8, bins), chan_ref[c, part], F32
+        for part in range(parts):
+            mix_ref[8 * (2 * c + part) : 8 * (2 * c + part + 1), :] = jnp.broadcast_to(
+                chan_ref[c : c + 1, part : part + 1], (8, bins)
             )
-    taps, owners, slots = index_ref.shape[1:]
-    per_row = ROW // slots
-    slot = lax.broadcasted_iota(jnp.int32, (taps, slots), 1)
-    lines = []
-    for first in range(0, owners, per_row):
-        parts = []
-        for o in range(first, first + per_row):
-            index = index_ref[0, :, o, :]
-            weight = jnp.where(slot < counts_ref[0, o], weight_ref[0, :, o, :], 0.0)
-            coarse = weight.astype(BF16).astype(F32)
-            parts.append(
-                jnp.concatenate(
-                    [
-                        (index // bins).astype(F32),
-                        (index % bins).astype(F32),
-                        coarse,
-                        weight - coarse,
-                    ],
-                    0,
-                )
-            )
-        lines.append(jnp.concatenate(parts, 1))
-    pack_ref[half:, :] = jnp.concatenate(lines, 0).astype(BF16)
 
 
 def turned(value, mix_ref, channel):
@@ -142,23 +158,16 @@
     out_ref[...] = total
 
 
-def edge_kernel(rng_axis, rng_size, main_ref, edge_ref, steer_ref, end_ref, mix_ref, out_ref):
-    channels, _, _, pulses = edge_ref.shape
+def edge_kernel(main_ref, edge_ref, steer_ref, end_ref, mix_ref, out_ref):
+    count, pulses = edge_ref.shape
     bins = main_ref.shape[1]
-    count = channels * 4 * EDGE
-    block = lax.axis_index(rng_axis)
-    row = lax.broadcasted_iota(jnp.int32, (count, pulses), 0)
-    below = (row & EDGE) > 0
-    first = jnp.where(block > 0, 1.0, 0.0)
-    last = jnp.where(block < rng_size - 1, 1.0, 0.0)
-    keep = jnp.where(below, first, last).astype(BF16)
-    edges = edge_ref[...].reshape(count, pulses) * keep
+    edges = edge_ref[...]
     nothing = jnp.zeros((count, pulses), BF16)
     taken = dot_nt(steer_ref[0, :, :pulses], jnp.concatenate([edges, nothing], 0))
     taken = taken + dot_nt(steer_ref[0, :, pulses:], jnp.concatenate([nothing, edges], 0))
     images = dot(taken.astype(BF16), end_ref[...])
     total = main_ref[...]
-    for c in range(channels):
+    for c in range(end_ref.shape[1] // bins):
         total = total + turned(images[:, c * bins : (c + 1) * bins], mix_ref, c)
     out_ref[...] = total.astype(BF16)
 
@@ -272,9 +281,10 @@
     count = lax.axis_size("rng")
     if count == 2:
         return lax.ppermute(edges, "rng", [(0, 1), (1, 0)])
-    after = lax.ppermute(edges, "rng", [(i + 1, i) for i in range(count - 1)])
-    before = lax.ppermute(edges, "rng", [(i, i + 1) for i in range(count - 1)])
-    return jnp.concatenate([after[:, :, :EDGE], before[:, :, EDGE:]], 2)
+    half = edges.shape[0] // 2
+    after = lax.ppermute(edges[:half], "rng", [(i + 1, i) for i in range(count - 1)])
+    before = lax.ppermute(edges[half:], "rng", [(i, i + 1) for i in range(count - 1)])
+    return jnp.concatenate([after, before], 0)
 
 
 def local(raw, filt, steer, chan_w, merge_w, samp_index, samp_weight, counts, pixel_id):
@@ -283,29 +293,34 @@
     levels = merge_w.shape[1]
     taps, owners, slots = samp_index.shape[1:]
     extra = 4 * taps * owners * slots // ROW
+    blocks = lax.axis_size("rng")
+    rims = channels * 2 * EDGE * (1 if blocks == 2 else 2)
     edges = call(
-        rim_kernel,
-        shape((channels, 2, 2 * EDGE, pulses), BF16),
+        functools.partial(rim_kernel, "rng", blocks),
+        shape((rims, pulses), BF16),
         [VMEM],
         VMEM,
         flops=2**32,
         nbytes=2**24,
     )(raw)
     beside = neighbour_edges(edges)
-    pack, bands, ends, mix = call(
-        functools.partial(prepare_kernel, bins, "chan"),
+    pack = call(
+        functools.partial(pack_kernel, bins.bit_length() - 1, "chan"),
+        shape((size // 2 + extra, ROW), BF16),
+        [VMEM] * 4,
+        VMEM,
+    )(merge_w, samp_index, samp_weight, counts)
+    near = swapped(pack, "sub", levels - 1)
+    bands, ends, mix = call(
+        functools.partial(filter_kernel, bins, "rng", blocks),
         (
-            shape((size // 2 + extra, ROW), BF16),
             shape((channels, 2, bins, bins), BF16),
-            shape((channels * 8 * EDGE, channels * bins), BF16),
+            shape((2 * rims, channels * bins), BF16),
             shape((16 * channels, bins), F32),
         ),
-        [VMEM] * 3 + [SMEM] * 3,
-        (VMEM,) * 4,
-        flops=2**28,
-        nbytes=2**20,
-    )(merge_w, samp_index, samp_weight, filt, chan_w, counts)
-    near = swapped(pack, "sub", levels - 1)
+        [VMEM] * 2,
+        (VMEM,) * 3,
+    )(filt, chan_w)
     main = call(
         image_kernel,
         shape((size, bins), F32),
@@ -315,7 +330,7 @@
         nbytes=2**21,
     )(raw, steer, bands, mix)
     polar = call(
-        functools.partial(edge_kernel, "rng", lax.axis_size("rng")),
+        edge_kernel,
         shape((size, bins), BF16),
         [VMEM] * 5,
         VMEM,

time: 27.3 us -> 26.8 us (0.982)
  Pallas kernels: 5.07 us -> 4.27 us
  blocking collectives: 10 us -> 10.3 us
    pallas_call x3 -> x4, Pallas kernels: 1.99 us -> 1.18 us  [the longest x1 0.55 us: local(): call(edge_kernel, shape((size, bins), BF16), [VMEM] * 5, VMEM, flops=2 **...]
    all_to_all x1, blocking collectives: 10 us -> 10.3 us  [local(): lax.all_to_all(outgoing, ('chan', 'sub', 'rng'), split_axis=0, concat_axi...]
  transfers between devices with their start and end apart: 4 -> 4, of which waited for: 3 -> 3; matrix products, arithmetic and copies ran while one was open for 0% -> 0% of each run, Pallas kernels for 10% -> 8%
where the time goes in v3:
time: 26.8 us; the launch traced here: 26.7 us
  blocking collectives  10.3 us (38%)
  starting transfers between devices  7.31 us (27%)
  Pallas kernels  4.27 us (16%)
  waiting for transfers between devices  3.39 us (13%)
  local copies, waits for them, and re-layouts  1.31 us (5%)
    all_to_all x1, blocking collectives, local(): lax.all_to_all(outgoing, ('chan', 'sub', 'rng'), split_axis=0, concat_axi...  10.3 us
    ppermute x3, starting transfers between devices, swapped(): lax.ppermute(value, axis, [(i, i ^ 1 << bit) for i in range(lax.axis_size...  4.3 us
    ppermute x3, waiting for transfers between devices, swapped(): lax.ppermute(value, axis, [(i, i ^ 1 << bit) for i in range(lax.axis_size...  3.39 us
    ppermute x1, starting transfers between devices, neighbour_edges(): return lax.ppermute(edges, 'rng', [(0, 1), (1, 0)])  3.01 us
    unnamed x20, local copies, waits for them, and re-layouts  1.31 us
    pallas_call x1, Pallas kernels, local(): call(image_kernel, shape((size, bins), F32), [VMEM] * 4, VMEM, flops=2 **...  1.1 us
    pallas_call x1, Pallas kernels, local(): call(functools.partial(sample_kernel, taps, slots, 'chan'), shape((2 * ow...  1.07 us
    pallas_call x1, Pallas kernels, local(): call(scatter_kernel, shape((2, PIX_OWN), F32), [VMEM, VMEM], VMEM, scratc...  0.91 us
  transfers between devices with their start and end apart: 4, of which 3 were waited for; matrix products, arithmetic and copies ran while one was open for 0% of the time, Pallas kernels for 8%

profile of v3, /device:TPU:0, one launch (start us, length us, event | category | flops | bytes accessed | tf_op | source)
XLA Modules:
  0.0 26.7 jit_solution(13557326347038535142)
XLA Ops:
  0.0 0.0 copy-start
  0.0 0.0 copy-start.2
  0.0 0.0 copy-start.3
  0.0 0.0 copy-start.7
  0.0 0.0 copy-start.8
  0.0 1.3 %copy-done.8 = bf16[2,2,512,256]{3,2,1,0:T(8,128)(2,1)S(1)} copy-done((bf16[2,2,512,256]{3,2,1,0:T(8,128)(2,1)S(1)}, bf16[2,2,512,256]{3,2,1,0:T(8,128)(2,1)}, u32[]{:S(2)}) %copy-start.8) | copy-done | bytes 1048600
  1.3 0.0 copy-start.9
  1.3 0.2 shard_map.93
  1.5 0.0 copy-start.5
  1.5 0.0 copy-start.6
  1.5 0.0 copy-start.1
  1.6 3.0 %collective-permute-start = (bf16[32,512]{1,0:T(8,128)(2,1)S(1)}, bf16[32,512]{1,0:T(8,128)(2,1)S(1)}, u32[]{:S(2)}, u32[]{:S(2)}) collective-permute-start(bf16[32,512]{1,0:T(8,128)(2,1)S(1)} %shard_map.93), channel_id=1, source_target_pairs={{0,2},{2,0},{1,3},{3,1},{4,6},{6,4},{5,7},{7,5},{8,10},{10,8},{9,1... | collective-permute-start | bytes 98312 | tf_op jit(solution)/shard_map/ppermute | solution.py:283
  4.6 0.0 copy-done
  4.6 0.0 copy-done.2
  4.6 0.0 copy-done.3
  4.6 0.0 copy-done.7
  4.6 0.2 shard_map.95.pack_ref
  4.7 2.7 %collective-permute-start.2 = (bf16[144,256]{1,0:T(8,128)(2,1)S(1)}, bf16[144,256]{1,0:T(8,128)(2,1)S(1)}, u32[]{:S(2)}, u32[]{:S(2)}) collective-permute-start(bf16[144,256]{1,0:T(8,128)(2,1)S(1)} %shard_map.95.pack_ref), channel_id=1, source_target_pairs={{0,8},{4,12},{8,0},{12,4},{1,9},{5,13},{9,1},{13,5},{2,10},{6,14},... | collective-permute-start | bytes 221192 | tf_op jit(solution)/shard_map/ppermute | solution.py:277
  7.4 0.0 copy-done.5
  7.4 0.0 copy-done.6
  7.4 0.2 shard_map.91
  7.7 0.0 copy-done.9
  7.7 0.0 copy-done.1
  7.7 1.1 %shard_map.92.main_ref = f32[256,256]{1,0:T(8,128)S(1)} custom-call(bf16[2,2,512,256]{3,2,1,0:T(8,128)(2,1)S(1)} %copy-done.9, bf16[1,256,1024]{2,1,0:T(8,128)(2,1)S(1)} %copy-done.1, bf16[2,2,256,256]{3,2,1,0:T(8,128)(2,1)S(1)} %get-tuple-element.9.band_ref, f32[32,256]{1,0:T(8,128)S(1)} %get-tuple-element.10.mix_ref), custom_call_target="tpu_custom_call" | custom-call | flops 1073741824 | bytes 2097152 | tf_op jit(solution)/shard_map/pallas_call | solution.py:324
  8.8 0.0 collective-permute-done.edge_ref
  8.8 0.6 %shard_map.94.own_ref = bf16[256,256]{1,0:T(8,128)(2,1)S(1)} custom-call(f32[256,256]{1,0:T(8,128)S(1)} %shard_map.92.main_ref, bf16[32,512]{1,0:T(8,128)(2,1)S(1)} %collective-permute-done.edge_ref, bf16[1,256,1024]{2,1,0:T(8,128)(2,1)S(1)} %copy-done.1, bf16[64,512]{1,0:T(8,128)(2,1)S(1)} %get-tuple-element.11.end_ref, f32[32,256]{1,0:T(8,128)S(1)} %get-tuple-element.10.mix_ref), custom_call_target="tpu_custom_call" | custom-call | flops 134217728 | bytes 1048576 | tf_op jit(solution)/shard_map/pallas_call | solution.py:332
  9.3 1.6 %collective-permute-start.1 = (bf16[256,256]{1,0:T(8,128)(2,1)S(1)}, bf16[256,256]{1,0:T(8,128)(2,1)S(1)}, u32[]{:S(2)}, u32[]{:S(2)}) collective-permute-start(bf16[256,256]{1,0:T(8,128)(2,1)S(1)} %shard_map.94.own_ref), channel_id=1, source_target_pairs={{0,4},{4,0},{8,12},{12,8},{1,5},{5,1},{9,13},{13,9},{2,6},{6,2},{1... | collective-permute-start | bytes 393224 | tf_op jit(solution)/shard_map/ppermute | solution.py:277
  11.0 0.2 collective-permute-done.2.near_ref
  11.2 0.0 collective-permute-start.3
  11.2 1.3 %collective-permute-done.3.far_ref = bf16[144,256]{1,0:T(8,128)(2,1)S(1)} collective-permute-done((bf16[144,256]{1,0:T(8,128)(2,1)S(1)}, bf16[144,256]{1,0:T(8,128)(2,1)S(1)}, u32[]{:S(2)}, u32[]{:S(2)}) %collective-permute-start.3) | collective-permute-done | bytes 73760 | tf_op jit(solution)/shard_map/ppermute | solution.py:277
  12.5 1.9 %collective-permute-done.1.other_ref = bf16[256,256]{1,0:T(8,128)(2,1)S(1)} collective-permute-done((bf16[256,256]{1,0:T(8,128)(2,1)S(1)}, bf16[256,256]{1,0:T(8,128)(2,1)S(1)}, u32[]{:S(2)}, u32[]{:S(2)}) %collective-permute-start.1) | collective-permute-done | bytes 131104 | tf_op jit(solution)/shard_map/ppermute | solution.py:277
  14.4 0.0 copy-start.4
  14.4 1.1 %shard_map.96 = f32[16,128]{1,0:T(8,128)S(1)} custom-call(bf16[1,2,2,256,256]{4,3,2,1,0:T(8,128)(2,1)S(1)} %copy-done, bf16[256,256]{1,0:T(8,128)(2,1)S(1)} %shard_map.94.own_ref, bf16[256,256]{1,0:T(8,128)(2,1)S(1)} %collective-permute-done.1.other_ref, bf16[144,256]{1,0:T(8,128)(2,1)S(1)} %shard_map.95.pack_ref, ...), custom_call_target="tpu_custom_call" | custom-call | flops 268435456 | bytes 1048576 | tf_op jit(solution)/shard_map/pallas_call | solution.py:355
  15.5 10.3 %all_to_all.11 = f32[16,1,128]{2,1,0:T(1,128)S(1)} all-to-all(f32[16,1,128]{2,1,0:T(1,128)S(1)} %bitcast.4), channel_id=1, replica_groups=mesh['groups'=2,'sub'=4,'rng'=2,'chan'=2] {'chan','sub','rng'}, dimensions={0} | all-to-all | bytes 16384 | tf_op jit(solution)/shard_map/all_to_all | solution.py:363
  25.8 0.0 copy-done.4
  25.8 0.9 %shard_map.97 = f32[2,4096]{1,0:T(2,128)} custom-call(f32[16,128]{1,0:T(8,128)S(1)} %bitcast.5, s32[1,8,32]{2,1,0:T(8,128)S(1)} %copy-done.4), custom_call_target="tpu_custom_call" | custom-call | tf_op jit(solution)/shard_map/pallas_call | solution.py:366
Async XLA Ops:
  0.0 4.6 %copy-start = (bf16[1,2,2,256,256]{4,3,2,1,0:T(8,128)(2,1)S(1)}, bf16[1,2,2,256,256]{4,3,2,1,0:T(8,128)(2,1)}, u32[]{:S(2)}) copy-start(bf16[1,2,2,256,256]{4,3,2,1,0:T(8,128)(2,1)} %weight_ref.3) | copy-start | bytes 1572868
  0.0 4.6 %copy-start.2 = (s32[1,4,8,32]{3,2,1,0:T(8,128)S(1)}, s32[1,4,8,32]{3,2,1,0:T(8,128)}, u32[]{:S(2)}) copy-start(s32[1,4,8,32]{3,2,1,0:T(8,128)} %index_ref.1) | copy-start | bytes 12292
  0.0 4.6 %copy-start.3 = (f32[1,4,8,32]{3,2,1,0:T(8,128)S(1)}, f32[1,4,8,32]{3,2,1,0:T(8,128)}, u32[]{:S(2)}) copy-start(f32[1,4,8,32]{3,2,1,0:T(8,128)} %weight_ref.2) | copy-start | bytes 12292
  0.0 4.6 %copy-start.7 = (s32[1,8]{1,0:T(1,128)S(1)}, s32[1,8]{1,0:T(1,128)}, u32[]{:S(2)}) copy-start(s32[1,8]{1,0:T(1,128)} %counts_ref.1) | copy-start | bytes 100
  0.0 1.3 %copy-start.8 = (bf16[2,2,512,256]{3,2,1,0:T(8,128)(2,1)S(1)}, bf16[2,2,512,256]{3,2,1,0:T(8,128)(2,1)}, u32[]{:S(2)}) copy-start(bf16[2,2,512,256]{3,2,1,0:T(8,128)(2,1)} %raw_ref.3) | copy-start | bytes 3145732
  1.3 6.4 %copy-start.9 = (bf16[2,2,512,256]{3,2,1,0:T(8,128)(2,1)S(1)}, bf16[2,2,512,256]{3,2,1,0:T(8,128)(2,1)}, u32[]{:S(2)}) copy-start(bf16[2,2,512,256]{3,2,1,0:T(8,128)(2,1)} %raw_ref.3) | copy-start | bytes 3145732
  1.5 5.9 %copy-start.5 = (f32[2,2,16]{2,1,0:T(2,128)S(1)}, f32[2,2,16]{2,1,0:T(2,128)}, u32[]{:S(2)}) copy-start(f32[2,2,16]{2,1,0:T(2,128)} %filt_ref.1) | copy-start | bytes 772
  1.5 5.9 %copy-start.6 = (f32[2,2]{1,0:T(2,128)S(1)}, f32[2,2]{1,0:T(2,128)}, u32[]{:S(2)}) copy-start(f32[2,2]{1,0:T(2,128)} %chan_ref.1) | copy-start | bytes 52
  1.5 6.1 %copy-start.1 = (bf16[1,256,1024]{2,1,0:T(8,128)(2,1)S(1)}, bf16[1,256,1024]{2,1,0:T(8,128)(2,1)}, u32[]{:S(2)}) copy-start(bf16[1,256,1024]{2,1,0:T(8,128)(2,1)} %steer_ref.3) | copy-start | bytes 1572868
  1.6 7.2 %collective-permute-start = (bf16[32,512]{1,0:T(8,128)(2,1)S(1)}, bf16[32,512]{1,0:T(8,128)(2,1)S(1)}, u32[]{:S(2)}, u32[]{:S(2)}) collective-permute-start(bf16[32,512]{1,0:T(8,128)(2,1)S(1)} %shard_map.93), channel_id=1, source_target_pairs={{0,2},{2,0},{1,3},{3,1},{4,6},{6,4},{5,7},{7,5},{8,10},{10,8},{9,1... | collective-permute-start | bytes 98312 | tf_op jit(solution)/shard_map/ppermute | solution.py:283
  4.7 6.5 %collective-permute-start.2 = (bf16[144,256]{1,0:T(8,128)(2,1)S(1)}, bf16[144,256]{1,0:T(8,128)(2,1)S(1)}, u32[]{:S(2)}, u32[]{:S(2)}) collective-permute-start(bf16[144,256]{1,0:T(8,128)(2,1)S(1)} %shard_map.95.pack_ref), channel_id=1, source_target_pairs={{0,8},{4,12},{8,0},{12,4},{1,9},{5,13},{9,1},{13,5},{2,10},{6,14},... | collective-permute-start | bytes 221192 | tf_op jit(solution)/shard_map/ppermute | solution.py:277
  9.3 5.0 %collective-permute-start.1 = (bf16[256,256]{1,0:T(8,128)(2,1)S(1)}, bf16[256,256]{1,0:T(8,128)(2,1)S(1)}, u32[]{:S(2)}, u32[]{:S(2)}) collective-permute-start(bf16[256,256]{1,0:T(8,128)(2,1)S(1)} %shard_map.94.own_ref), channel_id=1, source_target_pairs={{0,4},{4,0},{8,12},{12,8},{1,5},{5,1},{9,13},{13,9},{2,6},{6,2},{1... | collective-permute-start | bytes 393224 | tf_op jit(solution)/shard_map/ppermute | solution.py:277
  11.2 1.3 %collective-permute-start.3 = (bf16[144,256]{1,0:T(8,128)(2,1)S(1)}, bf16[144,256]{1,0:T(8,128)(2,1)S(1)}, u32[]{:S(2)}, u32[]{:S(2)}) collective-permute-start(bf16[144,256]{1,0:T(8,128)(2,1)S(1)} %collective-permute-done.2.near_ref), channel_id=1, source_target_pairs={{0,1},{1,0},{2,3},{3,2},{4,5},{5,4},{6,7},{7,6},{8,9},{9,8},{10,11... | collective-permute-start | bytes 221192 | tf_op jit(solution)/shard_map/ppermute | solution.py:277
  14.4 11.4 %copy-start.4 = (s32[1,8,32]{2,1,0:T(8,128)S(1)}, s32[1,8,32]{2,1,0:T(8,128)}, u32[]{:S(2)}) copy-start(s32[1,8,32]{2,1,0:T(8,128)} %pixel_ref.1) | copy-start | bytes 3076

commit v4 on v3

v4 whole, which is shorter than its diff:
```python
import functools

import jax
import jax.numpy as jnp
from jax import lax
from jax.experimental import pallas as pl
from jax.experimental.pallas import tpu as pltpu
from jax.sharding import PartitionSpec as P

PIX_OWN = 4096
LANES = 128
ROW = 256
EDGE = 8
F32 = jnp.float32
BF16 = jnp.bfloat16
VMEM = pl.BlockSpec(memory_space=pltpu.VMEM)
NT = (((1,), (1,)), ((), ()))


def dot(a, b):
    return jnp.dot(a, b, preferred_element_type=F32)


def dot_nt(a, b):
    return lax.dot_general(a, b, NT, preferred_element_type=F32)


def place_kernel(rng_axis, rng_size, place_ref):
    bins = place_ref.shape[1]
    block = lax.axis_index(rng_axis)
    row = lax.broadcasted_iota(jnp.int32, (2 * EDGE, bins), 0)
    column = lax.broadcasted_iota(jnp.int32, (2 * EDGE, bins), 1)
    after = jnp.where(block < rng_size - 1, bins - EDGE, 2 * bins)
    before = jnp.where(block > 0, -EDGE, 2 * bins)
    here = column == row + jnp.where(row < EDGE, after, before)
    place_ref[...] = here.astype(F32).astype(BF16)


def pack_kernel(
    shift, chan_axis, merge_ref, index_ref, weight_ref, counts_ref, _, pack_ref
):
    half = merge_ref.shape[3] // 2
    last = merge_ref.shape[1] - 1
    core = lax.axis_index(chan_axis) % 2
    rows = pl.ds(pl.multiple_of(core * half, half), half)
    pack_ref[:half, :] = merge_ref[0, last, 1, rows, :]
    taps, owners, slots = index_ref.shape[1:]
    per_row = ROW // slots
    slot = lax.broadcasted_iota(jnp.int32, (taps, slots), 1)
    for first in range(0, owners, per_row):
        index = jnp.concatenate([index_ref[0, :, first + k, :] for k in range(per_row)], 1)
        weight = jnp.concatenate(
            [
                jnp.where(slot < counts_ref[:, first + k : first + k + 1], weight_ref[0, :, first + k, :], 0.0)
                for k in range(per_row)
            ],
            1,
        )
        coarse = weight.astype(BF16).astype(F32)
        beam = (index >> shift).astype(F32)
        column = (index & ((1 << shift) - 1)).astype(F32)
        lines = jnp.concatenate([beam, column, coarse, weight - coarse], 0).astype(BF16)
        base = half + 4 * taps * (first // per_row)
        pack_ref[base : base + 4 * taps, :] = lines


def filter_kernel(bins, filt_ref, chan_ref, band_ref, outer_ref, mix_ref):
    channels, parts, taps = filt_ref.shape
    rows = jnp.concatenate([filt_ref[c] for c in range(channels)], 0).astype(BF16)
    source = lax.broadcasted_iota(jnp.int32, (taps, LANES), 0)
    target = lax.broadcasted_iota(jnp.int32, (taps, LANES), 1)
    mirror = (source == ((EDGE - target) & (LANES - 1))).astype(F32).astype(BF16)
    bases = dot(rows, mirror)
    forward = dot(rows, (source == target).astype(F32).astype(BF16))
    row = lax.broadcasted_iota(jnp.int32, (LANES, LANES), 0)
    column = lax.broadcasted_iota(jnp.int32, (LANES, LANES), 1)
    far = column - row
    zero = jnp.zeros((LANES, LANES), BF16)
    count = bins // LANES
    low = lax.broadcasted_iota(jnp.int32, (EDGE, LANES), 1) < LANES // 2
    blank = jnp.zeros((EDGE, bins - LANES), F32)

    def turning(base, size, shift):
        wide = jnp.broadcast_to(base, (size, LANES))
        return pltpu.roll(wide, shift, 1, stride=1, stride_axis=0)

    for c in range(channels):
        for part in range(parts):
            line = slice(c * parts + part, c * parts + part + 1)
            ring = turning(bases[line], LANES, 0)
            blocks = {
                0: jnp.where((far < 64) & (far > -64), ring, 0.0).astype(BF16),
                1: jnp.where(far >= 64, ring, 0.0).astype(BF16),
                -1: jnp.where(far <= -64, ring, 0.0).astype(BF16),
            }
            for i in range(count):
                for o in range(count):
                    band_ref[
                        c, part, i * LANES : (i + 1) * LANES, o * LANES : (o + 1) * LANES
                    ] = blocks.get(i - o, zero)
            lower = jnp.where(low, turning(forward[line], EDGE, LANES - 2 * EDGE), 0.0)
            upper = jnp.where(low, 0.0, turning(forward[line], EDGE, LANES - EDGE))
            outer = jnp.concatenate(
                [jnp.concatenate([lower, blank], 1), jnp.concatenate([blank, upper], 1)], 0
            )
            outer_ref[c, part] = outer.astype(BF16)
            mix_ref[8 * (2 * c + part) : 8 * (2 * c + part + 1), :] = jnp.broadcast_to(
                chan_ref[c : c + 1, part : part + 1], (8, bins)
            )


def turned(value, mix_ref, channel):
    half = value.shape[0] // 2
    re, im = value[:half], value[half:]
    wr = mix_ref[16 * channel : 16 * channel + 1, :]
    wi = mix_ref[16 * channel + 8 : 16 * channel + 9, :]
    return jnp.concatenate([wr * re - wi * im, wr * im + wi * re], 0)


def image_kernel(raw_ref, steer_ref, band_ref, outer_ref, mix_ref, out_ref, rim_ref):
    channels, _, pulses, _ = raw_ref.shape
    s_re, s_im = steer_ref[0, :, :pulses], steer_ref[0, :, pulses:]
    half = steer_ref.shape[1] // 2
    total = jnp.zeros(out_ref.shape, F32)
    rim = jnp.zeros(rim_ref.shape, F32)
    for c in range(channels):
        x_re, x_im = raw_ref[c, 0], raw_ref[c, 1]
        direct = (dot(s_re, x_re) + dot(s_im, x_im)).astype(BF16)
        cross = (dot(s_im, x_re) - dot(s_re, x_im)).astype(BF16)
        image = dot(direct, band_ref[c, 0]) + dot(cross, band_ref[c, 1])
        total = total + turned(image, mix_ref, c)
        side = dot_nt(outer_ref[c, 0], direct) + dot_nt(outer_ref[c, 1], cross)
        re, im = side[:, :half], side[:, half:]
        wr = mix_ref[16 * c : 16 * c + 1, :half]
        wi = mix_ref[16 * c + 8 : 16 * c + 9, :half]
        rim = rim + jnp.concatenate([wr * re - wi * im, wr * im + wi * re], 1)
    out_ref[...] = total.astype(BF16)
    rim_ref[...] = rim.astype(BF16)


def spread_rim(rim_ref, place_ref):
    return lax.dot_general(
        rim_ref[...], place_ref[...], (((0,), (0,)), ((), ())), preferred_element_type=F32
    )


def whole_kernel(main_ref, rim_ref, place_ref, out_ref):
    added = spread_rim(rim_ref, place_ref)
    out_ref[...] = (main_ref[...].astype(F32) + added).astype(BF16)


def merge_kernel(weight_ref, own_ref, other_ref, out_ref):
    mixed = dot(weight_ref[0, 0, 0], own_ref[...]) + dot(weight_ref[0, 0, 1], other_ref[...])
    out_ref[...] = mixed.astype(BF16)


def slot_masks(ref, base, t, taps, bins, half):
    rows = ref[base : base + 4 * taps, :].astype(F32)
    beam = rows[t : t + 1]
    column = rows[taps + t : taps + t + 1]
    weight = rows[2 * taps + t : 2 * taps + t + 1] + rows[3 * taps + t : 3 * taps + t + 1]
    bin_ids = lax.broadcasted_iota(jnp.int32, (bins, ROW), 0).astype(F32)
    beam_ids = lax.broadcasted_iota(jnp.int32, (half, ROW), 0).astype(F32)
    pick_bin = (bin_ids == column).astype(F32).astype(BF16)
    return pick_bin, jnp.where(beam_ids == beam, weight, 0.0)


def mixed_kernel(weight_ref, own_ref, own_rim_ref, other_rim_ref, place_ref, mixed_ref):
    own = (own_ref[...].astype(F32) + spread_rim(own_rim_ref, place_ref)).astype(BF16)
    other = spread_rim(other_rim_ref, place_ref).astype(BF16)
    mixed_ref[...] = dot(weight_ref[0, 0, 0], own) + dot(weight_ref[0, 0, 1], other)


def ready_kernel(taps, pack_ref, near_ref, pixel_ref, _, low_ref, high_ref, bin_ref, beam_ref):
    half, bins = beam_ref.shape[1], bin_ref.shape[1]
    owners, slots = pixel_ref.shape[1:]
    for block, ref in enumerate((pack_ref, near_ref)):
        for t in range(taps):
            pick_bin, pick_beam = slot_masks(ref, half, t, taps, bins, half)
            bin_ref[block * taps + t] = pick_bin
            beam_ref[block * taps + t] = pick_beam
    pixel = jnp.concatenate([pixel_ref[0, b : b + 1, :] for b in range(owners)], 1)
    count = owners * slots
    low = lax.broadcasted_iota(jnp.int32, (LANES, count), 0) == (pixel & (LANES - 1))
    low_ref[...] = low.astype(F32).astype(BF16)
    tall = high_ref.shape[0]
    high = lax.broadcasted_iota(jnp.int32, (tall, count), 0) == pixel // LANES
    high_ref[...] = high.astype(F32)


def sample_kernel(
    taps, slots, chan_axis, weight_ref, mixed_ref, other_ref, pack_ref, near_ref, far_ref, *refs
):
    ready, out_ref = refs[:-1], refs[-1]
    size, bins = other_ref.shape
    half = size // 2
    mixed = mixed_ref[...] + dot(weight_ref[0, 0, 1], other_ref[...])
    polar = mixed.astype(BF16)
    chunks = (pack_ref.shape[0] - half) // (4 * taps)
    per_row = ROW // slots
    owners = per_row * chunks
    even = lax.axis_index(chan_axis) % 2 == 0
    far = jnp.concatenate([near_ref[:half, :], far_ref[:half, :]], 0)
    values = {}
    for block, (merge, ref) in enumerate(((weight_ref[0, 1, 0], pack_ref), (far, near_ref))):
        merged = dot(merge, polar).astype(BF16)
        for chunk in range(chunks):
            base = half + 4 * taps * chunk
            sums = [jnp.zeros((half, ROW), F32) for _ in range(2)]
            for t in range(taps):
                if ready:
                    pick_bin = ready[0][block * taps + t]
                    pick_beam = ready[1][block * taps + t]
                else:
                    pick_bin, pick_beam = slot_masks(ref, base, t, taps, bins, half)
                found = dot(merged, pick_bin)
                sums[0] = sums[0] + found[:half] * pick_beam
                sums[1] = sums[1] + found[half:] * pick_beam
            flat = [jnp.sum(value, axis=0, keepdims=True) for value in sums]
            if block == 1:
                flat = [jnp.where(even, flat[0], flat[1]), jnp.where(even, flat[1], flat[0])]
            values[chunk] = values.get(chunk, []) + flat
    for chunk in range(chunks):
        rows = [
            jnp.concatenate([v[:, k * slots : (k + 1) * slots] for v in values[chunk]], 1)
            for k in range(per_row)
        ]
        tile = jnp.concatenate(rows, 0)
        for copy in range(2):
            top = copy * owners + chunk * per_row
            out_ref[top : top + per_row, :] = tile


def scatter_kernel(slots, value_ref, low_ref, high_ref, out_ref):
    owners = value_ref.shape[0] // 2
    total = value_ref[:owners, :] + value_ref[owners:, :]
    flat = []
    for part in range(2):
        lane = part * slots
        own = total[:, lane : lane + slots]
        far = total[:, 2 * slots + lane : 2 * slots + lane + slots]
        far = jnp.concatenate([far[owners // 2 :], far[: owners // 2]], 0)
        both = own + far
        flat.append(jnp.concatenate([both[b : b + 1] for b in range(owners)], 1))
    high = high_ref[...]
    tall = high.shape[0]
    spread = jnp.concatenate([high * flat[part] for part in range(2)], 0)
    coarse = spread.astype(BF16)
    fine = (spread - coarse.astype(F32)).astype(BF16)
    low = low_ref[...]
    image = dot_nt(coarse, low) + dot_nt(fine, low)
    for part in range(2):
        for h in range(tall):
            row = part * tall + h
            out_ref[part : part + 1, h * LANES : (h + 1) * LANES] = image[row : row + 1, :]


def shape(dims, dtype):
    return jax.ShapeDtypeStruct(dims, dtype)


def call(kernel, out_shape, in_specs, out_specs, flops=0, nbytes=0, scratch=(), grid=None):
    extra = {} if grid is None else {"grid": grid}
    return pl.pallas_call(
        kernel,
        out_shape=out_shape,
        in_specs=in_specs,
        out_specs=out_specs,
        scratch_shapes=list(scratch),
        cost_estimate=pl.CostEstimate(flops=flops, bytes_accessed=nbytes, transcendentals=0),
        compiler_params=pltpu.CompilerParams(vmem_limit_bytes=24 * 2**20),
        **extra,
    )


def whole(array):
    return pl.BlockSpec(array.shape, lambda i: (0,) * array.ndim)


def swapped(value, axis, bit):
    return lax.ppermute(value, axis, [(i, i ^ 1 << bit) for i in range(lax.axis_size(axis))])


def neighbour_rims(rim):
    count = lax.axis_size("rng")
    if count == 2:
        return lax.ppermute(rim, "rng", [(0, 1), (1, 0)])
    after = lax.ppermute(rim, "rng", [(i + 1, i) for i in range(count - 1)])
    before = lax.ppermute(rim, "rng", [(i, i + 1) for i in range(count - 1)])
    return jnp.concatenate([after[:EDGE], before[EDGE:]], 0)


def local(raw, filt, steer, chan_w, merge_w, samp_index, samp_weight, counts, pixel_id):
    channels, _, pulses, bins = raw.shape
    size = steer.shape[1]
    levels = merge_w.shape[1]
    taps, owners, slots = samp_index.shape[1:]
    extra = 4 * taps * owners * slots // ROW
    blocks = lax.axis_size("rng")
    place = call(
        functools.partial(place_kernel, "rng", blocks),
        shape((2 * EDGE, bins), BF16),
        [],
        VMEM,
        flops=2**32,
        nbytes=2**24,
    )()
    pack = call(
        functools.partial(pack_kernel, bins.bit_length() - 1, "chan"),
        shape((size // 2 + extra, ROW), BF16),
        [VMEM] * 5,
        VMEM,
    )(merge_w, samp_index, samp_weight, counts, place)
    near = swapped(pack, "sub", levels - 1)
    bands, outer, mix = call(
        functools.partial(filter_kernel, bins),
        (
            shape((channels, 2, bins, bins), BF16),
            shape((channels, 2, 2 * EDGE, bins), BF16),
            shape((16 * channels, bins), F32),
        ),
        [VMEM] * 2,
        (VMEM,) * 3,
    )(filt, chan_w)
    main, rim = call(
        image_kernel,
        (shape((size, bins), BF16), shape((2 * EDGE, size), BF16)),
        [VMEM] * 5,
        (VMEM,) * 2,
        flops=2**30,
        nbytes=2**21,
    )(raw, steer, bands, outer, mix)
    polar, own_rim = main, neighbour_rims(rim)
    if levels == 2 and blocks == 2:
        groups = lax.axis_size("sub") * blocks
        other_rim = lax.ppermute(rim, ("sub", "rng"), [(i, i ^ 3) for i in range(groups)])
    else:
        polar = call(whole_kernel, shape((size, bins), BF16), [VMEM] * 3, VMEM)(
            main, own_rim, place
        )
        own_rim = other_rim = jnp.zeros((2 * EDGE, size), BF16)
    far = swapped(lax.optimization_barrier((polar, near))[1], "chan", 0)
    for level in range(levels - 2):
        other = swapped(polar, "sub", level)
        polar = call(
            merge_kernel,
            shape((size, bins), BF16),
            [
                pl.BlockSpec((1, 1, 2, size, size), lambda i, level=level: (0, level, 0, 0, 0)),
                whole(polar),
                whole(other),
            ],
            pl.BlockSpec((size, bins), lambda i: (0, 0)),
            grid=(1,),
        )(merge_w, polar, other)
    other = swapped(polar, "sub", levels - 2)
    chunks = owners * slots // ROW
    tall = PIX_OWN // LANES
    count = owners * slots
    sets = 2 * taps
    weights = merge_w[:, levels - 2 :]
    mixed = call(mixed_kernel, shape((size, bins), F32), [VMEM] * 5, VMEM, flops=2**31, nbytes=2**20)(
        weights, polar, own_rim, other_rim, place
    )
    low, high, *ready = call(
        functools.partial(ready_kernel, taps),
        (
            shape((LANES, count), BF16),
            shape((tall, count), F32),
            shape((sets, bins, ROW), BF16),
            shape((sets, size // 2, ROW), F32),
        ),
        [VMEM] * 4,
        (VMEM,) * 4,
        flops=2**27,
        nbytes=2**19,
    )(pack, near, pixel_id, mixed)
    if chunks > 1:
        ready = []
    outgoing = call(
        functools.partial(sample_kernel, taps, slots, "chan"),
        shape((2 * owners, 4 * slots), F32),
        [VMEM] * (6 + len(ready)),
        VMEM,
        flops=2**28,
        nbytes=2**20,
    )(weights, mixed, other, pack, near, far, *ready)
    values = lax.all_to_all(
        outgoing, ("chan", "sub", "rng"), split_axis=0, concat_axis=0, tiled=True
    )
    return call(
        functools.partial(scatter_kernel, slots), shape((2, PIX_OWN), F32), [VMEM] * 3, VMEM
    )(values, low, high)


def solution(mesh):
    placed = (
        P("chan", None, ("groups", "sub"), "rng"),
        P("chan", None, None),
        P("sub", None, None),
        P("chan", None),
        P("sub", None, None, None, None),
        P(("sub", "rng"), None, None, None),
        P(("sub", "rng"), None, None, None),
        P(("sub", "rng"), None),
        P(("sub", "rng"), None, None),
    )
    return jax.shard_map(
        local,
        mesh=mesh,
        in_specs=placed,
        out_specs=P(None, ("groups", "sub", "rng")),
        check_vma=False,
    )
```

time: 26.8 us -> 26.2 us (0.978)
  blocking collectives: 10.3 us -> 9.31 us
  starting transfers between devices: 7.31 us -> 7.66 us
  waiting for transfers between devices: 3.39 us -> 3.72 us
  local copies, waits for them, and re-layouts: 1.31 us -> 1.04 us
    ppermute x1 -> x2, waiting for transfers between devices: 0.01 us -> 2.66 us  [the longest x1 1.61 us: neighbour_rims(): return lax.ppermute(rim, 'rng', [(0, 1), (1, 0)])]
    ppermute x3, waiting for transfers between devices: 3.39 us -> 1.07 us  [swapped(): lax.ppermute(value, axis, [(i, i ^ 1 << bit) for i in range(lax.axis_size...]
    all_to_all x1, blocking collectives: 10.3 us -> 9.31 us  [local(): lax.all_to_all(outgoing, ('chan', 'sub', 'rng'), split_axis=0, concat_axi...]
    unnamed x20 -> x18, local copies, waits for them, and re-layouts: 1.31 us -> 1.04 us
    ppermute x1 -> x2, starting transfers between devices: 3.01 us -> 3.1 us  [the longest x1 2.57 us: local(): lax.ppermute(rim, ('sub', 'rng'), [(i, i ^ 3) for i in range(groups)])]
    pallas_call x5 -> x6, Pallas kernels: 3.04 us -> 3.04 us  [the longest x1 1.11 us: local(): call(image_kernel, (shape((size, bins), BF16), shape((2 * EDGE, size), BF...]
  transfers between devices with their start and end apart: 4 -> 5, of which waited for: 3 -> 3; matrix products, arithmetic and copies ran while one was open for 0% -> 0% of each run, Pallas kernels for 8% -> 8%
where the time goes in v4:
time: 26.2 us; the launch traced here: 26 us
  blocking collectives  9.31 us (36%)
  starting transfers between devices  7.66 us (29%)
  Pallas kernels  4.17 us (16%)
  waiting for transfers between devices  3.72 us (14%)
  local copies, waits for them, and re-layouts  1.04 us (4%)
    all_to_all x1, blocking collectives, local(): lax.all_to_all(outgoing, ('chan', 'sub', 'rng'), split_axis=0, concat_axi...  9.31 us
    ppermute x3, starting transfers between devices, swapped(): lax.ppermute(value, axis, [(i, i ^ 1 << bit) for i in range(lax.axis_size...  4.55 us
    ppermute x1, starting transfers between devices, local(): lax.ppermute(rim, ('sub', 'rng'), [(i, i ^ 3) for i in range(groups)])  2.57 us
    ppermute x1, waiting for transfers between devices, neighbour_rims(): return lax.ppermute(rim, 'rng', [(0, 1), (1, 0)])  1.61 us
    pallas_call x1, Pallas kernels, local(): call(image_kernel, (shape((size, bins), BF16), shape((2 * EDGE, size), BF...  1.11 us
    ppermute x3, waiting for transfers between devices, swapped(): lax.ppermute(value, axis, [(i, i ^ 1 << bit) for i in range(lax.axis_size...  1.07 us
    ppermute x1, waiting for transfers between devices, local(): lax.ppermute(rim, ('sub', 'rng'), [(i, i ^ 3) for i in range(groups)])  1.05 us
    unnamed x18, local copies, waits for them, and re-layouts  1.04 us
  transfers between devices with their start and end apart: 5, of which 3 were waited for; matrix products, arithmetic and copies ran while one was open for 0% of the time, Pallas kernels for 8%

profile of v4, /device:TPU:0, one launch (start us, length us, event | category | flops | bytes accessed | tf_op | source)
XLA Modules:
  0.0 26.0 jit_solution(16384391095549574811)
XLA Ops:
  0.0 0.0 copy-start
  0.0 0.0 copy-start.5
  0.0 0.0 copy-start.2
  0.0 0.0 copy-start.1
  0.0 0.0 copy-start.6
  0.0 1.0 %copy-done = bf16[1,2,2,256,256]{4,3,2,1,0:T(8,128)(2,1)S(1)} copy-done((bf16[1,2,2,256,256]{4,3,2,1,0:T(8,128)(2,1)S(1)}, bf16[1,2,2,256,256]{4,3,2,1,0:T(8,128)(2,1)}, u32[]{:S(2)}) %copy-start) | copy-done | bytes 524312
  1.0 0.0 copy-done.5
  1.0 0.0 copy-done.2
  1.0 0.0 copy-done.1
  1.1 0.0 copy-start.3
  1.1 0.0 copy-start.4
  1.1 0.0 copy-start.7
  1.1 0.2 shard_map.95.pack_ref
  1.2 4.1 %collective-permute-start.3 = (bf16[144,256]{1,0:T(8,128)(2,1)S(1)}, bf16[144,256]{1,0:T(8,128)(2,1)S(1)}, u32[]{:S(2)}, u32[]{:S(2)}) collective-permute-start(bf16[144,256]{1,0:T(8,128)(2,1)S(1)} %shard_map.95.pack_ref), channel_id=1, source_target_pairs={{0,8},{4,12},{8,0},{12,4},{1,9},{5,13},{9,1},{13,5},{2,10},{6,14},... | collective-permute-start | bytes 221192 | tf_op jit(solution)/shard_map/ppermute | solution.py:281
  5.3 0.0 copy-done.3
  5.3 0.0 copy-done.4
  5.3 0.2 shard_map.91
  5.6 0.0 copy-done.6
  5.6 0.0 copy-done.7
  5.6 1.1 %shard_map.92 = (bf16[256,256]{1,0:T(8,128)(2,1)S(1)}, bf16[16,256]{1,0:T(8,128)(2,1)S(1)}) custom-call(bf16[2,2,512,256]{3,2,1,0:T(8,128)(2,1)S(1)} %copy-done.6, bf16[1,256,1024]{2,1,0:T(8,128)(2,1)S(1)} %copy-done.7, bf16[2,2,256,256]{3,2,1,0:T(8,128)(2,1)S(1)} %get-tuple-element.15.band_ref, bf16[2,2,16,256]{3,2,1,0:T(8,128)(2,1)S(1)} %get-tuple-element.16.outer_ref, ...), custom_call_target="tpu_custom_call" | custom-call | flops 1073741824 | bytes 2097152 | tf_op jit(solution)/shard_map/pallas_call | solution.py:325
  6.7 2.6 %collective-permute-start.1 = (bf16[16,256]{1,0:T(8,128)(2,1)S(1)}, bf16[16,256]{1,0:T(8,128)(2,1)S(1)}, u32[]{:S(2)}, u32[]{:S(2)}) collective-permute-start(bf16[16,256]{1,0:T(8,128)(2,1)S(1)} %get-tuple-element.19), channel_id=1, source_target_pairs={{0,6},{2,4},{4,2},{6,0},{8,14},{10,12},{12,10},{14,8},{1,7},{3,5},... | collective-permute-start | bytes 24584 | tf_op jit(solution)/shard_map/ppermute | solution.py:336
  9.3 0.5 %collective-permute-start = (bf16[16,256]{1,0:T(8,128)(2,1)S(1)}, bf16[16,256]{1,0:T(8,128)(2,1)S(1)}, u32[]{:S(2)}, u32[]{:S(2)}) collective-permute-start(bf16[16,256]{1,0:T(8,128)(2,1)S(1)} %get-tuple-element.19), channel_id=1, source_target_pairs={{0,2},{2,0},{1,3},{3,1},{4,6},{6,4},{5,7},{7,5},{8,10},{10,8},{9,1... | collective-permute-start | bytes 24584 | tf_op jit(solution)/shard_map/ppermute | solution.py:287
  9.8 0.0 copy-start.8
  9.8 0.4 %collective-permute-start.2 = (bf16[256,256]{1,0:T(8,128)(2,1)S(1)}, bf16[256,256]{1,0:T(8,128)(2,1)S(1)}, u32[]{:S(2)}, u32[]{:S(2)}) collective-permute-start(bf16[256,256]{1,0:T(8,128)(2,1)S(1)} %get-tuple-element.18.own_ref), channel_id=1, source_target_pairs={{0,4},{4,0},{8,12},{12,8},{1,5},{5,1},{9,13},{13,9},{2,6},{6,2},{1... | collective-permute-start | bytes 393224 | tf_op jit(solution)/shard_map/ppermute | solution.py:281
  10.3 0.0 collective-permute-done.3.near_ref
  10.3 0.0 collective-permute-start.4
  10.3 1.1 %collective-permute-done.1.other_rim_ref = bf16[16,256]{1,0:T(8,128)(2,1)S(1)} collective-permute-done((bf16[16,256]{1,0:T(8,128)(2,1)S(1)}, bf16[16,256]{1,0:T(8,128)(2,1)S(1)}, u32[]{:S(2)}, u32[]{:S(2)}) %collective-permute-start.1) | collective-permute-done | bytes 8224 | tf_op jit(solution)/shard_map/ppermute | solution.py:336
  11.4 1.6 %collective-permute-done.own_rim_ref = bf16[16,256]{1,0:T(8,128)(2,1)S(1)} collective-permute-done((bf16[16,256]{1,0:T(8,128)(2,1)S(1)}, bf16[16,256]{1,0:T(8,128)(2,1)S(1)}, u32[]{:S(2)}, u32[]{:S(2)}) %collective-permute-start) | collective-permute-done | bytes 8224 | tf_op jit(solution)/shard_map/ppermute | solution.py:287
  13.0 0.4 %shard_map.94._.mixed_ref = f32[256,256]{1,0:T(8,128)S(1)} custom-call(bf16[1,2,2,256,256]{4,3,2,1,0:T(8,128)(2,1)S(1)} %copy-done, bf16[256,256]{1,0:T(8,128)(2,1)S(1)} %get-tuple-element.18.own_ref, bf16[16,256]{1,0:T(8,128)(2,1)S(1)} %collective-permute-done.own_rim_ref, bf16[16,256]{1,0:T(8,128)(2,1)S(1)} %collective-permute-done.1.other_rim_ref, ...), custom_call_target="tpu_custom_call" | custom-call | flops 2147483648 | bytes 1048576 | tf_op jit(solution)/shard_map/pallas_call | solution.py:362
  13.4 0.0 copy-done.8
  13.4 0.3 %shard_map.96 = (bf16[128,256]{1,0:T(8,128)(2,1)S(1)}, f32[32,256]{1,0:T(8,128)S(1)}, bf16[8,256,256]{2,1,0:T(8,128)(2,1)S(1)}, f32[8,128,256]{2,1,0:T(8,128)S(1)}) custom-call(bf16[144,256]{1,0:T(8,128)(2,1)S(1)} %shard_map.95.pack_ref, bf16[144,256]{1,0:T(8,128)(2,1)S(1)} %collective-permute-done.3.near_ref, s32[1,8,32]{2,1,0:T(8,128)S(1)} %copy-done.8, ...), custom_call_target="tpu_custom_call" | custom-call | flops 134217728 | bytes 524288 | tf_op jit(solution)/shard_map/pallas_call | solution.py:365
  13.7 1.1 %collective-permute-done.2.other_ref = bf16[256,256]{1,0:T(8,128)(2,1)S(1)} collective-permute-done((bf16[256,256]{1,0:T(8,128)(2,1)S(1)}, bf16[256,256]{1,0:T(8,128)(2,1)S(1)}, u32[]{:S(2)}, u32[]{:S(2)}) %collective-permute-start.2) | collective-permute-done | bytes 131104 | tf_op jit(solution)/shard_map/ppermute | solution.py:281
  14.8 0.0 collective-permute-done.4.far_ref
  14.8 1.0 %shard_map.97 = f32[16,128]{1,0:T(8,128)S(1)} custom-call(bf16[1,2,2,256,256]{4,3,2,1,0:T(8,128)(2,1)S(1)} %copy-done, f32[256,256]{1,0:T(8,128)S(1)} %shard_map.94._.mixed_ref, bf16[256,256]{1,0:T(8,128)(2,1)S(1)} %collective-permute-done.2.other_ref, bf16[144,256]{1,0:T(8,128)(2,1)S(1)} %shard_map.95.pack_ref, ...), custom_call_target="tpu_custom_call" | custom-call | flops 268435456 | bytes 1048576 | tf_op jit(solution)/shard_map/pallas_call | solution.py:380
  15.8 9.3 %all_to_all.11 = f32[16,1,128]{2,1,0:T(1,128)S(1)} all-to-all(f32[16,1,128]{2,1,0:T(1,128)S(1)} %bitcast.4), channel_id=1, replica_groups=mesh['groups'=2,'sub'=4,'rng'=2,'chan'=2] {'chan','sub','rng'}, dimensions={0} | all-to-all | bytes 16384 | tf_op jit(solution)/shard_map/all_to_all | solution.py:388
  25.1 0.9 %shard_map.98 = f32[2,4096]{1,0:T(2,128)} custom-call(f32[16,128]{1,0:T(8,128)S(1)} %bitcast.5, bf16[128,256]{1,0:T(8,128)(2,1)S(1)} %get-tuple-element.23.low_ref, f32[32,256]{1,0:T(8,128)S(1)} %get-tuple-element.24.high_ref), custom_call_target="tpu_custom_call" | custom-call | tf_op jit(solution)/shard_map/pallas_call | solution.py:391
  (1 shorter events, 0.0 us)
Async XLA Ops:
  0.0 1.0 %copy-start = (bf16[1,2,2,256,256]{4,3,2,1,0:T(8,128)(2,1)S(1)}, bf16[1,2,2,256,256]{4,3,2,1,0:T(8,128)(2,1)}, u32[]{:S(2)}) copy-start(bf16[1,2,2,256,256]{4,3,2,1,0:T(8,128)(2,1)} %weight_ref.5) | copy-start | bytes 1572868
  0.0 1.0 %copy-start.5 = (s32[1,8]{1,0:T(1,128)S(1)}, s32[1,8]{1,0:T(1,128)}, u32[]{:S(2)}) copy-start(s32[1,8]{1,0:T(1,128)} %counts_ref.1) | copy-start | bytes 100
  0.0 1.0 %copy-start.2 = (f32[1,4,8,32]{3,2,1,0:T(8,128)S(1)}, f32[1,4,8,32]{3,2,1,0:T(8,128)}, u32[]{:S(2)}) copy-start(f32[1,4,8,32]{3,2,1,0:T(8,128)} %weight_ref.4) | copy-start | bytes 12292
  0.0 1.0 %copy-start.1 = (s32[1,4,8,32]{3,2,1,0:T(8,128)S(1)}, s32[1,4,8,32]{3,2,1,0:T(8,128)}, u32[]{:S(2)}) copy-start(s32[1,4,8,32]{3,2,1,0:T(8,128)} %index_ref.1) | copy-start | bytes 12292
  0.0 5.6 %copy-start.6 = (bf16[2,2,512,256]{3,2,1,0:T(8,128)(2,1)S(1)}, bf16[2,2,512,256]{3,2,1,0:T(8,128)(2,1)}, u32[]{:S(2)}) copy-start(bf16[2,2,512,256]{3,2,1,0:T(8,128)(2,1)} %raw_ref.1) | copy-start | bytes 3145732
  1.1 4.3 %copy-start.3 = (f32[2,2,16]{2,1,0:T(2,128)S(1)}, f32[2,2,16]{2,1,0:T(2,128)}, u32[]{:S(2)}) copy-start(f32[2,2,16]{2,1,0:T(2,128)} %filt_ref.1) | copy-start | bytes 772
  1.1 4.3 %copy-start.4 = (f32[2,2]{1,0:T(2,128)S(1)}, f32[2,2]{1,0:T(2,128)}, u32[]{:S(2)}) copy-start(f32[2,2]{1,0:T(2,128)} %chan_ref.1) | copy-start | bytes 52
  1.1 4.5 %copy-start.7 = (bf16[1,256,1024]{2,1,0:T(8,128)(2,1)S(1)}, bf16[1,256,1024]{2,1,0:T(8,128)(2,1)}, u32[]{:S(2)}) copy-start(bf16[1,256,1024]{2,1,0:T(8,128)(2,1)} %steer_ref.1) | copy-start | bytes 1572868
  1.2 9.1 %collective-permute-start.3 = (bf16[144,256]{1,0:T(8,128)(2,1)S(1)}, bf16[144,256]{1,0:T(8,128)(2,1)S(1)}, u32[]{:S(2)}, u32[]{:S(2)}) collective-permute-start(bf16[144,256]{1,0:T(8,128)(2,1)S(1)} %shard_map.95.pack_ref), channel_id=1, source_target_pairs={{0,8},{4,12},{8,0},{12,4},{1,9},{5,13},{9,1},{13,5},{2,10},{6,14},... | collective-permute-start | bytes 221192 | tf_op jit(solution)/shard_map/ppermute | solution.py:281
  6.7 4.6 %collective-permute-start.1 = (bf16[16,256]{1,0:T(8,128)(2,1)S(1)}, bf16[16,256]{1,0:T(8,128)(2,1)S(1)}, u32[]{:S(2)}, u32[]{:S(2)}) collective-permute-start(bf16[16,256]{1,0:T(8,128)(2,1)S(1)} %get-tuple-element.19), channel_id=1, source_target_pairs={{0,6},{2,4},{4,2},{6,0},{8,14},{10,12},{12,10},{14,8},{1,7},{3,5},... | collective-permute-start | bytes 24584 | tf_op jit(solution)/shard_map/ppermute | solution.py:336
  9.3 3.7 %collective-permute-start = (bf16[16,256]{1,0:T(8,128)(2,1)S(1)}, bf16[16,256]{1,0:T(8,128)(2,1)S(1)}, u32[]{:S(2)}, u32[]{:S(2)}) collective-permute-start(bf16[16,256]{1,0:T(8,128)(2,1)S(1)} %get-tuple-element.19), channel_id=1, source_target_pairs={{0,2},{2,0},{1,3},{3,1},{4,6},{6,4},{5,7},{7,5},{8,10},{10,8},{9,1... | collective-permute-start | bytes 24584 | tf_op jit(solution)/shard_map/ppermute | solution.py:287
  9.8 3.6 %copy-start.8 = (s32[1,8,32]{2,1,0:T(8,128)S(1)}, s32[1,8,32]{2,1,0:T(8,128)}, u32[]{:S(2)}) copy-start(s32[1,8,32]{2,1,0:T(8,128)} %pixel_ref.1) | copy-start | bytes 3076
  9.8 5.0 %collective-permute-start.2 = (bf16[256,256]{1,0:T(8,128)(2,1)S(1)}, bf16[256,256]{1,0:T(8,128)(2,1)S(1)}, u32[]{:S(2)}, u32[]{:S(2)}) collective-permute-start(bf16[256,256]{1,0:T(8,128)(2,1)S(1)} %get-tuple-element.18.own_ref), channel_id=1, source_target_pairs={{0,4},{4,0},{8,12},{12,8},{1,5},{5,1},{9,13},{13,9},{2,6},{6,2},{1... | collective-permute-start | bytes 393224 | tf_op jit(solution)/shard_map/ppermute | solution.py:281
  10.3 4.5 %collective-permute-start.4 = (bf16[144,256]{1,0:T(8,128)(2,1)S(1)}, bf16[144,256]{1,0:T(8,128)(2,1)S(1)}, u32[]{:S(2)}, u32[]{:S(2)}) collective-permute-start(bf16[144,256]{1,0:T(8,128)(2,1)S(1)} %collective-permute-done.3.near_ref), channel_id=1, source_target_pairs={{0,1},{1,0},{2,3},{3,2},{4,5},{5,4},{6,7},{7,6},{8,9},{9,8},{10,11... | collective-permute-start | bytes 221192 | tf_op jit(solution)/shard_map/ppermute | solution.py:281

commit v5 on v4

--- a/solution.py
+++ b/solution.py
@@ -37,7 +37,7 @@
 
 
 def pack_kernel(
-    shift, chan_axis, merge_ref, index_ref, weight_ref, counts_ref, _, pack_ref
+    shift, chan_axis, merge_ref, index_ref, weight_ref, counts_ref, _first, _filt, _mix, pack_ref
 ):
     half = merge_ref.shape[3] // 2
     last = merge_ref.shape[1] - 1
@@ -165,13 +165,13 @@
     return pick_bin, jnp.where(beam_ids == beam, weight, 0.0)
 
 
-def mixed_kernel(weight_ref, own_ref, own_rim_ref, other_rim_ref, place_ref, mixed_ref):
+def mixed_kernel(weight_ref, own_ref, own_rim_ref, other_rim_ref, place_ref, _, mixed_ref):
     own = (own_ref[...].astype(F32) + spread_rim(own_rim_ref, place_ref)).astype(BF16)
     other = spread_rim(other_rim_ref, place_ref).astype(BF16)
     mixed_ref[...] = dot(weight_ref[0, 0, 0], own) + dot(weight_ref[0, 0, 1], other)
 
 
-def ready_kernel(taps, pack_ref, near_ref, pixel_ref, _, low_ref, high_ref, bin_ref, beam_ref):
+def ready_kernel(taps, pack_ref, near_ref, pixel_ref, low_ref, high_ref, bin_ref, beam_ref):
     half, bins = beam_ref.shape[1], bin_ref.shape[1]
     owners, slots = pixel_ref.shape[1:]
     for block, ref in enumerate((pack_ref, near_ref)):
@@ -308,9 +308,9 @@
     pack = call(
         functools.partial(pack_kernel, bins.bit_length() - 1, "chan"),
         shape((size // 2 + extra, ROW), BF16),
-        [VMEM] * 5,
+        [VMEM] * 7,
         VMEM,
-    )(merge_w, samp_index, samp_weight, counts, place)
+    )(merge_w, samp_index, samp_weight, counts, place, filt, chan_w)
     near = swapped(pack, "sub", levels - 1)
     bands, outer, mix = call(
         functools.partial(filter_kernel, bins),
@@ -359,9 +359,6 @@
     count = owners * slots
     sets = 2 * taps
     weights = merge_w[:, levels - 2 :]
-    mixed = call(mixed_kernel, shape((size, bins), F32), [VMEM] * 5, VMEM, flops=2**31, nbytes=2**20)(
-        weights, polar, own_rim, other_rim, place
-    )
     low, high, *ready = call(
         functools.partial(ready_kernel, taps),
         (
@@ -370,11 +367,14 @@
             shape((sets, bins, ROW), BF16),
             shape((sets, size // 2, ROW), F32),
         ),
-        [VMEM] * 4,
+        [VMEM] * 3,
         (VMEM,) * 4,
         flops=2**27,
         nbytes=2**19,
-    )(pack, near, pixel_id, mixed)
+    )(pack, near, pixel_id)
+    mixed = call(mixed_kernel, shape((size, bins), F32), [VMEM] * 6, VMEM, flops=2**30, nbytes=2**18)(
+        weights, polar, own_rim, other_rim, place, high
+    )
     if chunks > 1:
         ready = []
     outgoing = call(

time: 26.2 us -> 26.1 us (level)
    ppermute x1, starting transfers between devices: 2.57 us -> 0.42 us  [local(): lax.ppermute(rim, ('sub', 'rng'), [(i, i ^ 3) for i in range(groups)])]
    ppermute x1, waiting for transfers between devices: 1.05 us -> 2.39 us  [local(): lax.ppermute(rim, ('sub', 'rng'), [(i, i ^ 3) for i in range(groups)])]
    ppermute x3, starting transfers between devices: 4.55 us -> 5.75 us  [swapped(): lax.ppermute(value, axis, [(i, i ^ 1 << bit) for i in range(lax.axis_size...]
    ppermute x3, waiting for transfers between devices: 1.07 us -> 0.01 us  [swapped(): lax.ppermute(value, axis, [(i, i ^ 1 << bit) for i in range(lax.axis_size...]
    ppermute x1, starting transfers between devices: 0.53 us -> 1.49 us  [neighbour_rims(): return lax.ppermute(rim, 'rng', [(0, 1), (1, 0)])]
  transfers between devices with their start and end apart: 5 -> 5, of which waited for: 3 -> 2; matrix products, arithmetic and copies ran while one was open for 0% -> 0% of each run, Pallas kernels for 8% -> 8%
where the time goes in v5:
time: 26.1 us; the launch traced here: 25.9 us
  blocking collectives  9.13 us (35%)
  starting transfers between devices  7.66 us (29%)
  Pallas kernels  4.18 us (16%)
  waiting for transfers between devices  3.79 us (15%)
  local copies, waits for them, and re-layouts  1.02 us (4%)
    all_to_all x1, blocking collectives, local(): lax.all_to_all(outgoing, ('chan', 'sub', 'rng'), split_axis=0, concat_axi...  9.13 us
    ppermute x3, starting transfers between devices, swapped(): lax.ppermute(value, axis, [(i, i ^ 1 << bit) for i in range(lax.axis_size...  5.75 us
    ppermute x1, waiting for transfers between devices, local(): lax.ppermute(rim, ('sub', 'rng'), [(i, i ^ 3) for i in range(groups)])  2.39 us
    ppermute x1, starting transfers between devices, neighbour_rims(): return lax.ppermute(rim, 'rng', [(0, 1), (1, 0)])  1.49 us
    ppermute x1, waiting for transfers between devices, neighbour_rims(): return lax.ppermute(rim, 'rng', [(0, 1), (1, 0)])  1.4 us
    pallas_call x1, Pallas kernels, local(): call(image_kernel, (shape((size, bins), BF16), shape((2 * EDGE, size), BF...  1.11 us
    unnamed x18, local copies, waits for them, and re-layouts  1.02 us
    pallas_call x1, Pallas kernels, local(): call(functools.partial(sample_kernel, taps, slots, 'chan'), shape((2 * ow...  0.98 us
  transfers between devices with their start and end apart: 5, of which 2 were waited for; matrix products, arithmetic and copies ran while one was open for 0% of the time, Pallas kernels for 8%

profile of v5, /device:TPU:0, one launch (start us, length us, event | category | flops | bytes accessed | tf_op | source)
XLA Modules:
  0.0 25.9 jit_solution(4820938812179256400)
XLA Ops:
  0.0 0.0 copy-start
  0.0 0.0 copy-start.3
  0.0 0.0 copy-start.4
  0.0 0.0 copy-start.1
  0.0 0.0 copy-start.2
  0.0 0.0 copy-start.5
  0.0 0.0 copy-start.6
  0.1 1.0 %copy-done = bf16[1,2,2,256,256]{4,3,2,1,0:T(8,128)(2,1)S(1)} copy-done((bf16[1,2,2,256,256]{4,3,2,1,0:T(8,128)(2,1)S(1)}, bf16[1,2,2,256,256]{4,3,2,1,0:T(8,128)(2,1)}, u32[]{:S(2)}) %copy-start) | copy-done | bytes 524312
  1.0 0.0 copy-done.3
  1.0 0.0 copy-done.4
  1.0 0.0 copy-done.1
  1.1 0.0 copy-done.2
  1.1 0.0 copy-done.5
  1.1 0.0 copy-start.7
  1.1 0.2 shard_map.94.pack_ref
  1.2 4.1 %collective-permute-start.2 = (bf16[144,256]{1,0:T(8,128)(2,1)S(1)}, bf16[144,256]{1,0:T(8,128)(2,1)S(1)}, u32[]{:S(2)}, u32[]{:S(2)}) collective-permute-start(bf16[144,256]{1,0:T(8,128)(2,1)S(1)} %shard_map.94.pack_ref), channel_id=1, source_target_pairs={{0,8},{4,12},{8,0},{12,4},{1,9},{5,13},{9,1},{13,5},{2,10},{6,14},... | collective-permute-start | bytes 221192 | tf_op jit(solution)/shard_map/ppermute | solution.py:281
  5.3 0.2 shard_map.91
  5.6 0.0 copy-done.6
  5.6 0.0 copy-done.7
  5.6 0.0 copy-start.8
  5.6 1.1 %shard_map.92 = (bf16[256,256]{1,0:T(8,128)(2,1)S(1)}, bf16[16,256]{1,0:T(8,128)(2,1)S(1)}) custom-call(bf16[2,2,512,256]{3,2,1,0:T(8,128)(2,1)S(1)} %copy-done.6, bf16[1,256,1024]{2,1,0:T(8,128)(2,1)S(1)} %copy-done.7, bf16[2,2,256,256]{3,2,1,0:T(8,128)(2,1)S(1)} %get-tuple-element.15.band_ref, bf16[2,2,16,256]{3,2,1,0:T(8,128)(2,1)S(1)} %get-tuple-element.16.outer_ref, ...), custom_call_target="tpu_custom_call" | custom-call | flops 1073741824 | bytes 2097152 | tf_op jit(solution)/shard_map/pallas_call | solution.py:325
  6.7 1.6 %collective-permute-start.3 = (bf16[256,256]{1,0:T(8,128)(2,1)S(1)}, bf16[256,256]{1,0:T(8,128)(2,1)S(1)}, u32[]{:S(2)}, u32[]{:S(2)}) collective-permute-start(bf16[256,256]{1,0:T(8,128)(2,1)S(1)} %get-tuple-element.18.own_ref), channel_id=1, source_target_pairs={{0,4},{4,0},{8,12},{12,8},{1,5},{5,1},{9,13},{13,9},{2,6},{6,2},{1... | collective-permute-start | bytes 393224 | tf_op jit(solution)/shard_map/ppermute | solution.py:281
  8.4 1.5 %collective-permute-start = (bf16[16,256]{1,0:T(8,128)(2,1)S(1)}, bf16[16,256]{1,0:T(8,128)(2,1)S(1)}, u32[]{:S(2)}, u32[]{:S(2)}) collective-permute-start(bf16[16,256]{1,0:T(8,128)(2,1)S(1)} %get-tuple-element.19), channel_id=1, source_target_pairs={{0,2},{2,0},{1,3},{3,1},{4,6},{6,4},{5,7},{7,5},{8,10},{10,8},{9,1... | collective-permute-start | bytes 24584 | tf_op jit(solution)/shard_map/ppermute | solution.py:287
  9.9 0.4 %collective-permute-start.1 = (bf16[16,256]{1,0:T(8,128)(2,1)S(1)}, bf16[16,256]{1,0:T(8,128)(2,1)S(1)}, u32[]{:S(2)}, u32[]{:S(2)}) collective-permute-start(bf16[16,256]{1,0:T(8,128)(2,1)S(1)} %get-tuple-element.19), channel_id=1, source_target_pairs={{0,6},{2,4},{4,2},{6,0},{8,14},{10,12},{12,10},{14,8},{1,7},{3,5},... | collective-permute-start | bytes 24584 | tf_op jit(solution)/shard_map/ppermute | solution.py:336
  10.3 0.0 collective-permute-done.2.near_ref
  10.3 0.0 collective-permute-start.4
  10.3 0.0 copy-done.8
  10.3 0.3 %shard_map.95 = (bf16[128,256]{1,0:T(8,128)(2,1)S(1)}, f32[32,256]{1,0:T(8,128)S(1)}, bf16[8,256,256]{2,1,0:T(8,128)(2,1)S(1)}, f32[8,128,256]{2,1,0:T(8,128)S(1)}) custom-call(bf16[144,256]{1,0:T(8,128)(2,1)S(1)} %shard_map.94.pack_ref, bf16[144,256]{1,0:T(8,128)(2,1)S(1)} %collective-permute-done.2.near_ref, s32[1,8,32]{2,1,0:T(8,128)S(1)} %copy-done.8), custom_call_target="tpu_custom_call" | custom-call | flops 134217728 | bytes 524288 | tf_op jit(solution)/shard_map/pallas_call | solution.py:362
  10.6 1.4 %collective-permute-done.own_rim_ref = bf16[16,256]{1,0:T(8,128)(2,1)S(1)} collective-permute-done((bf16[16,256]{1,0:T(8,128)(2,1)S(1)}, bf16[16,256]{1,0:T(8,128)(2,1)S(1)}, u32[]{:S(2)}, u32[]{:S(2)}) %collective-permute-start) | collective-permute-done | bytes 8224 | tf_op jit(solution)/shard_map/ppermute | solution.py:287
  12.0 2.4 %collective-permute-done.1.other_rim_ref = bf16[16,256]{1,0:T(8,128)(2,1)S(1)} collective-permute-done((bf16[16,256]{1,0:T(8,128)(2,1)S(1)}, bf16[16,256]{1,0:T(8,128)(2,1)S(1)}, u32[]{:S(2)}, u32[]{:S(2)}) %collective-permute-start.1) | collective-permute-done | bytes 8224 | tf_op jit(solution)/shard_map/ppermute | solution.py:336
  14.4 0.4 %shard_map.96.mixed_ref = f32[256,256]{1,0:T(8,128)S(1)} custom-call(bf16[1,2,2,256,256]{4,3,2,1,0:T(8,128)(2,1)S(1)} %copy-done, bf16[256,256]{1,0:T(8,128)(2,1)S(1)} %get-tuple-element.18.own_ref, bf16[16,256]{1,0:T(8,128)(2,1)S(1)} %collective-permute-done.own_rim_ref, bf16[16,256]{1,0:T(8,128)(2,1)S(1)} %collective-permute-done.1.other_rim_ref, ...), custom_call_target="tpu_custom_call" | custom-call | flops 1073741824 | bytes 262144 | tf_op jit(solution)/shard_map/pallas_call | solution.py:375
  14.9 0.0 collective-permute-done.3.other_ref
  14.9 0.0 collective-permute-done.4.far_ref
  14.9 1.0 %shard_map.97 = f32[16,128]{1,0:T(8,128)S(1)} custom-call(bf16[1,2,2,256,256]{4,3,2,1,0:T(8,128)(2,1)S(1)} %copy-done, f32[256,256]{1,0:T(8,128)S(1)} %shard_map.96.mixed_ref, bf16[256,256]{1,0:T(8,128)(2,1)S(1)} %collective-permute-done.3.other_ref, bf16[144,256]{1,0:T(8,128)(2,1)S(1)} %shard_map.94.pack_ref, ...), custom_call_target="tpu_custom_call" | custom-call | flops 268435456 | bytes 1048576 | tf_op jit(solution)/shard_map/pallas_call | solution.py:380
  15.9 9.1 %all_to_all.11 = f32[16,1,128]{2,1,0:T(1,128)S(1)} all-to-all(f32[16,1,128]{2,1,0:T(1,128)S(1)} %bitcast.4), channel_id=1, replica_groups=mesh['groups'=2,'sub'=4,'rng'=2,'chan'=2] {'chan','sub','rng'}, dimensions={0} | all-to-all | bytes 16384 | tf_op jit(solution)/shard_map/all_to_all | solution.py:388
  25.0 0.9 %shard_map.98 = f32[2,4096]{1,0:T(2,128)} custom-call(f32[16,128]{1,0:T(8,128)S(1)} %bitcast.5, bf16[128,256]{1,0:T(8,128)(2,1)S(1)} %get-tuple-element.24.low_ref, f32[32,256]{1,0:T(8,128)S(1)} %get-tuple-element.20._.high_ref), custom_call_target="tpu_custom_call" | custom-call | tf_op jit(solution)/shard_map/pallas_call | solution.py:391
  (1 shorter events, 0.0 us)
Async XLA Ops:
  0.0 1.0 %copy-start = (bf16[1,2,2,256,256]{4,3,2,1,0:T(8,128)(2,1)S(1)}, bf16[1,2,2,256,256]{4,3,2,1,0:T(8,128)(2,1)}, u32[]{:S(2)}) copy-start(bf16[1,2,2,256,256]{4,3,2,1,0:T(8,128)(2,1)} %weight_ref.5) | copy-start | bytes 1572868
  0.0 1.0 %copy-start.3 = (f32[2,2,16]{2,1,0:T(2,128)S(1)}, f32[2,2,16]{2,1,0:T(2,128)}, u32[]{:S(2)}) copy-start(f32[2,2,16]{2,1,0:T(2,128)} %_filt.1) | copy-start | bytes 772
  0.0 1.0 %copy-start.4 = (f32[2,2]{1,0:T(2,128)S(1)}, f32[2,2]{1,0:T(2,128)}, u32[]{:S(2)}) copy-start(f32[2,2]{1,0:T(2,128)} %_mix.1) | copy-start | bytes 52
  0.0 1.0 %copy-start.1 = (s32[1,4,8,32]{3,2,1,0:T(8,128)S(1)}, s32[1,4,8,32]{3,2,1,0:T(8,128)}, u32[]{:S(2)}) copy-start(s32[1,4,8,32]{3,2,1,0:T(8,128)} %index_ref.1) | copy-start | bytes 12292
  0.0 1.0 %copy-start.2 = (f32[1,4,8,32]{3,2,1,0:T(8,128)S(1)}, f32[1,4,8,32]{3,2,1,0:T(8,128)}, u32[]{:S(2)}) copy-start(f32[1,4,8,32]{3,2,1,0:T(8,128)} %weight_ref.3) | copy-start | bytes 12292
  0.0 1.0 %copy-start.5 = (s32[1,8]{1,0:T(1,128)S(1)}, s32[1,8]{1,0:T(1,128)}, u32[]{:S(2)}) copy-start(s32[1,8]{1,0:T(1,128)} %counts_ref.1) | copy-start | bytes 100
  0.0 5.6 %copy-start.6 = (bf16[2,2,512,256]{3,2,1,0:T(8,128)(2,1)S(1)}, bf16[2,2,512,256]{3,2,1,0:T(8,128)(2,1)}, u32[]{:S(2)}) copy-start(bf16[2,2,512,256]{3,2,1,0:T(8,128)(2,1)} %raw_ref.1) | copy-start | bytes 3145732
  1.1 4.5 %copy-start.7 = (bf16[1,256,1024]{2,1,0:T(8,128)(2,1)S(1)}, bf16[1,256,1024]{2,1,0:T(8,128)(2,1)}, u32[]{:S(2)}) copy-start(bf16[1,256,1024]{2,1,0:T(8,128)(2,1)} %steer_ref.1) | copy-start | bytes 1572868
  1.2 9.1 %collective-permute-start.2 = (bf16[144,256]{1,0:T(8,128)(2,1)S(1)}, bf16[144,256]{1,0:T(8,128)(2,1)S(1)}, u32[]{:S(2)}, u32[]{:S(2)}) collective-permute-start(bf16[144,256]{1,0:T(8,128)(2,1)S(1)} %shard_map.94.pack_ref), channel_id=1, source_target_pairs={{0,8},{4,12},{8,0},{12,4},{1,9},{5,13},{9,1},{13,5},{2,10},{6,14},... | collective-permute-start | bytes 221192 | tf_op jit(solution)/shard_map/ppermute | solution.py:281
  5.6 4.7 %copy-start.8 = (s32[1,8,32]{2,1,0:T(8,128)S(1)}, s32[1,8,32]{2,1,0:T(8,128)}, u32[]{:S(2)}) copy-start(s32[1,8,32]{2,1,0:T(8,128)} %pixel_ref.1) | copy-start | bytes 3076
  6.7 8.1 %collective-permute-start.3 = (bf16[256,256]{1,0:T(8,128)(2,1)S(1)}, bf16[256,256]{1,0:T(8,128)(2,1)S(1)}, u32[]{:S(2)}, u32[]{:S(2)}) collective-permute-start(bf16[256,256]{1,0:T(8,128)(2,1)S(1)} %get-tuple-element.18.own_ref), channel_id=1, source_target_pairs={{0,4},{4,0},{8,12},{12,8},{1,5},{5,1},{9,13},{13,9},{2,6},{6,2},{1... | collective-permute-start | bytes 393224 | tf_op jit(solution)/shard_map/ppermute | solution.py:281
  8.4 3.7 %collective-permute-start = (bf16[16,256]{1,0:T(8,128)(2,1)S(1)}, bf16[16,256]{1,0:T(8,128)(2,1)S(1)}, u32[]{:S(2)}, u32[]{:S(2)}) collective-permute-start(bf16[16,256]{1,0:T(8,128)(2,1)S(1)} %get-tuple-element.19), channel_id=1, source_target_pairs={{0,2},{2,0},{1,3},{3,1},{4,6},{6,4},{5,7},{7,5},{8,10},{10,8},{9,1... | collective-permute-start | bytes 24584 | tf_op jit(solution)/shard_map/ppermute | solution.py:287
  9.9 4.5 %collective-permute-start.1 = (bf16[16,256]{1,0:T(8,128)(2,1)S(1)}, bf16[16,256]{1,0:T(8,128)(2,1)S(1)}, u32[]{:S(2)}, u32[]{:S(2)}) collective-permute-start(bf16[16,256]{1,0:T(8,128)(2,1)S(1)} %get-tuple-element.19), channel_id=1, source_target_pairs={{0,6},{2,4},{4,2},{6,0},{8,14},{10,12},{12,10},{14,8},{1,7},{3,5},... | collective-permute-start | bytes 24584 | tf_op jit(solution)/shard_map/ppermute | solution.py:336
  10.3 4.6 %collective-permute-start.4 = (bf16[144,256]{1,0:T(8,128)(2,1)S(1)}, bf16[144,256]{1,0:T(8,128)(2,1)S(1)}, u32[]{:S(2)}, u32[]{:S(2)}) collective-permute-start(bf16[144,256]{1,0:T(8,128)(2,1)S(1)} %collective-permute-done.2.near_ref), channel_id=1, source_target_pairs={{0,1},{1,0},{2,3},{3,2},{4,5},{5,4},{6,7},{7,6},{8,9},{9,8},{10,11... | collective-permute-start | bytes 221192 | tf_op jit(solution)/shard_map/ppermute | solution.py:281

commit v6 on v5

--- a/solution.py
+++ b/solution.py
@@ -165,13 +165,17 @@
     return pick_bin, jnp.where(beam_ids == beam, weight, 0.0)
 
 
-def mixed_kernel(weight_ref, own_ref, own_rim_ref, other_rim_ref, place_ref, _, mixed_ref):
-    own = (own_ref[...].astype(F32) + spread_rim(own_rim_ref, place_ref)).astype(BF16)
-    other = spread_rim(other_rim_ref, place_ref).astype(BF16)
-    mixed_ref[...] = dot(weight_ref[0, 0, 0], own) + dot(weight_ref[0, 0, 1], other)
-
-
-def ready_kernel(taps, pack_ref, near_ref, pixel_ref, low_ref, high_ref, bin_ref, beam_ref):
+def mixed_kernel(weight_ref, begun_ref, own_rim_ref, other_rim_ref, place_ref, mixed_ref):
+    rims = dot_nt(weight_ref[0, 0, 0], own_rim_ref[...])
+    rims = rims + dot_nt(weight_ref[0, 0, 1], other_rim_ref[...])
+    mixed_ref[...] = begun_ref[...] + dot(rims.astype(BF16), place_ref[...])
+
+
+def ready_kernel(
+    taps, weight_ref, own_ref, pack_ref, near_ref, pixel_ref,
+    begun_ref, low_ref, high_ref, bin_ref, beam_ref,
+):
+    begun_ref[...] = dot(weight_ref[0, 0, 0], own_ref[...])
     half, bins = beam_ref.shape[1], bin_ref.shape[1]
     owners, slots = pixel_ref.shape[1:]
     for block, ref in enumerate((pack_ref, near_ref)):
@@ -359,21 +363,22 @@
     count = owners * slots
     sets = 2 * taps
     weights = merge_w[:, levels - 2 :]
-    low, high, *ready = call(
+    begun, low, high, *ready = call(
         functools.partial(ready_kernel, taps),
         (
+            shape((size, bins), F32),
             shape((LANES, count), BF16),
             shape((tall, count), F32),
             shape((sets, bins, ROW), BF16),
             shape((sets, size // 2, ROW), F32),
         ),
-        [VMEM] * 3,
-        (VMEM,) * 4,
+        [VMEM] * 5,
+        (VMEM,) * 5,
         flops=2**27,
         nbytes=2**19,
-    )(pack, near, pixel_id)
-    mixed = call(mixed_kernel, shape((size, bins), F32), [VMEM] * 6, VMEM, flops=2**30, nbytes=2**18)(
-        weights, polar, own_rim, other_rim, place, high
+    )(weights, polar, pack, near, pixel_id)
+    mixed = call(mixed_kernel, shape((size, bins), F32), [VMEM] * 5, VMEM, flops=2**30, nbytes=2**18)(
+        weights, begun, own_rim, other_rim, place
     )
     if chunks > 1:
         ready = []

time: 26.1 us -> 26 us (level)
  no operation moved by 1% of the time
where the time goes in v6:
time: 26 us; the launch traced here: 25.8 us
  blocking collectives  9.13 us (35%)
  starting transfers between devices  7.66 us (29%)
  Pallas kernels  4.16 us (16%)
  waiting for transfers between devices  3.71 us (14%)
  local copies, waits for them, and re-layouts  1.04 us (4%)
    all_to_all x1, blocking collectives, local(): lax.all_to_all(outgoing, ('chan', 'sub', 'rng'), split_axis=0, concat_axi...  9.13 us
    ppermute x3, starting transfers between devices, swapped(): lax.ppermute(value, axis, [(i, i ^ 1 << bit) for i in range(lax.axis_size...  5.75 us
    ppermute x1, waiting for transfers between devices, local(): lax.ppermute(rim, ('sub', 'rng'), [(i, i ^ 3) for i in range(groups)])  2.39 us
    ppermute x1, starting transfers between devices, neighbour_rims(): return lax.ppermute(rim, 'rng', [(0, 1), (1, 0)])  1.49 us
    ppermute x1, waiting for transfers between devices, neighbour_rims(): return lax.ppermute(rim, 'rng', [(0, 1), (1, 0)])  1.31 us
    pallas_call x1, Pallas kernels, local(): call(image_kernel, (shape((size, bins), BF16), shape((2 * EDGE, size), BF...  1.11 us
    unnamed x18, local copies, waits for them, and re-layouts  1.04 us
    pallas_call x1, Pallas kernels, local(): call(functools.partial(sample_kernel, taps, slots, 'chan'), shape((2 * ow...  0.98 us
  transfers between devices with their start and end apart: 5, of which 2 were waited for; matrix products, arithmetic and copies ran while one was open for 0% of the time, Pallas kernels for 8%

profile of v6, /device:TPU:0, one launch (start us, length us, event | category | flops | bytes accessed | tf_op | source)
XLA Modules:
  0.0 25.8 jit_solution(124244781956328224)
XLA Ops:
  0.0 0.0 copy-start.3
  0.0 0.0 copy-start.5
  0.0 0.0 copy-start
  0.0 0.0 copy-start.1
  0.0 0.0 copy-start.2
  0.0 0.0 copy-start.6
  0.0 0.0 copy-start.7
  0.1 0.6 %copy-done.3 = f32[2,2,16]{2,1,0:T(2,128)S(1)} copy-done((f32[2,2,16]{2,1,0:T(2,128)S(1)}, f32[2,2,16]{2,1,0:T(2,128)}, u32[]{:S(2)}) %copy-start.3) | copy-done | bytes 280
  0.7 0.0 copy-done.5
  0.7 0.4 %copy-done = bf16[1,2,2,256,256]{4,3,2,1,0:T(8,128)(2,1)S(1)} copy-done((bf16[1,2,2,256,256]{4,3,2,1,0:T(8,128)(2,1)S(1)}, bf16[1,2,2,256,256]{4,3,2,1,0:T(8,128)(2,1)}, u32[]{:S(2)}) %copy-start) | copy-done | bytes 524312
  1.1 0.0 copy-done.1
  1.1 0.0 copy-done.2
  1.1 0.0 copy-done.6
  1.1 0.0 copy-start.8
  1.1 0.2 shard_map.94.pack_ref
  1.2 4.1 %collective-permute-start = (bf16[144,256]{1,0:T(8,128)(2,1)S(1)}, bf16[144,256]{1,0:T(8,128)(2,1)S(1)}, u32[]{:S(2)}, u32[]{:S(2)}) collective-permute-start(bf16[144,256]{1,0:T(8,128)(2,1)S(1)} %shard_map.94.pack_ref), channel_id=1, source_target_pairs={{0,8},{4,12},{8,0},{12,4},{1,9},{5,13},{9,1},{13,5},{2,10},{6,14},... | collective-permute-start | bytes 221192 | tf_op jit(solution)/shard_map/ppermute | solution.py:285
  5.3 0.2 shard_map.91
  5.6 0.0 copy-done.7
  5.6 0.0 copy-done.8
  5.6 0.0 copy-start.4
  5.6 1.1 %shard_map.92 = (bf16[256,256]{1,0:T(8,128)(2,1)S(1)}, bf16[16,256]{1,0:T(8,128)(2,1)S(1)}) custom-call(bf16[2,2,512,256]{3,2,1,0:T(8,128)(2,1)S(1)} %copy-done.7, bf16[1,256,1024]{2,1,0:T(8,128)(2,1)S(1)} %copy-done.8, bf16[2,2,256,256]{3,2,1,0:T(8,128)(2,1)S(1)} %get-tuple-element.16.band_ref, bf16[2,2,16,256]{3,2,1,0:T(8,128)(2,1)S(1)} %get-tuple-element.17.outer_ref, ...), custom_call_target="tpu_custom_call" | custom-call | flops 1073741824 | bytes 2097152 | tf_op jit(solution)/shard_map/pallas_call | solution.py:329
  6.8 1.6 %collective-permute-start.3 = (bf16[256,256]{1,0:T(8,128)(2,1)S(1)}, bf16[256,256]{1,0:T(8,128)(2,1)S(1)}, u32[]{:S(2)}, u32[]{:S(2)}) collective-permute-start(bf16[256,256]{1,0:T(8,128)(2,1)S(1)} %get-tuple-element.19.own_ref), channel_id=1, source_target_pairs={{0,4},{4,0},{8,12},{12,8},{1,5},{5,1},{9,13},{13,9},{2,6},{6,2},{1... | collective-permute-start | bytes 393224 | tf_op jit(solution)/shard_map/ppermute | solution.py:285
  8.4 1.5 %collective-permute-start.1 = (bf16[16,256]{1,0:T(8,128)(2,1)S(1)}, bf16[16,256]{1,0:T(8,128)(2,1)S(1)}, u32[]{:S(2)}, u32[]{:S(2)}) collective-permute-start(bf16[16,256]{1,0:T(8,128)(2,1)S(1)} %get-tuple-element.21), channel_id=1, source_target_pairs={{0,2},{2,0},{1,3},{3,1},{4,6},{6,4},{5,7},{7,5},{8,10},{10,8},{9,1... | collective-permute-start | bytes 24584 | tf_op jit(solution)/shard_map/ppermute | solution.py:291
  9.9 0.4 %collective-permute-start.2 = (bf16[16,256]{1,0:T(8,128)(2,1)S(1)}, bf16[16,256]{1,0:T(8,128)(2,1)S(1)}, u32[]{:S(2)}, u32[]{:S(2)}) collective-permute-start(bf16[16,256]{1,0:T(8,128)(2,1)S(1)} %get-tuple-element.21), channel_id=1, source_target_pairs={{0,6},{2,4},{4,2},{6,0},{8,14},{10,12},{12,10},{14,8},{1,7},{3,5},... | collective-permute-start | bytes 24584 | tf_op jit(solution)/shard_map/ppermute | solution.py:340
  10.3 0.0 collective-permute-done.near_ref
  10.3 0.0 collective-permute-start.4
  10.3 0.0 copy-done.4
  10.3 0.4 %shard_map.95 = (f32[256,256]{1,0:T(8,128)S(1)}, bf16[128,256]{1,0:T(8,128)(2,1)S(1)}, f32[32,256]{1,0:T(8,128)S(1)}, bf16[8,256,256]{2,1,0:T(8,128)(2,1)S(1)}, f32[8,128,256]{2,1,0:T(8,128)S(1)}) custom-call(bf16[1,2,2,256,256]{4,3,2,1,0:T(8,128)(2,1)S(1)} %copy-done, bf16[256,256]{1,0:T(8,128)(2,1)S(1)} %get-tuple-element.19.own_ref, ...), custom_call_target="tpu_custom_call" | custom-call | flops 134217728 | bytes 524288 | tf_op jit(solution)/shard_map/pallas_call | solution.py:366
  10.7 1.3 %collective-permute-done.1.own_rim_ref = bf16[16,256]{1,0:T(8,128)(2,1)S(1)} collective-permute-done((bf16[16,256]{1,0:T(8,128)(2,1)S(1)}, bf16[16,256]{1,0:T(8,128)(2,1)S(1)}, u32[]{:S(2)}, u32[]{:S(2)}) %collective-permute-start.1) | collective-permute-done | bytes 8224 | tf_op jit(solution)/shard_map/ppermute | solution.py:291
  12.0 2.4 %collective-permute-done.2.other_rim_ref = bf16[16,256]{1,0:T(8,128)(2,1)S(1)} collective-permute-done((bf16[16,256]{1,0:T(8,128)(2,1)S(1)}, bf16[16,256]{1,0:T(8,128)(2,1)S(1)}, u32[]{:S(2)}, u32[]{:S(2)}) %collective-permute-start.2) | collective-permute-done | bytes 8224 | tf_op jit(solution)/shard_map/ppermute | solution.py:340
  14.4 0.3 %shard_map.96.mixed_ref = f32[256,256]{1,0:T(8,128)S(1)} custom-call(bf16[1,2,2,256,256]{4,3,2,1,0:T(8,128)(2,1)S(1)} %copy-done, f32[256,256]{1,0:T(8,128)S(1)} %get-tuple-element.20.begun_ref, bf16[16,256]{1,0:T(8,128)(2,1)S(1)} %collective-permute-done.1.own_rim_ref, bf16[16,256]{1,0:T(8,128)(2,1)S(1)} %collective-permute-done.2.other_rim_ref, ...), custom_call_target="tpu_custom_call" | custom-call | flops 1073741824 | bytes 262144 | tf_op jit(solution)/shard_map/pallas_call | solution.py:380
  14.8 0.0 collective-permute-done.3.other_ref
  14.8 0.0 collective-permute-done.4.far_ref
  14.8 1.0 %shard_map.97 = f32[16,128]{1,0:T(8,128)S(1)} custom-call(bf16[1,2,2,256,256]{4,3,2,1,0:T(8,128)(2,1)S(1)} %copy-done, f32[256,256]{1,0:T(8,128)S(1)} %shard_map.96.mixed_ref, bf16[256,256]{1,0:T(8,128)(2,1)S(1)} %collective-permute-done.3.other_ref, bf16[144,256]{1,0:T(8,128)(2,1)S(1)} %shard_map.94.pack_ref, ...), custom_call_target="tpu_custom_call" | custom-call | flops 268435456 | bytes 1048576 | tf_op jit(solution)/shard_map/pallas_call | solution.py:385
  15.8 9.1 %all_to_all.11 = f32[16,1,128]{2,1,0:T(1,128)S(1)} all-to-all(f32[16,1,128]{2,1,0:T(1,128)S(1)} %bitcast.4), channel_id=1, replica_groups=mesh['groups'=2,'sub'=4,'rng'=2,'chan'=2] {'chan','sub','rng'}, dimensions={0} | all-to-all | bytes 16384 | tf_op jit(solution)/shard_map/all_to_all | solution.py:393
  24.9 0.9 %shard_map.98 = f32[2,4096]{1,0:T(2,128)} custom-call(f32[16,128]{1,0:T(8,128)S(1)} %bitcast.5, bf16[128,256]{1,0:T(8,128)(2,1)S(1)} %get-tuple-element.25.low_ref, f32[32,256]{1,0:T(8,128)S(1)} %get-tuple-element.26.high_ref), custom_call_target="tpu_custom_call" | custom-call | tf_op jit(solution)/shard_map/pallas_call | solution.py:396
  (1 shorter events, 0.0 us)
Async XLA Ops:
  0.0 0.7 %copy-start.3 = (f32[2,2,16]{2,1,0:T(2,128)S(1)}, f32[2,2,16]{2,1,0:T(2,128)}, u32[]{:S(2)}) copy-start(f32[2,2,16]{2,1,0:T(2,128)} %_filt.1) | copy-start | bytes 772
  0.0 0.7 %copy-start.5 = (f32[2,2]{1,0:T(2,128)S(1)}, f32[2,2]{1,0:T(2,128)}, u32[]{:S(2)}) copy-start(f32[2,2]{1,0:T(2,128)} %_mix.1) | copy-start | bytes 52
  0.0 1.1 %copy-start = (bf16[1,2,2,256,256]{4,3,2,1,0:T(8,128)(2,1)S(1)}, bf16[1,2,2,256,256]{4,3,2,1,0:T(8,128)(2,1)}, u32[]{:S(2)}) copy-start(bf16[1,2,2,256,256]{4,3,2,1,0:T(8,128)(2,1)} %weight_ref.7) | copy-start | bytes 1572868
  0.0 1.1 %copy-start.1 = (s32[1,4,8,32]{3,2,1,0:T(8,128)S(1)}, s32[1,4,8,32]{3,2,1,0:T(8,128)}, u32[]{:S(2)}) copy-start(s32[1,4,8,32]{3,2,1,0:T(8,128)} %index_ref.1) | copy-start | bytes 12292
  0.0 1.1 %copy-start.2 = (f32[1,4,8,32]{3,2,1,0:T(8,128)S(1)}, f32[1,4,8,32]{3,2,1,0:T(8,128)}, u32[]{:S(2)}) copy-start(f32[1,4,8,32]{3,2,1,0:T(8,128)} %weight_ref.4) | copy-start | bytes 12292
  0.0 1.1 %copy-start.6 = (s32[1,8]{1,0:T(1,128)S(1)}, s32[1,8]{1,0:T(1,128)}, u32[]{:S(2)}) copy-start(s32[1,8]{1,0:T(1,128)} %counts_ref.1) | copy-start | bytes 100
  0.0 5.6 %copy-start.7 = (bf16[2,2,512,256]{3,2,1,0:T(8,128)(2,1)S(1)}, bf16[2,2,512,256]{3,2,1,0:T(8,128)(2,1)}, u32[]{:S(2)}) copy-start(bf16[2,2,512,256]{3,2,1,0:T(8,128)(2,1)} %raw_ref.1) | copy-start | bytes 3145732
  1.1 4.5 %copy-start.8 = (bf16[1,256,1024]{2,1,0:T(8,128)(2,1)S(1)}, bf16[1,256,1024]{2,1,0:T(8,128)(2,1)}, u32[]{:S(2)}) copy-start(bf16[1,256,1024]{2,1,0:T(8,128)(2,1)} %steer_ref.1) | copy-start | bytes 1572868
  1.2 9.1 %collective-permute-start = (bf16[144,256]{1,0:T(8,128)(2,1)S(1)}, bf16[144,256]{1,0:T(8,128)(2,1)S(1)}, u32[]{:S(2)}, u32[]{:S(2)}) collective-permute-start(bf16[144,256]{1,0:T(8,128)(2,1)S(1)} %shard_map.94.pack_ref), channel_id=1, source_target_pairs={{0,8},{4,12},{8,0},{12,4},{1,9},{5,13},{9,1},{13,5},{2,10},{6,14},... | collective-permute-start | bytes 221192 | tf_op jit(solution)/shard_map/ppermute | solution.py:285
  5.6 4.7 %copy-start.4 = (s32[1,8,32]{2,1,0:T(8,128)S(1)}, s32[1,8,32]{2,1,0:T(8,128)}, u32[]{:S(2)}) copy-start(s32[1,8,32]{2,1,0:T(8,128)} %pixel_ref.1) | copy-start | bytes 3076
  6.8 8.0 %collective-permute-start.3 = (bf16[256,256]{1,0:T(8,128)(2,1)S(1)}, bf16[256,256]{1,0:T(8,128)(2,1)S(1)}, u32[]{:S(2)}, u32[]{:S(2)}) collective-permute-start(bf16[256,256]{1,0:T(8,128)(2,1)S(1)} %get-tuple-element.19.own_ref), channel_id=1, source_target_pairs={{0,4},{4,0},{8,12},{12,8},{1,5},{5,1},{9,13},{13,9},{2,6},{6,2},{1... | collective-permute-start | bytes 393224 | tf_op jit(solution)/shard_map/ppermute | solution.py:285
  8.4 3.7 %collective-permute-start.1 = (bf16[16,256]{1,0:T(8,128)(2,1)S(1)}, bf16[16,256]{1,0:T(8,128)(2,1)S(1)}, u32[]{:S(2)}, u32[]{:S(2)}) collective-permute-start(bf16[16,256]{1,0:T(8,128)(2,1)S(1)} %get-tuple-element.21), channel_id=1, source_target_pairs={{0,2},{2,0},{1,3},{3,1},{4,6},{6,4},{5,7},{7,5},{8,10},{10,8},{9,1... | collective-permute-start | bytes 24584 | tf_op jit(solution)/shard_map/ppermute | solution.py:291
  9.9 4.5 %collective-permute-start.2 = (bf16[16,256]{1,0:T(8,128)(2,1)S(1)}, bf16[16,256]{1,0:T(8,128)(2,1)S(1)}, u32[]{:S(2)}, u32[]{:S(2)}) collective-permute-start(bf16[16,256]{1,0:T(8,128)(2,1)S(1)} %get-tuple-element.21), channel_id=1, source_target_pairs={{0,6},{2,4},{4,2},{6,0},{8,14},{10,12},{12,10},{14,8},{1,7},{3,5},... | collective-permute-start | bytes 24584 | tf_op jit(solution)/shard_map/ppermute | solution.py:340
  10.3 4.5 %collective-permute-start.4 = (bf16[144,256]{1,0:T(8,128)(2,1)S(1)}, bf16[144,256]{1,0:T(8,128)(2,1)S(1)}, u32[]{:S(2)}, u32[]{:S(2)}) collective-permute-start(bf16[144,256]{1,0:T(8,128)(2,1)S(1)} %collective-permute-done.near_ref), channel_id=1, source_target_pairs={{0,1},{1,0},{2,3},{3,2},{4,5},{5,4},{6,7},{7,6},{8,9},{9,8},{10,11... | collective-permute-start | bytes 221192 | tf_op jit(solution)/shard_map/ppermute | solution.py:285

commit v7 on v6

--- a/solution.py
+++ b/solution.py
@@ -123,10 +123,11 @@
     half = steer_ref.shape[1] // 2
     total = jnp.zeros(out_ref.shape, F32)
     rim = jnp.zeros(rim_ref.shape, F32)
+    crossed = jnp.concatenate([s_im, -s_re], 1)
     for c in range(channels):
-        x_re, x_im = raw_ref[c, 0], raw_ref[c, 1]
-        direct = (dot(s_re, x_re) + dot(s_im, x_im)).astype(BF16)
-        cross = (dot(s_im, x_re) - dot(s_re, x_im)).astype(BF16)
+        echoes = raw_ref[c].reshape(2 * pulses, raw_ref.shape[3])
+        direct = dot(steer_ref[0], echoes).astype(BF16)
+        cross = dot(crossed, echoes).astype(BF16)
         image = dot(direct, band_ref[c, 0]) + dot(cross, band_ref[c, 1])
         total = total + turned(image, mix_ref, c)
         side = dot_nt(outer_ref[c, 0], direct) + dot_nt(outer_ref[c, 1], cross)

time: 26 us -> 26 us (level)
  no operation moved by 1% of the time
where the time goes in v7:
time: 26 us; the launch traced here: 25.8 us
  blocking collectives  9.13 us (35%)
  starting transfers between devices  7.66 us (29%)
  Pallas kernels  4.18 us (16%)
  waiting for transfers between devices  3.71 us (14%)
  local copies, waits for them, and re-layouts  1.04 us (4%)
    all_to_all x1, blocking collectives, local(): lax.all_to_all(outgoing, ('chan', 'sub', 'rng'), split_axis=0, concat_axi...  9.13 us
    ppermute x3, starting transfers between devices, swapped(): lax.ppermute(value, axis, [(i, i ^ 1 << bit) for i in range(lax.axis_size...  5.73 us
    ppermute x1, waiting for transfers between devices, local(): lax.ppermute(rim, ('sub', 'rng'), [(i, i ^ 3) for i in range(groups)])  2.4 us
    ppermute x1, starting transfers between devices, neighbour_rims(): return lax.ppermute(rim, 'rng', [(0, 1), (1, 0)])  1.5 us
    ppermute x1, waiting for transfers between devices, neighbour_rims(): return lax.ppermute(rim, 'rng', [(0, 1), (1, 0)])  1.3 us
    pallas_call x1, Pallas kernels, local(): call(image_kernel, (shape((size, bins), BF16), shape((2 * EDGE, size), BF...  1.12 us
    unnamed x18, local copies, waits for them, and re-layouts  1.04 us
    pallas_call x1, Pallas kernels, local(): call(functools.partial(sample_kernel, taps, slots, 'chan'), shape((2 * ow...  0.98 us
  transfers between devices with their start and end apart: 5, of which 2 were waited for; matrix products, arithmetic and copies ran while one was open for 0% of the time, Pallas kernels for 8%

profile of v7, /device:TPU:0, one launch (start us, length us, event | category | flops | bytes accessed | tf_op | source)
XLA Modules:
  0.0 25.8 jit_solution(9864030442798233977)
XLA Ops:
  0.0 0.0 copy-start.3
  0.0 0.0 copy-start.5
  0.0 0.0 copy-start
  0.0 0.0 copy-start.1
  0.0 0.0 copy-start.2
  0.0 0.0 copy-start.6
  0.0 0.0 copy-start.7
  0.1 0.6 %copy-done.3 = f32[2,2,16]{2,1,0:T(2,128)S(1)} copy-done((f32[2,2,16]{2,1,0:T(2,128)S(1)}, f32[2,2,16]{2,1,0:T(2,128)}, u32[]{:S(2)}) %copy-start.3) | copy-done | bytes 280
  0.7 0.0 copy-done.5
  0.7 0.4 %copy-done = bf16[1,2,2,256,256]{4,3,2,1,0:T(8,128)(2,1)S(1)} copy-done((bf16[1,2,2,256,256]{4,3,2,1,0:T(8,128)(2,1)S(1)}, bf16[1,2,2,256,256]{4,3,2,1,0:T(8,128)(2,1)}, u32[]{:S(2)}) %copy-start) | copy-done | bytes 524312
  1.1 0.0 copy-done.1
  1.1 0.0 copy-done.2
  1.1 0.0 copy-done.6
  1.1 0.0 copy-start.8
  1.1 0.2 shard_map.94.pack_ref
  1.2 4.1 %collective-permute-start = (bf16[144,256]{1,0:T(8,128)(2,1)S(1)}, bf16[144,256]{1,0:T(8,128)(2,1)S(1)}, u32[]{:S(2)}, u32[]{:S(2)}) collective-permute-start(bf16[144,256]{1,0:T(8,128)(2,1)S(1)} %shard_map.94.pack_ref), channel_id=1, source_target_pairs={{0,8},{4,12},{8,0},{12,4},{1,9},{5,13},{9,1},{13,5},{2,10},{6,14},... | collective-permute-start | bytes 221192 | tf_op jit(solution)/shard_map/ppermute | solution.py:286
  5.3 0.2 shard_map.91
  5.6 0.0 copy-done.7
  5.6 0.0 copy-done.8
  5.6 0.0 copy-start.4
  5.6 1.1 %shard_map.92 = (bf16[256,256]{1,0:T(8,128)(2,1)S(1)}, bf16[16,256]{1,0:T(8,128)(2,1)S(1)}) custom-call(bf16[2,2,512,256]{3,2,1,0:T(8,128)(2,1)S(1)} %copy-done.7, bf16[1,256,1024]{2,1,0:T(8,128)(2,1)S(1)} %copy-done.8, bf16[2,2,256,256]{3,2,1,0:T(8,128)(2,1)S(1)} %get-tuple-element.16.band_ref, bf16[2,2,16,256]{3,2,1,0:T(8,128)(2,1)S(1)} %get-tuple-element.17.outer_ref, ...), custom_call_target="tpu_custom_call" | custom-call | flops 1073741824 | bytes 2097152 | tf_op jit(solution)/shard_map/pallas_call | solution.py:330
  6.8 1.6 %collective-permute-start.3 = (bf16[256,256]{1,0:T(8,128)(2,1)S(1)}, bf16[256,256]{1,0:T(8,128)(2,1)S(1)}, u32[]{:S(2)}, u32[]{:S(2)}) collective-permute-start(bf16[256,256]{1,0:T(8,128)(2,1)S(1)} %get-tuple-element.19.own_ref), channel_id=1, source_target_pairs={{0,4},{4,0},{8,12},{12,8},{1,5},{5,1},{9,13},{13,9},{2,6},{6,2},{1... | collective-permute-start | bytes 393224 | tf_op jit(solution)/shard_map/ppermute | solution.py:286
  8.4 1.5 %collective-permute-start.1 = (bf16[16,256]{1,0:T(8,128)(2,1)S(1)}, bf16[16,256]{1,0:T(8,128)(2,1)S(1)}, u32[]{:S(2)}, u32[]{:S(2)}) collective-permute-start(bf16[16,256]{1,0:T(8,128)(2,1)S(1)} %get-tuple-element.21), channel_id=1, source_target_pairs={{0,2},{2,0},{1,3},{3,1},{4,6},{6,4},{5,7},{7,5},{8,10},{10,8},{9,1... | collective-permute-start | bytes 24584 | tf_op jit(solution)/shard_map/ppermute | solution.py:292
  9.9 0.4 %collective-permute-start.2 = (bf16[16,256]{1,0:T(8,128)(2,1)S(1)}, bf16[16,256]{1,0:T(8,128)(2,1)S(1)}, u32[]{:S(2)}, u32[]{:S(2)}) collective-permute-start(bf16[16,256]{1,0:T(8,128)(2,1)S(1)} %get-tuple-element.21), channel_id=1, source_target_pairs={{0,6},{2,4},{4,2},{6,0},{8,14},{10,12},{12,10},{14,8},{1,7},{3,5},... | collective-permute-start | bytes 24584 | tf_op jit(solution)/shard_map/ppermute | solution.py:341
  10.3 0.0 collective-permute-done.near_ref
  10.3 0.0 collective-permute-start.4
  10.3 0.0 copy-done.4
  10.3 0.4 %shard_map.95 = (f32[256,256]{1,0:T(8,128)S(1)}, bf16[128,256]{1,0:T(8,128)(2,1)S(1)}, f32[32,256]{1,0:T(8,128)S(1)}, bf16[8,256,256]{2,1,0:T(8,128)(2,1)S(1)}, f32[8,128,256]{2,1,0:T(8,128)S(1)}) custom-call(bf16[1,2,2,256,256]{4,3,2,1,0:T(8,128)(2,1)S(1)} %copy-done, bf16[256,256]{1,0:T(8,128)(2,1)S(1)} %get-tuple-element.19.own_ref, ...), custom_call_target="tpu_custom_call" | custom-call | flops 134217728 | bytes 524288 | tf_op jit(solution)/shard_map/pallas_call | solution.py:367
  10.7 1.3 %collective-permute-done.1.own_rim_ref = bf16[16,256]{1,0:T(8,128)(2,1)S(1)} collective-permute-done((bf16[16,256]{1,0:T(8,128)(2,1)S(1)}, bf16[16,256]{1,0:T(8,128)(2,1)S(1)}, u32[]{:S(2)}, u32[]{:S(2)}) %collective-permute-start.1) | collective-permute-done | bytes 8224 | tf_op jit(solution)/shard_map/ppermute | solution.py:292
  12.0 2.4 %collective-permute-done.2.other_rim_ref = bf16[16,256]{1,0:T(8,128)(2,1)S(1)} collective-permute-done((bf16[16,256]{1,0:T(8,128)(2,1)S(1)}, bf16[16,256]{1,0:T(8,128)(2,1)S(1)}, u32[]{:S(2)}, u32[]{:S(2)}) %collective-permute-start.2) | collective-permute-done | bytes 8224 | tf_op jit(solution)/shard_map/ppermute | solution.py:341
  14.4 0.3 %shard_map.96.mixed_ref = f32[256,256]{1,0:T(8,128)S(1)} custom-call(bf16[1,2,2,256,256]{4,3,2,1,0:T(8,128)(2,1)S(1)} %copy-done, f32[256,256]{1,0:T(8,128)S(1)} %get-tuple-element.20.begun_ref, bf16[16,256]{1,0:T(8,128)(2,1)S(1)} %collective-permute-done.1.own_rim_ref, bf16[16,256]{1,0:T(8,128)(2,1)S(1)} %collective-permute-done.2.other_rim_ref, ...), custom_call_target="tpu_custom_call" | custom-call | flops 1073741824 | bytes 262144 | tf_op jit(solution)/shard_map/pallas_call | solution.py:381
  14.8 0.0 collective-permute-done.3.other_ref
  14.8 0.0 collective-permute-done.4.far_ref
  14.8 1.0 %shard_map.97 = f32[16,128]{1,0:T(8,128)S(1)} custom-call(bf16[1,2,2,256,256]{4,3,2,1,0:T(8,128)(2,1)S(1)} %copy-done, f32[256,256]{1,0:T(8,128)S(1)} %shard_map.96.mixed_ref, bf16[256,256]{1,0:T(8,128)(2,1)S(1)} %collective-permute-done.3.other_ref, bf16[144,256]{1,0:T(8,128)(2,1)S(1)} %shard_map.94.pack_ref, ...), custom_call_target="tpu_custom_call" | custom-call | flops 268435456 | bytes 1048576 | tf_op jit(solution)/shard_map/pallas_call | solution.py:386
  15.8 9.1 %all_to_all.11 = f32[16,1,128]{2,1,0:T(1,128)S(1)} all-to-all(f32[16,1,128]{2,1,0:T(1,128)S(1)} %bitcast.4), channel_id=1, replica_groups=mesh['groups'=2,'sub'=4,'rng'=2,'chan'=2] {'chan','sub','rng'}, dimensions={0} | all-to-all | bytes 16384 | tf_op jit(solution)/shard_map/all_to_all | solution.py:394
  24.9 0.9 %shard_map.98 = f32[2,4096]{1,0:T(2,128)} custom-call(f32[16,128]{1,0:T(8,128)S(1)} %bitcast.5, bf16[128,256]{1,0:T(8,128)(2,1)S(1)} %get-tuple-element.25.low_ref, f32[32,256]{1,0:T(8,128)S(1)} %get-tuple-element.26.high_ref), custom_call_target="tpu_custom_call" | custom-call | tf_op jit(solution)/shard_map/pallas_call | solution.py:397
  (1 shorter events, 0.0 us)
Async XLA Ops:
  0.0 0.7 %copy-start.3 = (f32[2,2,16]{2,1,0:T(2,128)S(1)}, f32[2,2,16]{2,1,0:T(2,128)}, u32[]{:S(2)}) copy-start(f32[2,2,16]{2,1,0:T(2,128)} %_filt.1) | copy-start | bytes 772
  0.0 0.7 %copy-start.5 = (f32[2,2]{1,0:T(2,128)S(1)}, f32[2,2]{1,0:T(2,128)}, u32[]{:S(2)}) copy-start(f32[2,2]{1,0:T(2,128)} %_mix.1) | copy-start | bytes 52
  0.0 1.1 %copy-start = (bf16[1,2,2,256,256]{4,3,2,1,0:T(8,128)(2,1)S(1)}, bf16[1,2,2,256,256]{4,3,2,1,0:T(8,128)(2,1)}, u32[]{:S(2)}) copy-start(bf16[1,2,2,256,256]{4,3,2,1,0:T(8,128)(2,1)} %weight_ref.7) | copy-start | bytes 1572868
  0.0 1.1 %copy-start.1 = (s32[1,4,8,32]{3,2,1,0:T(8,128)S(1)}, s32[1,4,8,32]{3,2,1,0:T(8,128)}, u32[]{:S(2)}) copy-start(s32[1,4,8,32]{3,2,1,0:T(8,128)} %index_ref.1) | copy-start | bytes 12292
  0.0 1.1 %copy-start.2 = (f32[1,4,8,32]{3,2,1,0:T(8,128)S(1)}, f32[1,4,8,32]{3,2,1,0:T(8,128)}, u32[]{:S(2)}) copy-start(f32[1,4,8,32]{3,2,1,0:T(8,128)} %weight_ref.4) | copy-start | bytes 12292
  0.0 1.1 %copy-start.6 = (s32[1,8]{1,0:T(1,128)S(1)}, s32[1,8]{1,0:T(1,128)}, u32[]{:S(2)}) copy-start(s32[1,8]{1,0:T(1,128)} %counts_ref.1) | copy-start | bytes 100
  0.0 5.6 %copy-start.7 = (bf16[2,2,512,256]{3,2,1,0:T(8,128)(2,1)S(1)}, bf16[2,2,512,256]{3,2,1,0:T(8,128)(2,1)}, u32[]{:S(2)}) copy-start(bf16[2,2,512,256]{3,2,1,0:T(8,128)(2,1)} %raw_ref.1) | copy-start | bytes 3145732
  1.1 4.5 %copy-start.8 = (bf16[1,256,1024]{2,1,0:T(8,128)(2,1)S(1)}, bf16[1,256,1024]{2,1,0:T(8,128)(2,1)}, u32[]{:S(2)}) copy-start(bf16[1,256,1024]{2,1,0:T(8,128)(2,1)} %steer_ref.1) | copy-start | bytes 1572868
  1.2 9.1 %collective-permute-start = (bf16[144,256]{1,0:T(8,128)(2,1)S(1)}, bf16[144,256]{1,0:T(8,128)(2,1)S(1)}, u32[]{:S(2)}, u32[]{:S(2)}) collective-permute-start(bf16[144,256]{1,0:T(8,128)(2,1)S(1)} %shard_map.94.pack_ref), channel_id=1, source_target_pairs={{0,8},{4,12},{8,0},{12,4},{1,9},{5,13},{9,1},{13,5},{2,10},{6,14},... | collective-permute-start | bytes 221192 | tf_op jit(solution)/shard_map/ppermute | solution.py:286
  5.6 4.7 %copy-start.4 = (s32[1,8,32]{2,1,0:T(8,128)S(1)}, s32[1,8,32]{2,1,0:T(8,128)}, u32[]{:S(2)}) copy-start(s32[1,8,32]{2,1,0:T(8,128)} %pixel_ref.1) | copy-start | bytes 3076
  6.8 8.0 %collective-permute-start.3 = (bf16[256,256]{1,0:T(8,128)(2,1)S(1)}, bf16[256,256]{1,0:T(8,128)(2,1)S(1)}, u32[]{:S(2)}, u32[]{:S(2)}) collective-permute-start(bf16[256,256]{1,0:T(8,128)(2,1)S(1)} %get-tuple-element.19.own_ref), channel_id=1, source_target_pairs={{0,4},{4,0},{8,12},{12,8},{1,5},{5,1},{9,13},{13,9},{2,6},{6,2},{1... | collective-permute-start | bytes 393224 | tf_op jit(solution)/shard_map/ppermute | solution.py:286
  8.4 3.7 %collective-permute-start.1 = (bf16[16,256]{1,0:T(8,128)(2,1)S(1)}, bf16[16,256]{1,0:T(8,128)(2,1)S(1)}, u32[]{:S(2)}, u32[]{:S(2)}) collective-permute-start(bf16[16,256]{1,0:T(8,128)(2,1)S(1)} %get-tuple-element.21), channel_id=1, source_target_pairs={{0,2},{2,0},{1,3},{3,1},{4,6},{6,4},{5,7},{7,5},{8,10},{10,8},{9,1... | collective-permute-start | bytes 24584 | tf_op jit(solution)/shard_map/ppermute | solution.py:292
  9.9 4.5 %collective-permute-start.2 = (bf16[16,256]{1,0:T(8,128)(2,1)S(1)}, bf16[16,256]{1,0:T(8,128)(2,1)S(1)}, u32[]{:S(2)}, u32[]{:S(2)}) collective-permute-start(bf16[16,256]{1,0:T(8,128)(2,1)S(1)} %get-tuple-element.21), channel_id=1, source_target_pairs={{0,6},{2,4},{4,2},{6,0},{8,14},{10,12},{12,10},{14,8},{1,7},{3,5},... | collective-permute-start | bytes 24584 | tf_op jit(solution)/shard_map/ppermute | solution.py:341
  10.3 4.5 %collective-permute-start.4 = (bf16[144,256]{1,0:T(8,128)(2,1)S(1)}, bf16[144,256]{1,0:T(8,128)(2,1)S(1)}, u32[]{:S(2)}, u32[]{:S(2)}) collective-permute-start(bf16[144,256]{1,0:T(8,128)(2,1)S(1)} %collective-permute-done.near_ref), channel_id=1, source_target_pairs={{0,1},{1,0},{2,3},{3,2},{4,5},{5,4},{6,7},{7,6},{8,9},{9,8},{10,11... | collective-permute-start | bytes 221192 | tf_op jit(solution)/shard_map/ppermute | solution.py:286
